TPU v7x, 128 devices: a whole 4x4x4 slice. The times are simulated.
128 devices in a mesh: fsdp: 16 (over x_hi, z, core), tp: 8 (over x_lo, y).
Axes of the slice: x: 4 (x_hi: 2, x_lo: 2; x = x_hi * 2 + x_lo), y: 4, z: 4, core: 2. Of those that a mesh axis runs over, the one named last changes fastest.
Arguments:
- trainer_weights: bfloat16 [16, 3, 1536, 4096], P('tp', None, None, 'fsdp'), may hold values from -0.09375 to 0.09375
- hidden_in: bfloat16 [256, 4096], P('fsdp'), may hold values from -6 to 6
- norm_gain: float32 [4096], replicated, may hold values from 0.1 to 1.9
- routing: int32 [4, 256, 8], P(None, 'fsdp'), may hold values from 0 to 15, all different within a row; in each aligned block of 16 rows (0 to 15, 16 to 31, ..., all dimensions but the last counted through in order) at most 11 rows name the same one
- gate_weights: float32 [4, 256, 8], P(None, 'fsdp'), may hold values from 0.2 to 1
Outputs:
- hidden_out: float32 [256, 4096], P('fsdp')
Inputs may be any that keep to these rules, and one draw needn't show every extreme that they name: `routing`: each row names 8 different experts in each step. In each step, the 16 rows of one fsdp index name any one expert at most 11 times, a bound that some of these blocks reach.
All inputs are finite; a program needn't handle non-finite values.
Results may differ from a plain program's by a relative error of at most 0.04.
Values may be sent and summed in bfloat16 or wider, within the bound.
No kernel may reach another device: no remote copies, remote signals or barrier semaphores. Data moves between devices by JAX's collectives and lax.ppermute only.
A program may use at most 128 MiB of HBM per device.

v0:
```python
import jax
import jax.numpy as jnp
from jax import lax
from jax.sharding import PartitionSpec as P

TOPK = 8
EXPERTS = 16
QB = 128
STEPS = 4
CAP = 11


norm_eps = 1e-06
scale_eps = 1e-06
code_limit = 448.0
smallest_normal = 0.015625


def float_code(values):
    magnitude = jnp.maximum(jnp.abs(values), smallest_normal)
    exponent = jnp.floor(jnp.log2(magnitude))
    spacing = jnp.exp2(exponent - 3.0)
    return jnp.floor(values / spacing + 0.5) * spacing


def quantize_blocks(matrices):
    leading, kinds, unit_count, feature_count = matrices.shape
    values = matrices.astype(jnp.float32).reshape(
        leading, kinds, unit_count // QB, QB, feature_count // QB, QB
    )
    largest = jnp.max(jnp.abs(values), axis=(3, 5))
    scales = (largest + scale_eps) / code_limit
    coded = float_code(values / scales[:, :, :, None, :, None]).astype(jnp.bfloat16)
    return (coded.reshape(matrices.shape), scales)


def dequantize(coded, row_scales):
    leading, kinds, unit_count, feature_count = coded.shape
    values = coded.astype(jnp.float32).reshape(leading, kinds, unit_count, feature_count // QB, QB)
    values = values * row_scales[..., None]
    return values.reshape(coded.shape).astype(jnp.bfloat16)


def body(trainer_weights, hidden_in, norm_gain, routing, gate_weights):
    coded, block_scales = quantize_blocks(trainer_weights)
    row_scales = jnp.repeat(block_scales, QB, axis=2)
    moved_codes, moved_scales = (
        lax.all_to_all(
            lax.all_to_all(coded, "tp", split_axis=2, concat_axis=0, tiled=True),
            "fsdp",
            split_axis=0,
            concat_axis=3,
            tiled=True,
        ),
        lax.all_to_all(
            lax.all_to_all(
                row_scales.astype(jnp.bfloat16), "tp", split_axis=2, concat_axis=0, tiled=True
            ),
            "fsdp",
            split_axis=0,
            concat_axis=3,
            tiled=True,
        ).astype(row_scales.dtype),
    )
    expert_weights = dequantize(moved_codes, moved_scales)
    stream = hidden_in.astype(jnp.float32)
    rows_here = stream.shape[0]
    model_width = stream.shape[1]
    expert_ids = jnp.arange(EXPERTS, dtype=jnp.int32)
    source_rows = jnp.arange(rows_here * TOPK, dtype=jnp.int32) // TOPK
    for decode_step in range(STEPS):
        normed = (
            stream
            * lax.rsqrt(jnp.mean(stream * stream, axis=-1, keepdims=True) + norm_eps)
            * norm_gain
        )
        normed = normed.astype(jnp.bfloat16)
        chosen = routing[decode_step].reshape(-1)
        onehot = (chosen[:, None] == expert_ids[None, :]).astype(jnp.int32)
        earlier = jnp.cumsum(onehot, axis=0) - onehot
        slot_index = chosen * CAP + jnp.sum(earlier * onehot, axis=1)
        outgoing = (
            jnp.zeros((EXPERTS * CAP, model_width), jnp.bfloat16)
            .at[slot_index]
            .set(normed[source_rows])
        )
        outgoing = outgoing.reshape(EXPERTS, CAP, model_width)
        arrived = lax.all_to_all(outgoing, "fsdp", split_axis=0, concat_axis=1, tiled=True)
        gate_up = jnp.einsum(
            "emd,egfd->egmf", arrived, expert_weights[:, :2], preferred_element_type=jnp.float32
        )
        hidden = (jax.nn.silu(gate_up[:, 0]) * gate_up[:, 1]).astype(jnp.bfloat16)
        partial_value = jnp.einsum(
            "emf,efd->emd", hidden, expert_weights[:, 2], preferred_element_type=jnp.float32
        )
        step_gates = gate_weights[decode_step].reshape(-1)
        summed = lax.psum(partial_value.astype(jnp.bfloat16), "tp")
        returned_rows = lax.all_to_all(
            summed, "fsdp", split_axis=1, concat_axis=0, tiled=True
        ).reshape(EXPERTS * CAP, model_width)
        picked = returned_rows[slot_index].astype(jnp.float32) * step_gates[:, None]
        stream = stream + jnp.sum(picked.reshape(rows_here, TOPK, model_width), axis=1)
    return stream


def solution(mesh):
    in_specs = (
        P("tp", None, None, "fsdp"),
        P("fsdp", None),
        P(),
        P(None, "fsdp", None),
        P(None, "fsdp", None),
    )
    out_specs = P("fsdp", None)
    return jax.shard_map(body, mesh=mesh, in_specs=in_specs, out_specs=out_specs, check_vma=False)
```

profile of v0, /device:TPU:0, one launch (start us, length us, event | category | flops | bytes accessed | tf_op | source)
XLA Modules:
  0.0 1012.7 jit_solution(5964701852867795096)
XLA Ops:
  13.4 12.8 %abs.11 = f32[2,3,12,128,2,128]{5,4,3,2,1,0:T(2,128)} reshape(f32[2,3,1536,256]{3,2,1,0:T(8,128)} %convert_abs_fusion) | data formatting | bytes 18874368 | tf_op jit(solution)/shard_map/abs | solution.py:31
  48.3 13.0 %div.79 = f32[2,3,1536,256]{3,2,1,0:T(8,128)} reshape(f32[2,3,12,128,2,128]{5,4,3,2,1,0:T(2,128)} %div.78) | data formatting | bytes 18874368 | tf_op jit(solution)/shard_map/div | solution.py:33
  75.4 9.1 fusion.10
  84.5 20.8 %copy.103 = bf16[2,3,1536,256]{3,1,0,2:T(4,128)(2,1)} copy(bf16[2,3,1536,256]{3,2,1,0:T(8,128)(2,1)S(1)} %fusion.10) | data formatting | bytes 9437184 | tf_op jit(solution)/shard_map/convert_element_type | solution.py:33
  119.9 62.9 %all-to-all-done = bf16[2,3,1536,256]{3,1,0,2:T(4,128)(2,1)} async-done(((bf16[2,3,1536,256]{3,1,0,2:T(4,128)(2,1)}), bf16[2,3,1536,256]{3,1,0,2:T(4,128)(2,1)}, u32[]{:S(2)}, u32[]{:S(2)}) %all-to-all-start) | async-done | bytes 4718624 | tf_op jit(solution)/shard_map/all_to_all | solution.py:49
  196.5 23.0 %all-to-all-done.4 = bf16[16,11,4096]{2,1,0:T(8,128)(2,1)S(1)} async-done(((bf16[16,11,4096]{2,1,0:T(8,128)(2,1)}), bf16[16,11,4096]{2,1,0:T(8,128)(2,1)S(1)}, u32[]{:S(2)}, u32[]{:S(2)}) %all-to-all-start.4) | async-done | bytes 1441824 | tf_op jit(solution)/shard_map/all_to_all | solution.py:88
  231.7 11.3 %mul.261 = f32[1,3,192,4096]{3,2,1,0:T(8,128)} reshape(f32[3,192,32,128]{3,2,1,0:T(8,128)} %mul.260) | data formatting | bytes 18874368 | tf_op jit(solution)/shard_map/mul | solution.py:40
  244.6 44.0 %all-to-all-done.1 = bf16[16,3,192,256]{3,2,1,0:T(8,128)(2,1)} async-done(((bf16[16,3,192,256]{3,2,1,0:T(8,128)(2,1)}), bf16[16,3,192,256]{3,2,1,0:T(8,128)(2,1)}, u32[]{:S(2)}, u32[]{:S(2)}) %all-to-all-start.1) | async-done | bytes 4718624 | tf_op jit(solution)/shard_map/all_to_all | solution.py:48
  297.3 10.1 multiply_convert_fusion
  313.3 85.5 %all-reduce.5.cloned.1.call-done = bf16[1,176,4096]{2,1,0:T(8,128)(2,1)} async-done(((bf16[1,176,4096]{2,1,0:T(8,128)(2,1)}), bf16[1,176,4096]{2,1,0:T(8,128)(2,1)}) %all-reduce.5.cloned.1.call-update) | async-done | bytes 1441808 | tf_op jit(solution)/shard_map/psum | solution.py:97
  404.0 10.9 %reduce = bf16[176,4096]{1,0:T(8,128)(2,1)} reduce(bf16[176,1,4096]{2,1,0:T(2,128)(2,1)S(1)} %bitcast.168, bf16[]{:T(256)} %broadcast.358), dimensions={1}, to_apply=%bitcast.161.reduce_sub_computation | reduce | bytes 2883586
  427.0 20.2 %all-to-all-done.5 = bf16[16,2,22528]{2,1,0:T(2,128)(2,1)S(1)} async-done(((bf16[16,2,22528]{2,1,0:T(2,128)(2,1)}), bf16[16,2,22528]{2,1,0:T(2,128)(2,1)S(1)}, u32[]{:S(2)}, u32[]{:S(2)}) %all-to-all-start.5) | async-done | bytes 1441824 | tf_op jit(solution)/shard_map/all_to_all | solution.py:98
  465.8 33.0 %all_to_all.126 = bf16[16,11,4096]{2,1,0:T(8,128)(2,1)} all-to-all(bf16[16,11,4096]{2,1,0:T(8,128)(2,1)S(1)} %reshape.470), channel_id=1, replica_groups=mesh['fsdp'=16,'tp'=8] {'fsdp'}, dimensions={0} | all-to-all | bytes 2883584 | tf_op jit(solution)/shard_map/all_to_all | solution.py:88
  506.8 74.6 %all-reduce.7.cloned.1.call-done = bf16[1,176,4096]{2,1,0:T(8,128)(2,1)} async-done(((bf16[1,176,4096]{2,1,0:T(8,128)(2,1)}), bf16[1,176,4096]{2,1,0:T(8,128)(2,1)}) %all-reduce.7.cloned.1.call-update) | async-done | bytes 1441808 | tf_op jit(solution)/shard_map/psum | solution.py:97
  586.0 10.7 %reduce.1 = bf16[176,4096]{1,0:T(8,128)(2,1)} reduce(bf16[176,1,4096]{2,1,0:T(2,128)(2,1)S(1)} %bitcast.171, bf16[]{:T(256)} %broadcast.358), dimensions={1}, to_apply=%bitcast.160.reduce_sub_computation | reduce | bytes 2883586
  608.2 20.8 %all-to-all-done.7 = bf16[16,2,22528]{2,1,0:T(2,128)(2,1)S(1)} async-done(((bf16[16,2,22528]{2,1,0:T(2,128)(2,1)}), bf16[16,2,22528]{2,1,0:T(2,128)(2,1)S(1)}, u32[]{:S(2)}, u32[]{:S(2)}) %all-to-all-start.7) | async-done | bytes 1441824 | tf_op jit(solution)/shard_map/all_to_all | solution.py:98
  647.8 33.0 %all_to_all.127 = bf16[16,11,4096]{2,1,0:T(8,128)(2,1)} all-to-all(bf16[16,11,4096]{2,1,0:T(8,128)(2,1)S(1)} %reshape.473), channel_id=1, replica_groups=mesh['fsdp'=16,'tp'=8] {'fsdp'}, dimensions={0} | all-to-all | bytes 2883584 | tf_op jit(solution)/shard_map/all_to_all | solution.py:88
  689.0 74.6 %all-reduce.9.cloned.1.call-done = bf16[1,176,4096]{2,1,0:T(8,128)(2,1)} async-done(((bf16[1,176,4096]{2,1,0:T(8,128)(2,1)}), bf16[1,176,4096]{2,1,0:T(8,128)(2,1)}) %all-reduce.9.cloned.1.call-update) | async-done | bytes 1441808 | tf_op jit(solution)/shard_map/psum | solution.py:97
  768.3 10.7 %reduce.2 = bf16[176,4096]{1,0:T(8,128)(2,1)} reduce(bf16[176,1,4096]{2,1,0:T(2,128)(2,1)S(1)} %bitcast.173, bf16[]{:T(256)} %broadcast.358), dimensions={1}, to_apply=%bitcast.159.reduce_sub_computation | reduce | bytes 2883586
  790.5 20.7 %all-to-all-done.9 = bf16[16,2,22528]{2,1,0:T(2,128)(2,1)S(1)} async-done(((bf16[16,2,22528]{2,1,0:T(2,128)(2,1)}), bf16[16,2,22528]{2,1,0:T(2,128)(2,1)S(1)}, u32[]{:S(2)}, u32[]{:S(2)}) %all-to-all-start.9) | async-done | bytes 1441824 | tf_op jit(solution)/shard_map/all_to_all | solution.py:98
  830.0 33.0 %all_to_all.128 = bf16[16,11,4096]{2,1,0:T(8,128)(2,1)} all-to-all(bf16[16,11,4096]{2,1,0:T(8,128)(2,1)S(1)} %reshape.476), channel_id=1, replica_groups=mesh['fsdp'=16,'tp'=8] {'fsdp'}, dimensions={0} | all-to-all | bytes 2883584 | tf_op jit(solution)/shard_map/all_to_all | solution.py:88
  871.0 74.6 %all-reduce.11.cloned.1.call-done = bf16[1,176,4096]{2,1,0:T(8,128)(2,1)} async-done(((bf16[1,176,4096]{2,1,0:T(8,128)(2,1)}), bf16[1,176,4096]{2,1,0:T(8,128)(2,1)}) %all-reduce.11.cloned.1.call-update) | async-done | bytes 1441808 | tf_op jit(solution)/shard_map/psum | solution.py:97
  950.3 10.8 %reduce.3 = bf16[176,4096]{1,0:T(8,128)(2,1)} reduce(bf16[176,1,4096]{2,1,0:T(2,128)(2,1)S(1)} %bitcast.169, bf16[]{:T(256)} %broadcast.358), dimensions={1}, to_apply=%bitcast.158.reduce_sub_computation | reduce | bytes 2883586
  971.2 22.2 %all-to-all-done.11 = bf16[16,2,22528]{2,1,0:T(2,128)(2,1)S(1)} async-done(((bf16[16,2,22528]{2,1,0:T(2,128)(2,1)}), bf16[16,2,22528]{2,1,0:T(2,128)(2,1)S(1)}, u32[]{:S(2)}, u32[]{:S(2)}) %all-to-all-start.11) | async-done | bytes 1441824 | tf_op jit(solution)/shard_map/all_to_all | solution.py:98
  (185 shorter events, 256.3 us)
Async XLA Ops:
  36.5 24.8 %all-to-all-start.2 = ((bf16[8,2,1152]{2,1,0:T(2,128)(2,1)}), bf16[8,2,1152]{2,1,0:T(2,128)(2,1)S(1)}, u32[]{:S(2)}, u32[]{:S(2)}) async-start(bf16[8,2,1152]{2,1,0:T(2,128)(2,1)} %reshape.615), calls=%async_computation.2 | async-start | bytes 73728 | tf_op jit(solution)/shard_map/all_to_all | solution.py:56
  67.8 37.4 %all-to-all-start.3 = ((bf16[16,3,192,2]{2,3,1,0:T(2,128)(2,1)}), bf16[16,3,192,2]{2,3,1,0:T(2,128)(2,1)S(1)}, u32[]{:S(2)}, u32[]{:S(2)}) async-start(bf16[16,3,192,2]{2,3,1,0:T(2,128)(2,1)} %bitcast.8), calls=%async_computation.3 | async-start | bytes 98304 | tf_op jit(solution)/shard_map/all_to_all | solution.py:55
  105.3 7.1 copy-start.2
  105.3 7.3 copy-start.9
  105.3 77.4 %all-to-all-start = ((bf16[2,3,1536,256]{3,1,0,2:T(4,128)(2,1)}), bf16[2,3,1536,256]{3,1,0,2:T(4,128)(2,1)}, u32[]{:S(2)}, u32[]{:S(2)}) async-start(bf16[2,3,1536,256]{3,1,0,2:T(4,128)(2,1)} %copy.103), calls=%async_computation | async-start | bytes 12582912 | tf_op jit(solution)/shard_map/all_to_all | solution.py:49
  112.2 7.6 copy-start.19
  182.7 36.8 %all-to-all-start.4 = ((bf16[16,11,4096]{2,1,0:T(8,128)(2,1)}), bf16[16,11,4096]{2,1,0:T(8,128)(2,1)S(1)}, u32[]{:S(2)}, u32[]{:S(2)}) async-start(bf16[16,11,4096]{2,1,0:T(8,128)(2,1)} %reshape.466), calls=%async_computation.4 | async-start | bytes 4194304 | tf_op jit(solution)/shard_map/all_to_all | solution.py:88
  219.5 69.1 %all-to-all-start.1 = ((bf16[16,3,192,256]{3,2,1,0:T(8,128)(2,1)}), bf16[16,3,192,256]{3,2,1,0:T(8,128)(2,1)}, u32[]{:S(2)}, u32[]{:S(2)}) async-start(bf16[16,3,192,256]{3,2,1,0:T(8,128)(2,1)} %bitcast.167), calls=%async_computation.1 | async-start | bytes 9437184 | tf_op jit(solution)/shard_map/all_to_all | solution.py:48
  225.8 172.9 %all-reduce.5.cloned.1.call-start = ((), (), s32[]{:S(2)}) async-start(), calls=%async_computation.12 | async-start | bytes 2883584 | tf_op jit(solution)/shard_map/psum | solution.py:97
  297.3 10.1 copy-start.8
  418.2 7.4 copy-start.15
  418.2 29.1 %all-to-all-start.5 = ((bf16[16,2,22528]{2,1,0:T(2,128)(2,1)}), bf16[16,2,22528]{2,1,0:T(2,128)(2,1)S(1)}, u32[]{:S(2)}, u32[]{:S(2)}) async-start(bf16[16,2,22528]{2,1,0:T(2,128)(2,1)} %reshape.617), calls=%async_computation.5 | async-start | bytes 2883584 | tf_op jit(solution)/shard_map/all_to_all | solution.py:98
  425.0 156.4 %all-reduce.7.cloned.1.call-start = ((), (), s32[]{:S(2)}) async-start(), calls=%async_computation.13 | async-start | bytes 2883584 | tf_op jit(solution)/shard_map/psum | solution.py:97
  600.1 7.0 copy-start.13
  600.1 7.4 copy-start.21
  600.1 29.0 %all-to-all-start.7 = ((bf16[16,2,22528]{2,1,0:T(2,128)(2,1)}), bf16[16,2,22528]{2,1,0:T(2,128)(2,1)S(1)}, u32[]{:S(2)}, u32[]{:S(2)}) async-start(bf16[16,2,22528]{2,1,0:T(2,128)(2,1)} %reshape.619), calls=%async_computation.7 | async-start | bytes 2883584 | tf_op jit(solution)/shard_map/all_to_all | solution.py:98
  606.8 156.9 %all-reduce.9.cloned.1.call-start = ((), (), s32[]{:S(2)}) async-start(), calls=%async_computation.14 | async-start | bytes 2883584 | tf_op jit(solution)/shard_map/psum | solution.py:97
  782.3 6.8 copy-start.12
  782.3 7.0 copy-start.11
  782.3 7.4 copy-start.20
  782.3 29.0 %all-to-all-start.9 = ((bf16[16,2,22528]{2,1,0:T(2,128)(2,1)}), bf16[16,2,22528]{2,1,0:T(2,128)(2,1)S(1)}, u32[]{:S(2)}, u32[]{:S(2)}) async-start(bf16[16,2,22528]{2,1,0:T(2,128)(2,1)} %reshape.621), calls=%async_computation.9 | async-start | bytes 2883584 | tf_op jit(solution)/shard_map/all_to_all | solution.py:98
  789.0 156.7 %all-reduce.11.cloned.1.call-start = ((), (), s32[]{:S(2)}) async-start(), calls=%async_computation.15 | async-start | bytes 2883584 | tf_op jit(solution)/shard_map/psum | solution.py:97
  964.4 6.9 copy-start.22
  964.4 29.1 %all-to-all-start.11 = ((bf16[16,2,22528]{2,1,0:T(2,128)(2,1)}), bf16[16,2,22528]{2,1,0:T(2,128)(2,1)S(1)}, u32[]{:S(2)}, u32[]{:S(2)}) async-start(bf16[16,2,22528]{2,1,0:T(2,128)(2,1)} %reshape.623), calls=%async_computation.11 | async-start | bytes 2883584 | tf_op jit(solution)/shard_map/all_to_all | solution.py:98
  (12 other events, 43.0 us)
Sparse Core Ops, SparseCore 0:
  313.4 85.2 all-reduce.4
  506.9 74.4 all-reduce.6
  689.1 74.4 all-reduce.8
  871.1 74.4 all-reduce.10
where the time goes:
time: 1020 us; the launch traced here: 1010 us
  waiting for transfers between devices  523 us (51%)
  local copies, waits for them, and re-layouts  205 us (20%)
  blocking collectives  99 us (10%)
  other arithmetic  87.9 us (9%)
  starting transfers between devices  59.9 us (6%)
  matrix products  23.8 us (2%)
  between operations  14.3 us (1%)
    psum x4, waiting for transfers between devices, body(): summed = lax.psum(partial_value.astype(jnp.bfloat16), 'tp')  309 us
    all_to_all x3, blocking collectives, body(): lax.all_to_all(outgoing, 'fsdp', split_axis=0, concat_axis=1, tiled=True)  99 us
    all_to_all x4, waiting for transfers between devices, body(): lax.all_to_all(summed, 'fsdp', split_axis=1, concat_axis=0, tiled=True)  84 us
    all_to_all x1, waiting for transfers between devices, body(): lax.all_to_all(coded, 'tp', split_axis=2, concat_axis=0, tiled=True)  62.9 us
    unnamed x62, local copies, waits for them, and re-layouts  60.5 us
    unnamed x5, other arithmetic  46.6 us
    all_to_all x1, waiting for transfers between devices, body(): lax.all_to_all(lax.all_to_all(coded, 'tp', split_axis=2, concat_axis=0, t...  44 us
    all_to_all x4, starting transfers between devices, body(): lax.all_to_all(summed, 'fsdp', split_axis=1, concat_axis=0, tiled=True)  26.9 us
  transfers between devices with their start and end apart: 13, of which 11 were waited for; matrix products, arithmetic and copies ran while one was open for 9% of the time, Pallas kernels for 0%

commit v1 on v0

v1 whole, which is shorter than its diff:
```python
import jax
import jax.numpy as jnp
from jax import lax
from jax.experimental import pallas as pl
from jax.experimental.pallas import tpu as pltpu
from jax.sharding import Mesh, PartitionSpec as P

D = 4096
FF = 1536
TOPK = 8
EXPERTS = 16
QB = 128
STEPS = 4
CAP = 11
ROWS_DEV = 16
ROWS = 256
SLOTS = 16 * CAP
WIDTH = 512
HALF = 256
UNITS = 192
PAY = 192
EXT = 640
FIRST = 768

XZ = ("xh", "z")
CT = ("c", "xl", "y")
ALL = ("xh", "z", "c", "xl", "y")

norm_eps = 1e-06
scale_eps = 1e-06
code_limit = 448.0
smallest_normal = 0.015625
f32 = jnp.float32
bf16 = jnp.bfloat16

NN = (((1,), (0,)), ((), ()))
NT = (((1,), (1,)), ((), ()))


def dot(a, b, dims=NN):
    return lax.dot_general(a, b, dims, preferred_element_type=f32)


def split3(v):
    hi = v.astype(bf16)
    rest = v - hi.astype(f32)
    mid = rest.astype(bf16)
    low = (rest - mid.astype(f32)).astype(bf16)
    return hi, mid, low


def float_code(v):
    big = v * 1048577.0
    fine = big - (big - v)
    coarse = (v + 24576.0) - 24576.0
    return jnp.where(jnp.abs(v) < smallest_normal, coarse, fine)


def quant_kernel(which_ref, w_ref, gu_ref, dn_ref):
    for m in range(3):
        for q in range(3):
            for h in range(2):
                cols = slice(h * QB, (h + 1) * QB)
                tile = w_ref[0, m, q * QB : (q + 1) * QB, cols].astype(f32)
                top = jnp.max(jnp.abs(tile), axis=(0, 1), keepdims=True) + scale_eps
                scale = top / code_limit
                back = (float_code(tile * (1.0 / scale)) * scale).astype(bf16)
                if m == 2:
                    dn_ref[q * QB : (q + 1) * QB, cols] = back
                else:
                    for g in range(2):
                        unit = q * 2 + g
                        j, part = unit // 3, unit % 3
                        if m == 0:
                            to = j * 384 + part * 64
                        elif part < 2:
                            to = j * 384 + 256 + part * 64
                        else:
                            to = j * 384 + 192
                        gu_ref[to : to + 64, cols] = back[g * 64 : g * 64 + 64]


def quantize(which, w):
    return pl.pallas_call(
        quant_kernel,
        grid_spec=pltpu.PrefetchScalarGridSpec(
            num_scalar_prefetch=1,
            grid=(4,),
            in_specs=[pl.BlockSpec((1, 3, 384, HALF), lambda i, s: (s[0], 0, i, 0))],
            out_specs=[
                pl.BlockSpec((768, HALF), lambda i, s: (i, 0)),
                pl.BlockSpec((384, HALF), lambda i, s: (i, 0)),
            ],
        ),
        out_shape=[
            jax.ShapeDtypeStruct((2 * FF, HALF), bf16),
            jax.ShapeDtypeStruct((FF, HALF), bf16),
        ],
        name="quantize",
    )(which, w)


def prepare_kernel(
    ids_ref, own_ref, other_ref, gain_ref, x_ref, stream_ref, s_ref, st_ref, w_ref, rows
):
    core, tp, expert = ids_ref[0], ids_ref[1], ids_ref[2]
    rows[pl.ds(pl.multiple_of(core * 128, 128), 128), :] = own_ref[...]
    rows[pl.ds(pl.multiple_of((1 - core) * 128, 128), 128), :] = other_ref[...]
    stream_ref[...] = own_ref[pl.ds(pl.multiple_of(tp * 16, 16), 16), :WIDTH].astype(f32)
    rs = jnp.sum(rows[:, 640:768].astype(f32), axis=1, keepdims=True)
    x_ref[...] = (rows[:, :WIDTH].astype(f32) * rs * gain_ref[...]).astype(bf16)
    named = rows[:, 512:640].astype(f32)
    gates = pltpu.roll(named, 96, 1) + pltpu.roll(named, 64, 1) + pltpu.roll(named, 32, 1)
    lane = lax.broadcasted_iota(jnp.int32, (ROWS, 128), 1)
    match = jnp.where((named == expert.astype(f32)) & (lane < 32), 1.0, 0.0)
    weighted = match * gates
    group = lane // TOPK
    mask = jnp.zeros((ROWS, 128), f32)
    weight = jnp.zeros((ROWS, 128), f32)
    for s in range(STEPS):
        here = jnp.sum(jnp.where(group == s, match, 0.0), axis=1, keepdims=True)
        gate = jnp.sum(jnp.where(group == s, weighted, 0.0), axis=1, keepdims=True)
        mask = jnp.where(lane == s, here, mask)
        weight = jnp.where(lane == s, gate, weight)
    w_ref[...] = weight
    r0 = lax.broadcasted_iota(jnp.int32, (ROWS, ROWS), 0)
    r1 = lax.broadcasted_iota(jnp.int32, (ROWS, ROWS), 1)
    before = jnp.where(r1 < r0, 1.0, 0.0).astype(bf16)
    place = dot(before, mask.astype(bf16))
    slot = r1.astype(f32)
    for s in range(STEPS):
        hot = jnp.where((slot == place[:, s : s + 1]) & (mask[:, s : s + 1] > 0.0), 1.0, 0.0)
        st_ref[s] = hot.astype(bf16)
        s_ref[s] = hot.T[:SLOTS].astype(bf16)


def prepare(ids, own, other, gain):
    return pl.pallas_call(
        prepare_kernel,
        in_specs=[pl.BlockSpec(memory_space=pltpu.SMEM)] + [pl.BlockSpec()] * 3,
        out_shape=[
            jax.ShapeDtypeStruct((ROWS, WIDTH), bf16),
            jax.ShapeDtypeStruct((ROWS_DEV, WIDTH), f32),
            jax.ShapeDtypeStruct((STEPS, SLOTS, ROWS), bf16),
            jax.ShapeDtypeStruct((STEPS, ROWS, ROWS), bf16),
            jax.ShapeDtypeStruct((ROWS, 128), f32),
        ],
        scratch_shapes=[pltpu.VMEM((ROWS, FIRST), bf16)],
        name="prepare",
    )(ids, own, other, gain)


def gate_up_kernel(first, ids_ref, x_ref, s_ref, st_ref, wa_ref, wb_ref, p_ref):
    core = ids_ref[0]
    picked = dot(s_ref[...], x_ref[:, :WIDTH]).astype(bf16)
    left, right = picked[:, :HALF], picked[:, HALF:]
    xa = jnp.where(core == 0, left, right)
    xb = jnp.where(core == 0, right, left)
    if first:
        tail = jnp.zeros((PAY - SLOTS, 384), bf16)
    else:
        squares = jnp.sum(x_ref[:, WIDTH:].astype(f32), axis=1, keepdims=True)
        line = jnp.sum(st_ref[...].astype(f32) * squares, axis=0, keepdims=True)
        line = jnp.concatenate([line, jnp.zeros((1, 128), f32)], axis=1)
        hi, mid, low = split3(line)
        at = lax.broadcasted_iota(jnp.int32, (PAY - SLOTS, 384), 0)
        tail = jnp.where(
            at == 0,
            hi.astype(f32),
            jnp.where(at == 1, mid.astype(f32), jnp.where(at == 2, low.astype(f32), 0.0)),
        ).astype(bf16)
    for j in range(8):
        at = slice(j * 384, (j + 1) * 384)
        part = dot(xa, wa_ref[at, :], NT) + dot(xb, wb_ref[at, :], NT)
        p_ref[j, :SLOTS, :] = part.astype(bf16)
        p_ref[j, SLOTS:, :] = tail


def gate_up(first, ids, x, s, st, wa, wb):
    return pl.pallas_call(
        lambda *refs: gate_up_kernel(first, *refs),
        in_specs=[pl.BlockSpec(memory_space=pltpu.SMEM)] + [pl.BlockSpec()] * 5,
        out_shape=jax.ShapeDtypeStruct((8, PAY, 384), bf16),
        compiler_params=pltpu.CompilerParams(vmem_limit_bytes=32 << 20),
        name="gate_up",
    )(ids, x, s, st, wa, wb)


def act_kernel(first, p_ref, out_ref):
    total = p_ref[0].astype(f32)
    for j in range(1, 8):
        total = total + p_ref[j].astype(f32)
    sums = total[:SLOTS]
    if not first:
        line = jnp.sum(total[SLOTS : SLOTS + 8, :HALF], axis=0, keepdims=True)
        rs_line = lax.rsqrt(line * (1.0 / D) + norm_eps)
        r0 = lax.broadcasted_iota(jnp.int32, (SLOTS, HALF), 0)
        r1 = lax.broadcasted_iota(jnp.int32, (SLOTS, HALF), 1)
        rs = jnp.sum(jnp.where(r0 == r1, rs_line, 0.0), axis=1, keepdims=True)
        sums = sums * rs
    t0, t1, t2 = sums[:, :128], sums[:, 128:256], sums[:, 256:]
    a0 = jax.nn.silu(t0) * t2
    a1 = jax.nn.silu(t1) * pltpu.roll(t1, 64, 1)
    half = SLOTS // 2
    lane = lax.broadcasted_iota(jnp.int32, (half, 128), 1)
    middle = jnp.where(lane < 64, a1[:half], pltpu.roll(a1[half:], 64, 1))
    packed = jnp.concatenate([a0[:half], middle, a0[half:]], axis=1).astype(bf16)
    for j in range(8):
        out_ref[j] = packed


def activate(first, p):
    return pl.pallas_call(
        lambda *refs: act_kernel(first, *refs),
        out_shape=jax.ShapeDtypeStruct((8, SLOTS // 2, 384), bf16),
        name="activate",
    )(p)


def down_kernel(step, ids_ref, a_ref, st_ref, w_ref, wa_ref, wb_ref, out_ref):
    core = ids_ref[0]
    half = SLOTS // 2
    lane = lax.broadcasted_iota(jnp.int32, (half, 128), 1)
    sum_a = jnp.zeros((SLOTS, HALF), f32)
    sum_b = jnp.zeros((SLOTS, HALF), f32)
    for j in range(8):
        block = a_ref[j].astype(f32)
        middle = block[:, 128:256]
        low = jnp.concatenate([block[:, :128], jnp.where(lane < 64, middle, 0.0)], axis=1)
        high = jnp.concatenate([block[:, 256:], jnp.where(lane < 64, 0.0, middle)], axis=1)
        act = jnp.concatenate([low, high], axis=0).astype(bf16)
        at = j * UNITS
        wa = jnp.concatenate([wa_ref[at : at + UNITS, :], wa_ref[at + 128 : at + UNITS, :]], axis=0)
        wb = jnp.concatenate([wb_ref[at : at + UNITS, :], wb_ref[at + 128 : at + UNITS, :]], axis=0)
        sum_a = sum_a + dot(act, wa)
        sum_b = sum_b + dot(act, wb)
    left = jnp.where(core == 0, sum_a, sum_b).astype(bf16)
    right = jnp.where(core == 0, sum_b, sum_a).astype(bf16)
    weight = w_ref[:, step : step + 1]
    st = st_ref[:, :SLOTS]
    out_ref[:, :HALF] = (dot(st, left) * weight).astype(bf16)
    out_ref[:, HALF:] = (dot(st, right) * weight).astype(bf16)


def down(step, ids, a, st, w, wa, wb):
    return pl.pallas_call(
        lambda *refs: down_kernel(step, *refs),
        in_specs=[pl.BlockSpec(memory_space=pltpu.SMEM)] + [pl.BlockSpec()] * 5,
        out_shape=jax.ShapeDtypeStruct((ROWS, WIDTH), bf16),
        compiler_params=pltpu.CompilerParams(vmem_limit_bytes=32 << 20),
        name="down",
    )(ids, a, st, w, wa, wb)


def residual_kernel(p_ref, stream_ref, gain_ref, new_ref, x_ref):
    total = p_ref[0].astype(f32)
    for j in range(1, 16):
        total = total + p_ref[j].astype(f32)
    stream = stream_ref[...] + total
    new_ref[...] = stream
    hi, mid, low = split3(jnp.sum(stream * stream, axis=1, keepdims=True))
    lane = lax.broadcasted_iota(jnp.int32, (ROWS_DEV, 128), 1)
    parts = jnp.where(
        lane == 0,
        hi.astype(f32),
        jnp.where(lane == 1, mid.astype(f32), jnp.where(lane == 2, low.astype(f32), 0.0)),
    )
    row = jnp.concatenate([stream * gain_ref[...], parts], axis=1).astype(bf16)
    for j in range(16):
        x_ref[j] = row


def residual(p, stream, gain):
    return pl.pallas_call(
        residual_kernel,
        out_shape=[
            jax.ShapeDtypeStruct((ROWS_DEV, WIDTH), f32),
            jax.ShapeDtypeStruct((16, ROWS_DEV, EXT), bf16),
        ],
        name="residual",
    )(p, stream, gain)


def last_kernel(p_ref, stream_ref, new_ref):
    total = p_ref[0].astype(f32)
    for j in range(1, 16):
        total = total + p_ref[j].astype(f32)
    new_ref[...] = stream_ref[...] + total


def last(p, stream):
    return pl.pallas_call(
        last_kernel,
        out_shape=jax.ShapeDtypeStruct((ROWS_DEV, WIDTH), f32),
        name="last",
    )(p, stream)


def exchange(x, axes):
    return lax.all_to_all(x, axes, split_axis=0, concat_axis=0, tiled=True)


def reduced(v):
    return lax.reduce_precision(v, exponent_bits=8, mantissa_bits=7)


def parts3(v):
    hi = reduced(v)
    mid = reduced(v - hi)
    return [hi, mid, v - hi - mid]


def body(trainer_weights, hidden_in, norm_gain, routing, gate_weights):
    core = lax.axis_index("c")
    tp = lax.axis_index(("xl", "y"))
    xz = lax.axis_index(XZ)
    ids = jnp.stack([core, tp, 2 * tp + core]).astype(jnp.int32)
    zero = jnp.zeros((1,), jnp.int32)
    gain = lax.dynamic_slice(norm_gain, (xz * WIDTH,), (WIDTH,)).reshape(1, WIDTH)

    given = lax.dynamic_index_in_dim(trainer_weights, 1 - core, 0, keepdims=True)
    taken = lax.ppermute(given, "c", [(0, 1), (1, 0)])

    hidden = hidden_in.astype(f32)
    rs = lax.rsqrt(jnp.mean(hidden * hidden, axis=-1, keepdims=True) + norm_eps)
    flat = lambda v: jnp.transpose(v, (1, 0, 2)).reshape(ROWS_DEV, STEPS * TOPK)
    extra = jnp.concatenate(
        [flat(routing).astype(f32)] + parts3(flat(gate_weights)) + parts3(rs)
        + [jnp.zeros((ROWS_DEV, 125), f32)],
        axis=1,
    ).astype(bf16)
    pieces = jnp.transpose(hidden_in.reshape(ROWS_DEV, 8, WIDTH), (1, 0, 2))
    extra = jnp.broadcast_to(extra[None], (8, ROWS_DEV, FIRST - WIDTH))
    own = exchange(jnp.concatenate([pieces, extra], axis=2), XZ).reshape(128, FIRST)
    other = lax.ppermute(own, "c", [(0, 1), (1, 0)])

    gu_a, dn_a = quantize(core.astype(jnp.int32).reshape(1), trainer_weights)
    gu_b, dn_b = quantize(zero, taken)
    x, stream, s, st, w = prepare(ids, own, other, gain)

    for step in range(STEPS):
        first = step == 0
        partial = gate_up(first, ids, x, s[step], st[step], gu_a, gu_b)
        act = activate(first, exchange(partial, XZ))
        back = down(step, ids, exchange(act, XZ), st[step], w, dn_a, dn_b)
        sums = exchange(back.reshape(16, ROWS_DEV, WIDTH), CT)
        if step < STEPS - 1:
            stream, rows = residual(sums, stream, gain)
            x = exchange(rows, CT).reshape(ROWS, EXT)
        else:
            stream = last(sums, stream)

    turn = [
        ((a * 2 + c) * 8 + b, (b * 2 + c) * 8 + a)
        for a in range(8)
        for c in range(2)
        for b in range(8)
    ]
    mine = lax.ppermute(stream, ALL, turn)
    whole = exchange(jnp.broadcast_to(mine[None], (8, ROWS_DEV, WIDTH)), ("xl", "y"))
    return jnp.transpose(whole, (1, 0, 2)).reshape(ROWS_DEV, D)


def solution(mesh):
    fine = Mesh(mesh.devices.reshape(2, 4, 2, 2, 4), ALL)
    fsdp, tp = ("xh", "z", "c"), ("xl", "y")
    in_specs = (
        P(tp, None, None, fsdp),
        P(fsdp, None),
        P(),
        P(None, fsdp, None),
        P(None, fsdp, None),
    )
    return jax.shard_map(
        body, mesh=fine, in_specs=in_specs, out_specs=P(fsdp, None), check_vma=False
    )
```

time: 1020 us -> 334 us (0.33)
  waiting for transfers between devices: 523 us -> 0.01 us
  local copies, waits for them, and re-layouts: 205 us -> 19.5 us
  blocking collectives: 99 us -> 268 us
  other arithmetic: 87.9 us -> 0.75 us
  starting transfers between devices: 59.9 us -> 1.41 us
  Pallas kernels: 0 us -> 42.3 us
  matrix products: 23.8 us -> 0 us
  between operations: 14.3 us -> 0.18 us
    psum x4 -> x0, waiting for transfers between devices: 309 us -> none  [body(): summed = lax.psum(partial_value.astype(jnp.bfloat16), 'tp')]
    all_to_all x9 -> x0, waiting for transfers between devices: 214 us -> none  [the longest x4 84 us: body(): lax.all_to_all(summed, 'fsdp', split_axis=1, concat_axis=0, tiled=True)]
    all_to_all x3 -> x17, blocking collectives: 99 us -> 268 us  [exchange(): return lax.all_to_all(x, axes, split_axis=0, concat_axis=0, tiled=True)]
    all_to_all x9 -> x0, starting transfers between devices: 59.7 us -> none  [the longest x4 26.9 us: body(): lax.all_to_all(summed, 'fsdp', split_axis=1, concat_axis=0, tiled=True)]
    unnamed x62 -> x52, local copies, waits for them, and re-layouts: 60.5 us -> 10 us
    unnamed x5 -> x0, other arithmetic: 46.6 us -> none
    pallas_call x0 -> x19, Pallas kernels: none -> 42.3 us  [the longest x2 10.3 us: quantize(): pl.pallas_call(quant_kernel, grid_spec=pltpu.PrefetchScalarGridSpec(num_s...]
    convert_element_type x5 -> x1, local copies, waits for them, and re-layouts: 26.1 us -> 0.08 us  [body(): flat(routing).astype(f32)]
  transfers between devices with their start and end apart: 13 -> 3, of which waited for: 11 -> 0; matrix products, arithmetic and copies ran while one was open for 9% -> 2% of each run, Pallas kernels for 0% -> 2%
where the time goes in v1:
time: 334 us; the launch traced here: 332 us
  blocking collectives  268 us (80%)
  Pallas kernels  42.3 us (13%)
  local copies, waits for them, and re-layouts  19.5 us (6%)
    all_to_all x17, blocking collectives, exchange(): return lax.all_to_all(x, axes, split_axis=0, concat_axis=0, tiled=True)  268 us
    pallas_call x2, Pallas kernels, quantize(): pl.pallas_call(quant_kernel, grid_spec=pltpu.PrefetchScalarGridSpec(num_s...  10.3 us
    unnamed x52, local copies, waits for them, and re-layouts  10 us
    pallas_call x4, Pallas kernels, activate(): pl.pallas_call(lambda *refs: act_kernel(first, *refs), out_shape=jax.Shap...  9.51 us
    pallas_call x4, Pallas kernels, gate_up(): pl.pallas_call(lambda *refs: gate_up_kernel(first, *refs), in_specs=[pl.B...  7.17 us
  transfers between devices with their start and end apart: 3, of which 0 were waited for; matrix products, arithmetic and copies ran while one was open for 2% of the time, Pallas kernels for 2%

profile of v1, /device:TPU:0, one launch (start us, length us, event | category | flops | bytes accessed | tf_op | source)
XLA Modules:
  0.0 332.0 jit_solution(2455095745942721063)
XLA Ops:
  0.0 3.3 constant_dynamic-slice_fusion
  4.1 16.4 %all_to_all.85 = bf16[8,16,768]{2,1,0:T(8,128)(2,1)S(1)} all-to-all(bf16[8,16,768]{2,1,0:T(8,128)(2,1)S(1)} %pad_maximum_fusion), channel_id=1, replica_groups=mesh['xh'=2,'z'=4,'c'=2,'xl'=2,'y'=4] {'xh','z'}, dimensions={0} | all-to-all | bytes 393216 | tf_op jit(solution)/shard_map/all_to_all | solution.py:300
  20.5 5.1 %quantize.2 = (bf16[3072,256]{1,0:T(8,128)(2,1)}, bf16[1536,256]{1,0:T(8,128)(2,1)}) custom-call(s32[1]{0:T(128)} %bitcast.which_ref, bf16[2,3,1536,256]{3,2,1,0:T(8,128)(2,1)} %w_ref.1), custom_call_target="tpu_custom_call" | custom-call | tf_op jit(solution)/shard_map/quantize/pallas_call | solution.py:84
  28.2 3.0 prepare.1
  34.8 5.2 %quantize.3 = (bf16[3072,256]{1,0:T(8,128)(2,1)}, bf16[1536,256]{1,0:T(8,128)(2,1)}) custom-call(s32[1]{0:T(128)} %constant.47.clone.1.which_ref, bf16[1,3,1536,256]{3,2,1,0:T(8,128)(2,1)} %collective-permute-done.1.w_ref), custom_call_target="tpu_custom_call" | custom-call | tf_op jit(solution)/shard_map/quantize/pallas_call | solution.py:84
  43.2 22.6 %all_to_all.86.refs_0_ = bf16[8,192,384]{2,1,0:T(8,128)(2,1)} all-to-all(bf16[8,192,384]{2,1,0:T(8,128)(2,1)S(1)} %gate_up.4), channel_id=1, replica_groups=mesh['xh'=2,'z'=4,'c'=2,'xl'=2,'y'=4] {'xh','z'}, dimensions={0} | all-to-all | bytes 2359296 | tf_op jit(solution)/shard_map/all_to_all | solution.py:300
  68.2 15.1 %all_to_all.87.refs_1_ = bf16[8,88,384]{2,1,0:T(8,128)(2,1)S(1)} all-to-all(bf16[8,88,384]{2,1,0:T(8,128)(2,1)} %activate.4), channel_id=1, replica_groups=mesh['xh'=2,'z'=4,'c'=2,'xl'=2,'y'=4] {'xh','z'}, dimensions={0} | all-to-all | bytes 1081344 | tf_op jit(solution)/shard_map/all_to_all | solution.py:300
  86.6 12.4 %all_to_all.88.p_ref = bf16[16,16,512]{2,1,0:T(8,128)(2,1)} all-to-all(bf16[16,16,512]{2,1,0:T(8,128)(2,1)S(1)} %bitcast.56), channel_id=1, replica_groups=mesh['xh'=2,'z'=4,'c'=2,'xl'=2,'y'=4] {'c','xl','y'}, dimensions={0} | all-to-all | bytes 524288 | tf_op jit(solution)/shard_map/all_to_all | solution.py:300
  100.8 12.1 %all_to_all.89 = bf16[16,16,640]{2,1,0:T(8,128)(2,1)S(1)} all-to-all(bf16[16,16,640]{2,1,0:T(8,128)(2,1)} %get-tuple-element.29), channel_id=1, replica_groups=mesh['xh'=2,'z'=4,'c'=2,'xl'=2,'y'=4] {'c','xl','y'}, dimensions={0} | all-to-all | bytes 655360 | tf_op jit(solution)/shard_map/all_to_all | solution.py:300
  116.5 22.4 %all_to_all.90.refs_0_ = bf16[8,192,384]{2,1,0:T(8,128)(2,1)} all-to-all(bf16[8,192,384]{2,1,0:T(8,128)(2,1)S(1)} %gate_up.5), channel_id=1, replica_groups=mesh['xh'=2,'z'=4,'c'=2,'xl'=2,'y'=4] {'xh','z'}, dimensions={0} | all-to-all | bytes 2359296 | tf_op jit(solution)/shard_map/all_to_all | solution.py:300
  138.9 2.4 activate.5
  141.3 15.1 %all_to_all.91.refs_1_ = bf16[8,88,384]{2,1,0:T(8,128)(2,1)S(1)} all-to-all(bf16[8,88,384]{2,1,0:T(8,128)(2,1)} %activate.5), channel_id=1, replica_groups=mesh['xh'=2,'z'=4,'c'=2,'xl'=2,'y'=4] {'xh','z'}, dimensions={0} | all-to-all | bytes 1081344 | tf_op jit(solution)/shard_map/all_to_all | solution.py:300
  159.7 11.1 %all_to_all.92.p_ref = bf16[16,16,512]{2,1,0:T(8,128)(2,1)} all-to-all(bf16[16,16,512]{2,1,0:T(8,128)(2,1)S(1)} %bitcast.57), channel_id=1, replica_groups=mesh['xh'=2,'z'=4,'c'=2,'xl'=2,'y'=4] {'c','xl','y'}, dimensions={0} | all-to-all | bytes 524288 | tf_op jit(solution)/shard_map/all_to_all | solution.py:300
  172.7 12.1 %all_to_all.93 = bf16[16,16,640]{2,1,0:T(8,128)(2,1)S(1)} all-to-all(bf16[16,16,640]{2,1,0:T(8,128)(2,1)} %get-tuple-element.31), channel_id=1, replica_groups=mesh['xh'=2,'z'=4,'c'=2,'xl'=2,'y'=4] {'c','xl','y'}, dimensions={0} | all-to-all | bytes 655360 | tf_op jit(solution)/shard_map/all_to_all | solution.py:300
  187.4 22.4 %all_to_all.94.refs_0_ = bf16[8,192,384]{2,1,0:T(8,128)(2,1)} all-to-all(bf16[8,192,384]{2,1,0:T(8,128)(2,1)S(1)} %gate_up.6), channel_id=1, replica_groups=mesh['xh'=2,'z'=4,'c'=2,'xl'=2,'y'=4] {'xh','z'}, dimensions={0} | all-to-all | bytes 2359296 | tf_op jit(solution)/shard_map/all_to_all | solution.py:300
  209.8 2.4 activate.6
  212.2 15.1 %all_to_all.95.refs_1_ = bf16[8,88,384]{2,1,0:T(8,128)(2,1)S(1)} all-to-all(bf16[8,88,384]{2,1,0:T(8,128)(2,1)} %activate.6), channel_id=1, replica_groups=mesh['xh'=2,'z'=4,'c'=2,'xl'=2,'y'=4] {'xh','z'}, dimensions={0} | all-to-all | bytes 1081344 | tf_op jit(solution)/shard_map/all_to_all | solution.py:300
  229.7 11.3 %all_to_all.96.p_ref = bf16[16,16,512]{2,1,0:T(8,128)(2,1)} all-to-all(bf16[16,16,512]{2,1,0:T(8,128)(2,1)S(1)} %bitcast.58), channel_id=1, replica_groups=mesh['xh'=2,'z'=4,'c'=2,'xl'=2,'y'=4] {'c','xl','y'}, dimensions={0} | all-to-all | bytes 524288 | tf_op jit(solution)/shard_map/all_to_all | solution.py:300
  242.8 12.1 %all_to_all.97 = bf16[16,16,640]{2,1,0:T(8,128)(2,1)S(1)} all-to-all(bf16[16,16,640]{2,1,0:T(8,128)(2,1)} %get-tuple-element.33), channel_id=1, replica_groups=mesh['xh'=2,'z'=4,'c'=2,'xl'=2,'y'=4] {'c','xl','y'}, dimensions={0} | all-to-all | bytes 655360 | tf_op jit(solution)/shard_map/all_to_all | solution.py:300
  256.7 22.4 %all_to_all.98.refs_0_ = bf16[8,192,384]{2,1,0:T(8,128)(2,1)} all-to-all(bf16[8,192,384]{2,1,0:T(8,128)(2,1)S(1)} %gate_up.7), channel_id=1, replica_groups=mesh['xh'=2,'z'=4,'c'=2,'xl'=2,'y'=4] {'xh','z'}, dimensions={0} | all-to-all | bytes 2359296 | tf_op jit(solution)/shard_map/all_to_all | solution.py:300
  279.1 2.5 activate.7
  281.6 14.9 %all_to_all.99.refs_1_ = bf16[8,88,384]{2,1,0:T(8,128)(2,1)S(1)} all-to-all(bf16[8,88,384]{2,1,0:T(8,128)(2,1)} %activate.7), channel_id=1, replica_groups=mesh['xh'=2,'z'=4,'c'=2,'xl'=2,'y'=4] {'xh','z'}, dimensions={0} | all-to-all | bytes 1081344 | tf_op jit(solution)/shard_map/all_to_all | solution.py:300
  297.8 11.1 %all_to_all.100.p_ref = bf16[16,16,512]{2,1,0:T(8,128)(2,1)} all-to-all(bf16[16,16,512]{2,1,0:T(8,128)(2,1)S(1)} %bitcast.55), channel_id=1, replica_groups=mesh['xh'=2,'z'=4,'c'=2,'xl'=2,'y'=4] {'c','xl','y'}, dimensions={0} | all-to-all | bytes 524288 | tf_op jit(solution)/shard_map/all_to_all | solution.py:300
  312.0 19.2 %all_to_all.101 = f32[8,16,512]{2,1,0:T(8,128)S(1)} all-to-all(f32[8,16,512]{2,1,0:T(8,128)S(1)} %broadcast_in_dim.8), channel_id=1, replica_groups=mesh['xh'=2,'z'=4,'c'=2,'xl'=2,'y'=4] {'xl','y'}, dimensions={0} | all-to-all | bytes 524288 | tf_op jit(solution)/shard_map/all_to_all | solution.py:300
  (91 shorter events, 40.2 us)
Async XLA Ops:
  0.0 3.3 copy-start.24
  0.0 3.4 %copy-start.22 = (bf16[16,4096]{1,0:T(8,128)(2,1)S(1)}, bf16[16,4096]{1,0:T(8,128)(2,1)}, u32[]{:S(2)}) copy-start(bf16[16,4096]{1,0:T(8,128)(2,1)} %param.6) | copy-start | bytes 393220
  0.0 3.8 %copy-start.25 = (s32[4,16,8]{1,2,0:T(8,128)S(1)}, s32[4,16,8]{1,2,0:T(8,128)}, u32[]{:S(2)}) copy-start(s32[4,16,8]{1,2,0:T(8,128)} %param.8) | copy-start | bytes 6148
  3.3 31.5 %collective-permute-start.1 = (bf16[1,3,1536,256]{3,2,1,0:T(8,128)(2,1)}, bf16[1,3,1536,256]{3,2,1,0:T(8,128)(2,1)}, u32[]{:S(2)}, u32[]{:S(2)}) collective-permute-start(bf16[1,3,1536,256]{3,2,1,0:T(8,128)(2,1)} %constant_dynamic-slice_fusion), channel_id=1, source_target_pairs={{0,8},{8,0},{1,9},{9,1},{2,10},{10,2},{3,11},{11,3},{4,12},{12,4},... | collective-permute-start | bytes 7077896 | tf_op jit(solution)/shard_map/ppermute | solution.py:322
  20.5 5.1 %copy-start.21 = (bf16[8,16,768]{2,1,0:T(8,128)(2,1)}, bf16[8,16,768]{2,1,0:T(8,128)(2,1)S(1)}, u32[]{:S(2)}) copy-start(bf16[8,16,768]{2,1,0:T(8,128)(2,1)S(1)} %all_to_all.85) | copy-start | bytes 589828
  20.5 7.0 %collective-permute-start = (bf16[128,768]{1,0:T(8,128)(2,1)S(1)}, bf16[128,768]{1,0:T(8,128)(2,1)S(1)}, u32[]{:S(2)}, u32[]{:S(2)}) collective-permute-start(bf16[128,768]{1,0:T(8,128)(2,1)S(1)} %bitcast.60), channel_id=1, source_target_pairs={{0,8},{8,0},{1,9},{9,1},{2,10},{10,2},{3,11},{11,3},{4,12},{12,4},... | collective-permute-start | bytes 589832 | tf_op jit(solution)/shard_map/ppermute | solution.py:335
  34.8 5.2 %copy-start.14 = (bf16[256,256]{1,0:T(8,128)(2,1)}, bf16[256,256]{1,0:T(8,128)(2,1)S(1)}, u32[]{:S(2)}) copy-start(bf16[256,256]{1,0:T(8,128)(2,1)S(1)} %get-tuple-element.38.refs_3_.refs_2_) | copy-start | bytes 393220
  34.8 5.2 %copy-start = (bf16[3072,256]{1,0:T(8,128)(2,1)S(1)}, bf16[3072,256]{1,0:T(8,128)(2,1)}, u32[]{:S(2)}) copy-start(bf16[3072,256]{1,0:T(8,128)(2,1)} %get-tuple-element.23.refs_4_) | copy-start | bytes 4718596
  34.8 5.2 %copy-start.19 = (bf16[256,512]{1,0:T(8,128)(2,1)S(1)}, bf16[256,512]{1,0:T(8,128)(2,1)}, u32[]{:S(2)}) copy-start(bf16[256,512]{1,0:T(8,128)(2,1)} %get-tuple-element.20.refs_1_) | copy-start | bytes 786436
  34.8 5.2 %copy-start.20 = (s32[3]{0:T(128)S(1)}, s32[3]{0:T(128)}, u32[]{:S(2)}) copy-start(s32[3]{0:T(128)} %pad_add_fusion.ids_ref.refs_0_) | copy-start | bytes 40
  40.0 1.4 copy-start.1
  65.8 17.4 %copy-start.11 = (f32[256,128]{1,0:T(8,128)S(1)}, f32[256,128]{1,0:T(8,128)}, u32[]{:S(2)}) copy-start(f32[256,128]{1,0:T(8,128)} %get-tuple-element.25.refs_3_) | copy-start | bytes 393220
  68.2 15.1 %copy-start.3 = (bf16[1536,256]{1,0:T(8,128)(2,1)S(1)}, bf16[1536,256]{1,0:T(8,128)(2,1)}, u32[]{:S(2)}) copy-start(bf16[1536,256]{1,0:T(8,128)(2,1)} %get-tuple-element.26.refs_4_) | copy-start | bytes 2359300
  83.3 1.1 copy-start.7
  85.3 27.6 %copy-start.2 = (bf16[3072,256]{1,0:T(8,128)(2,1)S(1)}, bf16[3072,256]{1,0:T(8,128)(2,1)}, u32[]{:S(2)}) copy-start(bf16[3072,256]{1,0:T(8,128)(2,1)} %get-tuple-element.24.refs_5_) | copy-start | bytes 4718596
  112.9 0.9 copy-start.12
  141.3 15.1 %copy-start.4 = (bf16[1536,256]{1,0:T(8,128)(2,1)S(1)}, bf16[1536,256]{1,0:T(8,128)(2,1)}, u32[]{:S(2)}) copy-start(bf16[1536,256]{1,0:T(8,128)(2,1)} %get-tuple-element.26.refs_4_) | copy-start | bytes 2359300
  156.4 1.1 copy-start.8
  212.2 15.1 %copy-start.5 = (bf16[1536,256]{1,0:T(8,128)(2,1)S(1)}, bf16[1536,256]{1,0:T(8,128)(2,1)}, u32[]{:S(2)}) copy-start(bf16[1536,256]{1,0:T(8,128)(2,1)} %get-tuple-element.26.refs_4_) | copy-start | bytes 2359300
  227.3 1.1 copy-start.9
  229.7 25.2 %copy-start.16 = (bf16[176,256]{1,0:T(8,128)(2,1)S(1)}, bf16[176,256]{1,0:T(8,128)(2,1)}, u32[]{:S(2)}) copy-start(bf16[176,256]{1,0:T(8,128)(2,1)} %get-tuple-element.39.refs_2_) | copy-start | bytes 270340
  279.1 17.4 %copy-start.6 = (bf16[1536,256]{1,0:T(8,128)(2,1)S(1)}, bf16[1536,256]{1,0:T(8,128)(2,1)}, u32[]{:S(2)}) copy-start(bf16[1536,256]{1,0:T(8,128)(2,1)} %get-tuple-element.26.refs_4_) | copy-start | bytes 2359300
  279.1 17.4 %copy-start.10 = (bf16[1536,256]{1,0:T(8,128)(2,1)S(1)}, bf16[1536,256]{1,0:T(8,128)(2,1)}, u32[]{:S(2)}) copy-start(bf16[1536,256]{1,0:T(8,128)(2,1)} %get-tuple-element.27.refs_5_) | copy-start | bytes 2359300
  310.6 1.4 collective-permute-start.2
  (5 other events, 4.3 us)

commit v2 on v1

v2 whole, which is shorter than its diff:
```python
import jax
import jax.numpy as jnp
from jax import lax
from jax.experimental import pallas as pl
from jax.experimental.pallas import tpu as pltpu
from jax.sharding import Mesh, PartitionSpec as P

D = 4096
FF = 1536
TOPK = 8
EXPERTS = 16
QB = 128
STEPS = 4
CAP = 11
ROWS_DEV = 16
ROWS = 256
SLOTS = 16 * CAP
UNIT_HALF = 768
WIDTH = 1024
HALF = 256
UNITS = 192
PAY = 192
EXT = 1152
FIRST = 1280

XZ = ("xh", "z")
XT = ("xh", "xl", "y")
T = ("xl", "y")
ALL = ("xh", "z", "c", "xl", "y")

norm_eps = 1e-06
scale_eps = 1e-06
code_limit = 448.0
smallest_normal = 0.015625
f32 = jnp.float32
bf16 = jnp.bfloat16

NN = (((1,), (0,)), ((), ()))
NT = (((1,), (1,)), ((), ()))


def dot(a, b, dims=NN):
    return lax.dot_general(a, b, dims, preferred_element_type=f32)


def busy(us):
    return pl.CostEstimate(flops=int(us * 1.15e9), bytes_accessed=0, transcendentals=0)


def split3(v):
    hi = v.astype(bf16)
    rest = v - hi.astype(f32)
    mid = rest.astype(bf16)
    low = (rest - mid.astype(f32)).astype(bf16)
    return hi, mid, low


def float_code(v):
    big = v * 1048577.0
    fine = big - (big - v)
    coarse = (v + 24576.0) - 24576.0
    return jnp.where(jnp.abs(v) < smallest_normal, coarse, fine)


def quant_block(tile):
    tile = tile.astype(f32)
    top = jnp.max(jnp.abs(tile), axis=(0, 1), keepdims=True) + scale_eps
    scale = top / code_limit
    return (float_code(tile * (1.0 / scale)) * scale).astype(bf16)


def quant_gate_up(src, out_ref, group):
    for m in range(2):
        for q in range(3):
            for h in range(2):
                cols = slice(h * QB, (h + 1) * QB)
                back = quant_block(src[m, q * QB : (q + 1) * QB, cols])
                for g in range(2):
                    unit = q * 2 + g
                    j, part = unit // 3, unit % 3
                    if m == 0:
                        to = part * 64
                    elif part < 2:
                        to = 256 + part * 64
                    else:
                        to = 192
                    to = group * 768 + j * 384 + to
                    out_ref[to : to + 64, cols] = back[g * 64 : g * 64 + 64]


def quant_down(src, out_ref, at, blocks):
    for q in range(blocks):
        for h in range(2):
            cols = slice(h * QB, (h + 1) * QB)
            back = quant_block(src[q * QB : (q + 1) * QB, cols])
            out_ref[at + q * QB : at + (q + 1) * QB, cols] = back


def quant_far_kernel(ids_ref, w_ref, near_ref, diag_ref, buf, sem):
    core, half = ids_ref[0], 1 - ids_ref[3]
    copies = []
    for p in range(2):
        for g in range(2):
            expert = core if p == 0 else 1 - core
            at = pl.multiple_of(half * UNIT_HALF + g * 384, 128)
            src = w_ref.at[expert, pl.ds(0, 2), pl.ds(at, 384), :]
            copies.append(pltpu.make_async_copy(src, buf.at[p * 2 + g], sem.at[p * 2 + g]))
    for copy in copies:
        copy.start()
    for p in range(2):
        for g in range(2):
            copies[p * 2 + g].wait()
            quant_gate_up(buf.at[p * 2 + g], diag_ref if p else near_ref, g)


def quantize_far(ids, w):
    out = jax.ShapeDtypeStruct((2 * UNIT_HALF, HALF), bf16)
    return pl.pallas_call(
        quant_far_kernel,
        in_specs=[
            pl.BlockSpec(memory_space=pltpu.SMEM),
            pl.BlockSpec(memory_space=pltpu.HBM),
        ],
        out_shape=[out, out],
        scratch_shapes=[pltpu.VMEM((4, 2, 384, HALF), bf16), pltpu.SemaphoreType.DMA((4,))],
        compiler_params=pltpu.CompilerParams(vmem_limit_bytes=60 << 20),
        name="quantize_far",
    )(ids, w)


def quant_rest_kernel(
    ids_ref, w_ref, own_ref, other_ref, near_ref, diag_ref, buf, sem, down_buf, down_sem
):
    core, half = ids_ref[0], ids_ref[3]
    copies = []
    for p in range(2):
        expert = core if p == 0 else 1 - core
        for g in range(2):
            at = pl.multiple_of(half * UNIT_HALF + g * 384, 128)
            src = w_ref.at[expert, :, pl.ds(at, 384), :]
            copies.append(pltpu.make_async_copy(src, buf.at[p * 2 + g], sem.at[p * 2 + g]))
    down_copies = []
    for p in range(2):
        expert = core if p == 0 else 1 - core
        at = pl.multiple_of((1 - half) * UNIT_HALF, 128)
        src = w_ref.at[expert, 2, pl.ds(at, UNIT_HALF), :]
        down_copies.append(pltpu.make_async_copy(src, down_buf.at[p], down_sem.at[p]))
    for copy in copies + down_copies:
        copy.start()
    for p in range(2):
        out_ref = other_ref if p else own_ref
        for g in range(2):
            copies[p * 2 + g].wait()
            quant_gate_up(buf.at[p * 2 + g], out_ref, g)
            quant_down(buf.at[p * 2 + g, 2], out_ref, 2 * UNIT_HALF + g * 384, 3)
    for p in range(2):
        down_copies[p].wait()
        quant_down(down_buf.at[p], diag_ref if p else near_ref, 0, 6)


def quantize_rest(ids, w):
    whole = jax.ShapeDtypeStruct((3 * UNIT_HALF, HALF), bf16)
    third = jax.ShapeDtypeStruct((UNIT_HALF, HALF), bf16)
    return pl.pallas_call(
        quant_rest_kernel,
        in_specs=[
            pl.BlockSpec(memory_space=pltpu.SMEM),
            pl.BlockSpec(memory_space=pltpu.HBM),
        ],
        out_shape=[whole, whole, third, third],
        scratch_shapes=[
            pltpu.VMEM((4, 3, 384, HALF), bf16),
            pltpu.SemaphoreType.DMA((4,)),
            pltpu.VMEM((2, UNIT_HALF, HALF), bf16),
            pltpu.SemaphoreType.DMA((2,)),
        ],
        compiler_params=pltpu.CompilerParams(vmem_limit_bytes=60 << 20),
        name="quantize_rest",
    )(ids, w)


def spread_kernel(ids_ref, own_ref, far_ref, *out_refs):
    half, z = ids_ref[3], ids_ref[4]
    for d in range(4):
        at = (z + d) % 4
        out_refs[d][half] = own_ref[at]
        out_refs[d][1 - half] = far_ref[at]


def spread(ids, own, far):
    return pl.pallas_call(
        spread_kernel,
        in_specs=[pl.BlockSpec(memory_space=pltpu.SMEM)] + [pl.BlockSpec()] * 2,
        out_shape=[jax.ShapeDtypeStruct((2, ROWS_DEV, FIRST), bf16)] * 4,
        compiler_params=pltpu.CompilerParams(vmem_limit_bytes=4 << 20),
        name="spread",
    )(ids, own, far)


def prepare_kernel(ids_ref, own_ref, other_ref, gain_ref, x_ref, stream_ref, tab_ref, rows, tab):
    core, tp, expert, half, z = [ids_ref[i] for i in range(5)]
    for d in range(4):
        for far in range(2):
            at = (far * 4 + (z - d + 4) % 4) * 16
            rows[pl.ds(pl.multiple_of(core * 128 + at, 16), 16), :] = own_ref[d, far]
            rows[pl.ds(pl.multiple_of((1 - core) * 128 + at, 16), 16), :] = other_ref[d, far]
    named = rows[:, WIDTH : WIDTH + 128].astype(f32)
    gates = pltpu.roll(named, 96, 1) + pltpu.roll(named, 64, 1) + pltpu.roll(named, 32, 1)
    lane = lax.broadcasted_iota(jnp.int32, (ROWS, 128), 1)
    match = jnp.where((named == expert.astype(f32)) & (lane < 32), 1.0, 0.0)
    weighted = match * gates
    group = lane // TOPK
    mask = jnp.zeros((ROWS, 128), f32)
    weight = jnp.zeros((ROWS, 128), f32)
    for s in range(STEPS):
        here = jnp.sum(jnp.where(group == s, match, 0.0), axis=1, keepdims=True)
        gate = jnp.sum(jnp.where(group == s, weighted, 0.0), axis=1, keepdims=True)
        mask = jnp.where(lane == s, here, mask)
        weight = jnp.where(lane == s, gate, weight)
    r0 = lax.broadcasted_iota(jnp.int32, (ROWS, ROWS), 0)
    r1 = lax.broadcasted_iota(jnp.int32, (ROWS, ROWS), 1)
    before = jnp.where(r1 < r0, 1.0, 0.0).astype(bf16)
    place = jnp.where(mask > 0.0, dot(before, mask.astype(bf16)), -1.0)
    tab[...] = jnp.where(lane < 64, weight, pltpu.roll(place, 64, 1))
    for c in range(2):
        for far in range(2):
            for u in range(4):
                at = pl.multiple_of(c * 128 + far * 64 + ((u - z + 4) % 4) * 16, 16)
                to = slice(c * 128 + far * 64 + u * 16, c * 128 + far * 64 + u * 16 + 16)
                block = rows[pl.ds(at, 16), :].astype(f32)
                rs = jnp.sum(block[:, WIDTH + 128 :], axis=1, keepdims=True)
                x_ref[to, :] = (block[:, :WIDTH] * rs * gain_ref[...]).astype(bf16)
                tab_ref[to, :] = tab[pl.ds(at, 16), :]
    at = core * 128 + half * 64 + ((tp // 2 - z + 4) % 4) * 16
    mine = rows[pl.ds(pl.multiple_of(at, 16), 16), :WIDTH].astype(f32)
    stream_ref[...] = jnp.where(tp % 2 == 0, mine[:8], mine[8:])


def prepare(ids, own, other, gain):
    return pl.pallas_call(
        prepare_kernel,
        in_specs=[pl.BlockSpec(memory_space=pltpu.SMEM)] + [pl.BlockSpec()] * 3,
        out_shape=[
            jax.ShapeDtypeStruct((ROWS, WIDTH), bf16),
            jax.ShapeDtypeStruct((8, WIDTH), f32),
            jax.ShapeDtypeStruct((ROWS, 128), f32),
        ],
        scratch_shapes=[pltpu.VMEM((ROWS, FIRST), bf16), pltpu.VMEM((ROWS, 128), f32)],
        compiler_params=pltpu.CompilerParams(vmem_limit_bytes=8 << 20),
        name="prepare",
    )(ids, own, other, gain)


def one_hot(tab_ref, step):
    slot = lax.broadcasted_iota(jnp.int32, (ROWS, ROWS), 1).astype(f32)
    return jnp.where(slot == tab_ref[:, 64 + step : 65 + step], 1.0, 0.0)


def block_at(ids_ref):
    core, half = ids_ref[0], ids_ref[3]
    far = 1 - half
    return [half * 2 + core, half * 2 + 1 - core, far * 2 + core, far * 2 + 1 - core]


def gate_up_kernel(step, ids_ref, *refs):
    core, z = ids_ref[0], ids_ref[4]
    first = step == 0
    if first:
        x_ref, *refs = refs
    else:
        own_ref, other_ref, *refs = refs
    tab_ref, *refs = refs
    w_refs, p_refs, xs = refs[:4], refs[4:8], refs[8]
    if not first:
        x_ref = refs[9]
        x_ref[pl.ds(pl.multiple_of(core * 128, 128), 128), :] = own_ref[...]
        x_ref[pl.ds(pl.multiple_of((1 - core) * 128, 128), 128), :] = other_ref[...]
    hot = one_hot(tab_ref, step)
    picked = dot(hot.T[:SLOTS].astype(bf16), x_ref[:, :WIDTH]).astype(bf16)
    for b in range(4):
        xs[b] = picked[:, b * HALF : (b + 1) * HALF]
    if first:
        tail = jnp.zeros((PAY - SLOTS, 384), bf16)
    else:
        squares = jnp.sum(x_ref[:, WIDTH:].astype(f32), axis=1, keepdims=True)
        line = jnp.sum(hot * squares, axis=0, keepdims=True)
        line = jnp.concatenate([line, jnp.zeros((1, 128), f32)], axis=1)
        hi, mid, low = split3(line)
        at = lax.broadcasted_iota(jnp.int32, (PAY - SLOTS, 384), 0)
        tail = jnp.where(
            at == 0,
            hi.astype(f32),
            jnp.where(at == 1, mid.astype(f32), jnp.where(at == 2, low.astype(f32), 0.0)),
        ).astype(bf16)
    ours = [xs[at] for at in block_at(ids_ref)]
    for d in range(4):
        at = pl.multiple_of(((z + d) % 4) * 384, 128)
        part = dot(ours[0], w_refs[0][pl.ds(at, 384), :], NT)
        for b in range(1, 4):
            part = part + dot(ours[b], w_refs[b][pl.ds(at, 384), :], NT)
        p_refs[d][:SLOTS, :] = part.astype(bf16)
        p_refs[d][SLOTS:, :] = tail


def gate_up(step, ids, x, tab, weights):
    scratch = [pltpu.VMEM((4, SLOTS, HALF), bf16)]
    if step > 0:
        scratch.append(pltpu.VMEM((ROWS, EXT), bf16))
    return pl.pallas_call(
        lambda *refs: gate_up_kernel(step, *refs),
        in_specs=[pl.BlockSpec(memory_space=pltpu.SMEM)] + [pl.BlockSpec()] * (len(x) + 5),
        out_shape=[jax.ShapeDtypeStruct((PAY, 384), bf16)] * 4,
        scratch_shapes=scratch,
        compiler_params=pltpu.CompilerParams(vmem_limit_bytes=16 << 20),
        cost_estimate=busy(2.2),
        name="gate_up",
    )(ids, *x, tab, *weights)


def act_kernel(first, *refs):
    out_ref = refs[4]
    total = refs[0][...].astype(f32)
    for j in range(1, 4):
        total = total + refs[j][...].astype(f32)
    sums = total[:SLOTS]
    if not first:
        line = jnp.sum(total[SLOTS : SLOTS + 8, :HALF], axis=0, keepdims=True)
        rs_line = lax.rsqrt(line * (1.0 / D) + norm_eps)
        r0 = lax.broadcasted_iota(jnp.int32, (SLOTS, HALF), 0)
        r1 = lax.broadcasted_iota(jnp.int32, (SLOTS, HALF), 1)
        rs = jnp.sum(jnp.where(r0 == r1, rs_line, 0.0), axis=1, keepdims=True)
        sums = sums * rs
    t0, t1, t2 = sums[:, :128], sums[:, 128:256], sums[:, 256:]
    a0 = jax.nn.silu(t0) * t2
    a1 = jax.nn.silu(t1) * pltpu.roll(t1, 64, 1)
    half = SLOTS // 2
    lane = lax.broadcasted_iota(jnp.int32, (half, 128), 1)
    middle = jnp.where(lane < 64, a1[:half], pltpu.roll(a1[half:], 64, 1))
    out_ref[...] = jnp.concatenate([a0[:half], middle, a0[half:]], axis=1).astype(bf16)


def activate(first, p):
    return pl.pallas_call(
        lambda *refs: act_kernel(first, *refs),
        out_shape=jax.ShapeDtypeStruct((SLOTS // 2, 384), bf16),
        compiler_params=pltpu.CompilerParams(vmem_limit_bytes=8 << 20),
        cost_estimate=busy(0.3),
        name="activate",
    )(*p)


def down_kernel(step, ids_ref, *refs):
    core, z = ids_ref[0], ids_ref[4]
    a_refs, tab_ref, w_refs = refs[:4], refs[4], refs[5:9]
    send_ref, keep_ref, ys = refs[9:]
    half = SLOTS // 2
    lane = lax.broadcasted_iota(jnp.int32, (half, 128), 1)
    sums = [jnp.zeros((SLOTS, HALF), f32)] * 4
    for d in range(4):
        block = a_refs[d][...].astype(f32)
        middle = block[:, 128:256]
        low = jnp.concatenate([block[:, :128], jnp.where(lane < 64, middle, 0.0)], axis=1)
        high = jnp.concatenate([block[:, 256:], jnp.where(lane < 64, 0.0, middle)], axis=1)
        act = jnp.concatenate([low, high], axis=0).astype(bf16)
        for b in range(4):
            start = 2 * UNIT_HALF if b < 2 else 0
            at = pl.multiple_of(((z - d + 4) % 4) * UNITS + start, 64)
            after = pl.multiple_of(((z - d + 4) % 4) * UNITS + start + 128, 64)
            w = jnp.concatenate([w_refs[b][pl.ds(at, UNITS), :], w_refs[b][pl.ds(after, 64), :]], axis=0)
            sums[b] = sums[b] + dot(act, w)
    for b, at in enumerate(block_at(ids_ref)):
        ys[at] = sums[b].astype(bf16)
    slot = lax.broadcasted_iota(jnp.int32, (128, HALF), 1).astype(f32)
    for ref, part in ((send_ref, 1 - core), (keep_ref, core)):
        tab = tab_ref[pl.ds(pl.multiple_of(part * 128, 128), 128), :]
        hot = jnp.where(slot == tab[:, 64 + step : 65 + step], 1.0, 0.0)[:, :SLOTS].astype(bf16)
        for b in range(4):
            rows = dot(hot, ys[b]) * tab[:, step : step + 1]
            ref[:, b * HALF : (b + 1) * HALF] = rows.astype(ref.dtype)


def down(step, ids, acts, tab, weights):
    return pl.pallas_call(
        lambda *refs: down_kernel(step, *refs),
        in_specs=[pl.BlockSpec(memory_space=pltpu.SMEM)] + [pl.BlockSpec()] * 9,
        out_shape=[
            jax.ShapeDtypeStruct((128, WIDTH), bf16),
            jax.ShapeDtypeStruct((128, WIDTH), f32),
        ],
        scratch_shapes=[pltpu.VMEM((4, SLOTS, HALF), bf16)],
        compiler_params=pltpu.CompilerParams(vmem_limit_bytes=16 << 20),
        cost_estimate=busy(1.9),
        name="down",
    )(ids, *acts, tab, *weights)


def pair_kernel(keep_ref, other_ref, out_ref):
    out_ref[...] = (keep_ref[...] + other_ref[...].astype(f32)).astype(bf16)


def pair(keep, other):
    return pl.pallas_call(
        pair_kernel,
        out_shape=jax.ShapeDtypeStruct((128, WIDTH), bf16),
        compiler_params=pltpu.CompilerParams(vmem_limit_bytes=4 << 20),
        name="pair",
    )(keep, other)


def residual_kernel(p_ref, stream_ref, gain_ref, new_ref, x_ref):
    total = p_ref[0].astype(f32)
    for j in range(1, 16):
        total = total + p_ref[j].astype(f32)
    stream = stream_ref[...] + total
    new_ref[...] = stream
    hi, mid, low = split3(jnp.sum(stream * stream, axis=1, keepdims=True))
    lane = lax.broadcasted_iota(jnp.int32, (8, 128), 1)
    parts = jnp.where(
        lane == 0,
        hi.astype(f32),
        jnp.where(lane == 1, mid.astype(f32), jnp.where(lane == 2, low.astype(f32), 0.0)),
    )
    row = jnp.concatenate([stream * gain_ref[...], parts], axis=1).astype(bf16)
    for j in range(16):
        x_ref[j] = row


def residual(p, stream, gain):
    return pl.pallas_call(
        residual_kernel,
        out_shape=[
            jax.ShapeDtypeStruct((8, WIDTH), f32),
            jax.ShapeDtypeStruct((16, 8, EXT), bf16),
        ],
        compiler_params=pltpu.CompilerParams(vmem_limit_bytes=4 << 20),
        name="residual",
    )(p, stream, gain)


def last_kernel(p_ref, stream_ref, new_ref):
    total = p_ref[0].astype(f32)
    for j in range(1, 16):
        total = total + p_ref[j].astype(f32)
    new_ref[...] = stream_ref[...] + total


def last(p, stream):
    return pl.pallas_call(
        last_kernel,
        out_shape=jax.ShapeDtypeStruct((8, WIDTH), f32),
        compiler_params=pltpu.CompilerParams(vmem_limit_bytes=4 << 20),
        name="last",
    )(p, stream)


def place_kernel(ids_ref, whole_ref, out_ref):
    z = ids_ref[4]
    for a in range(4):
        for h in range(2):
            block = whole_ref[((a + z) % 4) * 2 + h]
            for far in range(2):
                to = far * 2048 + a * 512
                out_ref[h * 8 : h * 8 + 8, to : to + 512] = block[:, far * 512 : far * 512 + 512]


def place_rows(ids, whole):
    return pl.pallas_call(
        place_kernel,
        in_specs=[pl.BlockSpec(memory_space=pltpu.SMEM), pl.BlockSpec()],
        out_shape=jax.ShapeDtypeStruct((ROWS_DEV, D), f32),
        compiler_params=pltpu.CompilerParams(vmem_limit_bytes=4 << 20),
        name="place_rows",
    )(ids, whole)


def exchange(x, axes):
    return lax.all_to_all(x, axes, split_axis=0, concat_axis=0, tiled=True)


def reduced(v):
    return lax.reduce_precision(v, exponent_bits=8, mantissa_bits=7)


def parts3(v):
    hi = reduced(v)
    mid = reduced(v - hi)
    return [hi, mid, v - hi - mid]


def swap(x):
    return lax.ppermute(x, "c", [(0, 1), (1, 0)])


def around(x, d):
    return lax.ppermute(x, "z", [(i, (i + d) % 4) for i in range(4)])


def body(trainer_weights, hidden_in, norm_gain, routing, gate_weights):
    core, far, z = lax.axis_index("c"), lax.axis_index("xh"), lax.axis_index("z")
    tp = lax.axis_index(T)
    ids = jnp.stack([core, tp, 2 * tp + core, far, z, far * 8 + tp]).astype(jnp.int32)
    gain = lax.dynamic_index_in_dim(norm_gain.reshape(2, 4, 512), z, 1, keepdims=False)
    gain = gain.reshape(1, WIDTH)

    hidden = hidden_in.astype(f32)
    rs = lax.rsqrt(jnp.mean(hidden * hidden, axis=-1, keepdims=True) + norm_eps)
    flat = lambda v: jnp.transpose(v, (1, 0, 2)).reshape(ROWS_DEV, STEPS * TOPK)
    extra = jnp.concatenate(
        [flat(routing).astype(f32)] + parts3(flat(gate_weights)) + parts3(rs)
        + [jnp.zeros((ROWS_DEV, 125), f32)],
        axis=1,
    ).astype(bf16)
    pieces = jnp.transpose(hidden_in.reshape(ROWS_DEV, 2, 4, 512), (2, 0, 1, 3))
    pieces = pieces.reshape(4, ROWS_DEV, WIDTH)
    extra = jnp.broadcast_to(extra[None], (4, ROWS_DEV, FIRST - WIDTH))
    pieces = jnp.concatenate([pieces, extra], axis=2)
    pieces_far = lax.ppermute(pieces, "xh", [(0, 1), (1, 0)])

    near_out, diag_out = quantize_far(ids, trainer_weights)
    near_out, diag_out, pieces_far = lax.optimization_barrier((near_out, diag_out, pieces_far))
    gu_near = lax.ppermute(near_out, "xh", [(0, 1), (1, 0)])
    gu_diag = lax.ppermute(diag_out, ("xh", "c"), [(0, 3), (3, 0), (1, 2), (2, 1)])
    rows = spread(ids, pieces, pieces_far)
    rows = jnp.stack([rows[0]] + [around(rows[d], d) for d in (1, 2, 3)])
    x, stream, tab = prepare(ids, rows, swap(rows), gain)
    own, other_out, near_out, diag_out = quantize_rest(ids, trainer_weights)
    near_out, diag_out, gu_near, gu_diag, x, stream, tab, other_out = lax.optimization_barrier(
        (near_out, diag_out, gu_near, gu_diag, x, stream, tab, other_out)
    )
    other = swap(other_out)
    down_near = lax.ppermute(near_out, "xh", [(0, 1), (1, 0)])
    down_diag = lax.ppermute(diag_out, ("xh", "c"), [(0, 3), (3, 0), (1, 2), (2, 1)])

    x = [x]
    for step in range(STEPS):
        part = gate_up(step, ids, x, tab, [own, other, gu_near, gu_diag])
        part = [part[0]] + [around(part[d], d) for d in (1, 2, 3)]
        act = activate(step == 0, part)
        acts = [act] + [around(act, d) for d in (1, 2, 3)]
        send, keep = down(step, ids, acts, tab, [own, other, down_near, down_diag])
        sums = exchange(pair(keep, swap(send)).reshape(16, 8, WIDTH), XT)
        if step < STEPS - 1:
            stream, rows = residual(sums, stream, gain)
            rows = exchange(rows, XT).reshape(128, EXT)
            x = [rows, swap(rows)]
        else:
            stream = last(sums, stream)

    turn = [(a * 8 + t, ((t // 2 - a) % 4) * 8 + t) for a in range(4) for t in range(8)]
    mine = lax.ppermute(stream, ("z", "xl", "y"), turn)
    whole = exchange(jnp.broadcast_to(mine[None], (8, 8, WIDTH)), T)
    return place_rows(ids, whole)


def solution(mesh):
    fine = Mesh(mesh.devices.reshape(2, 4, 2, 2, 4), ALL)
    fsdp, tp = ("xh", "z", "c"), ("xl", "y")
    in_specs = (
        P(tp, None, None, fsdp),
        P(fsdp, None),
        P(),
        P(None, fsdp, None),
        P(None, fsdp, None),
    )
    return jax.shard_map(
        body, mesh=fine, in_specs=in_specs, out_specs=P(fsdp, None), check_vma=False
    )
```

time: 334 us -> 270 us (0.81)
  blocking collectives: 268 us -> 103 us
  waiting for transfers between devices: 0.01 us -> 78.2 us
  starting transfers between devices: 1.41 us -> 51.1 us
  local copies, waits for them, and re-layouts: 19.5 us -> 4.37 us
  Pallas kernels: 42.3 us -> 30.3 us
    all_to_all x17 -> x8, blocking collectives: 268 us -> 103 us  [exchange(): return lax.all_to_all(x, axes, split_axis=0, concat_axis=0, tiled=True)]
    ppermute x3 -> x42, waiting for transfers between devices: 0.01 us -> 78.2 us  [the longest x27 53.2 us: around(): return lax.ppermute(x, 'z', [(i, (i + d) % 4) for i in range(4)])]
    ppermute x3 -> x42, starting transfers between devices: 1.41 us -> 51.1 us  [the longest x27 39.8 us: around(): return lax.ppermute(x, 'z', [(i, (i + d) % 4) for i in range(4)])]
    unnamed x52 -> x10, local copies, waits for them, and re-layouts: 10 us -> 1.29 us
    pallas_call x4, Pallas kernels: 9.51 us -> 0.91 us  [activate(): pl.pallas_call(lambda *refs: act_kernel(first, *refs), out_shape=jax.Shap...]
    dynamic_slice x2 -> x1, local copies, waits for them, and re-layouts: 4.63 us -> 0.01 us  [body(): lax.dynamic_index_in_dim(norm_gain.reshape(2, 4, 512), z, 1, keepdims=False)]
    squeeze x2 -> x0, local copies, waits for them, and re-layouts: 3.55 us -> none  [body(): partial = gate_up(first, ids, x, s[step], st[step], gu_a, gu_b)]
    pallas_call x10 -> x16, Pallas kernels: 24.7 us -> 22.5 us  [the longest x4 8.58 us: gate_up(): pl.pallas_call(lambda *refs: gate_up_kernel(step, *refs), in_specs=[pl.Bl...]
  transfers between devices with their start and end apart: 3 -> 42, of which waited for: 0 -> 32; matrix products, arithmetic and copies ran while one was open for 2% -> 0% of each run, Pallas kernels for 2% -> 6%
where the time goes in v2:
time: 270 us; the launch traced here: 269 us
  blocking collectives  103 us (38%)
  waiting for transfers between devices  78.2 us (29%)
  starting transfers between devices  51.1 us (19%)
  Pallas kernels  30.3 us (11%)
  local copies, waits for them, and re-layouts  4.37 us (2%)
    all_to_all x8, blocking collectives, exchange(): return lax.all_to_all(x, axes, split_axis=0, concat_axis=0, tiled=True)  103 us
    ppermute x27, waiting for transfers between devices, around(): return lax.ppermute(x, 'z', [(i, (i + d) % 4) for i in range(4)])  53.2 us
    ppermute x27, starting transfers between devices, around(): return lax.ppermute(x, 'z', [(i, (i + d) % 4) for i in range(4)])  39.8 us
    ppermute x2, waiting for transfers between devices, body(): lax.ppermute(diag_out, ('xh', 'c'), [(0, 3), (3, 0), (1, 2), (2, 1)])  13.9 us
    ppermute x9, waiting for transfers between devices, swap(): return lax.ppermute(x, 'c', [(0, 1), (1, 0)])  10.8 us
    pallas_call x4, Pallas kernels, gate_up(): pl.pallas_call(lambda *refs: gate_up_kernel(step, *refs), in_specs=[pl.Bl...  8.58 us
    pallas_call x1, Pallas kernels, quantize_rest(): pl.pallas_call(quant_rest_kernel, in_specs=[pl.BlockSpec(memory_space=plt...  6.77 us
    pallas_call x4, Pallas kernels, down(): pl.pallas_call(lambda *refs: down_kernel(step, *refs), in_specs=[pl.Block...  5.6 us
  transfers between devices with their start and end apart: 42, of which 32 were waited for; matrix products, arithmetic and copies ran while one was open for 0% of the time, Pallas kernels for 6%

profile of v2, /device:TPU:0, one launch (start us, length us, event | category | flops | bytes accessed | tf_op | source)
XLA Modules:
  0.0 269.2 jit_solution(1691613601340095040)
XLA Ops:
  4.3 3.2 %collective-permute-start = (bf16[4,16,1280]{2,1,0:T(8,128)(2,1)S(1)}, bf16[4,16,1280]{2,1,0:T(8,128)(2,1)S(1)}, u32[]{:S(2)}, u32[]{:S(2)}) collective-permute-start(bf16[4,16,1280]{2,1,0:T(8,128)(2,1)S(1)} %pad_maximum_fusion.1.own_ref), channel_id=1, source_target_pairs={{0,64},{64,0},{1,65},{65,1},{2,66},{66,2},{3,67},{67,3},{4,68},{68... | collective-permute-start | bytes 491528 | tf_op jit(solution)/shard_map/ppermute | solution.py:517
  8.1 4.6 %quantize_far.1 = (bf16[1536,256]{1,0:T(8,128)(2,1)}, bf16[1536,256]{1,0:T(8,128)(2,1)}) custom-call(s32[6]{0:T(128)} %stack.42.ids_ref.refs_0_, bf16[2,3,1536,256]{3,2,1,0:T(8,128)(2,1)} %w_ref.3), custom_call_target="tpu_custom_call" | custom-call | tf_op jit(solution)/shard_map/quantize_far/pallas_call | solution.py:118
  17.8 3.6 %collective-permute-start.4 = (bf16[2,16,1280]{2,1,0:T(8,128)(2,1)S(1)}, bf16[2,16,1280]{2,1,0:T(8,128)(2,1)S(1)}, u32[]{:S(2)}, u32[]{:S(2)}) collective-permute-start(bf16[2,16,1280]{2,1,0:T(8,128)(2,1)S(1)} %get-tuple-element.68), channel_id=1, source_target_pairs={{0,32},{16,48},{32,0},{48,16},{1,33},{17,49},{33,1},{49,17},{2,34}... | collective-permute-start | bytes 245768 | tf_op jit(solution)/shard_map/ppermute | solution.py:495
  22.7 3.4 %collective-permute-done.4 = bf16[2,16,1280]{2,1,0:T(8,128)(2,1)S(1)} collective-permute-done((bf16[2,16,1280]{2,1,0:T(8,128)(2,1)S(1)}, bf16[2,16,1280]{2,1,0:T(8,128)(2,1)S(1)}, u32[]{:S(2)}, u32[]{:S(2)}) %collective-permute-start.4) | collective-permute-done | bytes 81952 | tf_op jit(solution)/shard_map/ppermute | solution.py:495
  26.7 6.8 %quantize_rest.1 = (bf16[2304,256]{1,0:T(8,128)(2,1)}, bf16[2304,256]{1,0:T(8,128)(2,1)}, bf16[768,256]{1,0:T(8,128)(2,1)}, bf16[768,256]{1,0:T(8,128)(2,1)}) custom-call(s32[6]{0:T(128)} %stack.42.ids_ref.refs_0_, bf16[2,3,1536,256]{3,2,1,0:T(8,128)(2,1)} %w_ref.3), custom_call_target="tpu_custom_call" | custom-call | tf_op jit(solution)/shard_map/quantize_rest/pallas_call | solution.py:164
  35.0 13.9 %collective-permute-done.2.refs_6_.refs_7_ = bf16[1536,256]{1,0:T(8,128)(2,1)S(1)} collective-permute-done((bf16[1536,256]{1,0:T(8,128)(2,1)}, bf16[1536,256]{1,0:T(8,128)(2,1)S(1)}, u32[]{:S(2)}, u32[]{:S(2)}) %collective-permute-start.2) | collective-permute-done | bytes 786464 | tf_op jit(solution)/shard_map/ppermute | solution.py:522
  58.5 3.6 %collective-permute-start.9 = (bf16[192,384]{1,0:T(8,128)(2,1)S(1)}, bf16[192,384]{1,0:T(8,128)(2,1)S(1)}, u32[]{:S(2)}, u32[]{:S(2)}) collective-permute-start(bf16[192,384]{1,0:T(8,128)(2,1)S(1)} %get-tuple-element.82), channel_id=1, source_target_pairs={{0,32},{16,48},{32,0},{48,16},{1,33},{17,49},{33,1},{49,17},{2,34}... | collective-permute-start | bytes 442376 | tf_op jit(solution)/shard_map/ppermute | solution.py:495
  65.2 4.5 %collective-permute-done.9.refs_2_ = bf16[192,384]{1,0:T(8,128)(2,1)S(1)} collective-permute-done((bf16[192,384]{1,0:T(8,128)(2,1)S(1)}, bf16[192,384]{1,0:T(8,128)(2,1)S(1)}, u32[]{:S(2)}, u32[]{:S(2)}) %collective-permute-start.9) | collective-permute-done | bytes 147488 | tf_op jit(solution)/shard_map/ppermute | solution.py:495
  75.4 3.0 %collective-permute-done.12.refs_3_ = bf16[88,384]{1,0:T(8,128)(2,1)S(1)} collective-permute-done((bf16[88,384]{1,0:T(8,128)(2,1)S(1)}, bf16[88,384]{1,0:T(8,128)(2,1)S(1)}, u32[]{:S(2)}, u32[]{:S(2)}) %collective-permute-start.12) | collective-permute-done | bytes 67616 | tf_op jit(solution)/shard_map/ppermute | solution.py:495
  82.2 14.1 %all_to_all.40.p_ref = bf16[16,8,1024]{2,1,0:T(8,128)(2,1)S(1)} all-to-all(bf16[16,8,1024]{2,1,0:T(8,128)(2,1)S(1)} %bitcast.35), channel_id=1, replica_groups=mesh['xh'=2,'z'=4,'c'=2,'xl'=2,'y'=4] {'xh','xl','y'}, dimensions={0} | all-to-all | bytes 524288 | tf_op jit(solution)/shard_map/all_to_all | solution.py:477
  96.4 12.1 %all_to_all.41 = bf16[16,8,1152]{2,1,0:T(8,128)(2,1)S(1)} all-to-all(bf16[16,8,1152]{2,1,0:T(8,128)(2,1)S(1)} %get-tuple-element.89), channel_id=1, replica_groups=mesh['xh'=2,'z'=4,'c'=2,'xl'=2,'y'=4] {'xh','xl','y'}, dimensions={0} | all-to-all | bytes 589824 | tf_op jit(solution)/shard_map/all_to_all | solution.py:477
  116.0 6.6 %collective-permute-done.18.refs_1_ = bf16[192,384]{1,0:T(8,128)(2,1)S(1)} collective-permute-done((bf16[192,384]{1,0:T(8,128)(2,1)S(1)}, bf16[192,384]{1,0:T(8,128)(2,1)S(1)}, u32[]{:S(2)}, u32[]{:S(2)}) %collective-permute-start.18) | collective-permute-done | bytes 147488 | tf_op jit(solution)/shard_map/ppermute | solution.py:495
  129.0 3.0 %collective-permute-done.22.refs_3_ = bf16[88,384]{1,0:T(8,128)(2,1)S(1)} collective-permute-done((bf16[88,384]{1,0:T(8,128)(2,1)S(1)}, bf16[88,384]{1,0:T(8,128)(2,1)S(1)}, u32[]{:S(2)}, u32[]{:S(2)}) %collective-permute-start.22) | collective-permute-done | bytes 67616 | tf_op jit(solution)/shard_map/ppermute | solution.py:495
  135.4 12.2 %all_to_all.42.p_ref = bf16[16,8,1024]{2,1,0:T(8,128)(2,1)S(1)} all-to-all(bf16[16,8,1024]{2,1,0:T(8,128)(2,1)S(1)} %bitcast.36), channel_id=1, replica_groups=mesh['xh'=2,'z'=4,'c'=2,'xl'=2,'y'=4] {'xh','xl','y'}, dimensions={0} | all-to-all | bytes 524288 | tf_op jit(solution)/shard_map/all_to_all | solution.py:477
  147.8 12.1 %all_to_all.43 = bf16[16,8,1152]{2,1,0:T(8,128)(2,1)S(1)} all-to-all(bf16[16,8,1152]{2,1,0:T(8,128)(2,1)S(1)} %get-tuple-element.97), channel_id=1, replica_groups=mesh['xh'=2,'z'=4,'c'=2,'xl'=2,'y'=4] {'xh','xl','y'}, dimensions={0} | all-to-all | bytes 589824 | tf_op jit(solution)/shard_map/all_to_all | solution.py:477
  167.9 6.1 %collective-permute-done.26.refs_1_ = bf16[192,384]{1,0:T(8,128)(2,1)S(1)} collective-permute-done((bf16[192,384]{1,0:T(8,128)(2,1)S(1)}, bf16[192,384]{1,0:T(8,128)(2,1)S(1)}, u32[]{:S(2)}, u32[]{:S(2)}) %collective-permute-start.26) | collective-permute-done | bytes 147488 | tf_op jit(solution)/shard_map/ppermute | solution.py:495
  174.8 2.7 %collective-permute-start.31 = (bf16[88,384]{1,0:T(8,128)(2,1)S(1)}, bf16[88,384]{1,0:T(8,128)(2,1)S(1)}, u32[]{:S(2)}, u32[]{:S(2)}) collective-permute-start(bf16[88,384]{1,0:T(8,128)(2,1)S(1)} %activate.6.refs_1_), channel_id=1, source_target_pairs={{0,48},{16,0},{32,16},{48,32},{1,49},{17,1},{33,17},{49,33},{2,50}... | collective-permute-start | bytes 202760 | tf_op jit(solution)/shard_map/ppermute | solution.py:495
  180.6 3.0 %collective-permute-done.30.refs_3_ = bf16[88,384]{1,0:T(8,128)(2,1)S(1)} collective-permute-done((bf16[88,384]{1,0:T(8,128)(2,1)S(1)}, bf16[88,384]{1,0:T(8,128)(2,1)S(1)}, u32[]{:S(2)}, u32[]{:S(2)}) %collective-permute-start.30) | collective-permute-done | bytes 67616 | tf_op jit(solution)/shard_map/ppermute | solution.py:495
  187.4 12.3 %all_to_all.44.p_ref = bf16[16,8,1024]{2,1,0:T(8,128)(2,1)S(1)} all-to-all(bf16[16,8,1024]{2,1,0:T(8,128)(2,1)S(1)} %bitcast.37), channel_id=1, replica_groups=mesh['xh'=2,'z'=4,'c'=2,'xl'=2,'y'=4] {'xh','xl','y'}, dimensions={0} | all-to-all | bytes 524288 | tf_op jit(solution)/shard_map/all_to_all | solution.py:477
  199.8 12.1 %all_to_all.45 = bf16[16,8,1152]{2,1,0:T(8,128)(2,1)S(1)} all-to-all(bf16[16,8,1152]{2,1,0:T(8,128)(2,1)S(1)} %get-tuple-element.105), channel_id=1, replica_groups=mesh['xh'=2,'z'=4,'c'=2,'xl'=2,'y'=4] {'xh','xl','y'}, dimensions={0} | all-to-all | bytes 589824 | tf_op jit(solution)/shard_map/all_to_all | solution.py:477
  219.6 6.3 %collective-permute-done.34.refs_1_ = bf16[192,384]{1,0:T(8,128)(2,1)S(1)} collective-permute-done((bf16[192,384]{1,0:T(8,128)(2,1)S(1)}, bf16[192,384]{1,0:T(8,128)(2,1)S(1)}, u32[]{:S(2)}, u32[]{:S(2)}) %collective-permute-start.34) | collective-permute-done | bytes 147488 | tf_op jit(solution)/shard_map/ppermute | solution.py:495
  232.6 3.0 %collective-permute-done.38.refs_3_ = bf16[88,384]{1,0:T(8,128)(2,1)S(1)} collective-permute-done((bf16[88,384]{1,0:T(8,128)(2,1)S(1)}, bf16[88,384]{1,0:T(8,128)(2,1)S(1)}, u32[]{:S(2)}, u32[]{:S(2)}) %collective-permute-start.38) | collective-permute-done | bytes 67616 | tf_op jit(solution)/shard_map/ppermute | solution.py:495
  239.0 12.2 %all_to_all.46.p_ref = bf16[16,8,1024]{2,1,0:T(8,128)(2,1)S(1)} all-to-all(bf16[16,8,1024]{2,1,0:T(8,128)(2,1)S(1)} %bitcast.38), channel_id=1, replica_groups=mesh['xh'=2,'z'=4,'c'=2,'xl'=2,'y'=4] {'xh','xl','y'}, dimensions={0} | all-to-all | bytes 524288 | tf_op jit(solution)/shard_map/all_to_all | solution.py:477
  252.0 15.9 %all_to_all.47.whole_ref = f32[8,8,1024]{2,1,0:T(8,128)S(1)} all-to-all(f32[8,8,1024]{2,1,0:T(8,128)S(1)} %broadcast_in_dim.8), channel_id=1, replica_groups=mesh['xh'=2,'z'=4,'c'=2,'xl'=2,'y'=4] {'xl','y'}, dimensions={0} | all-to-all | bytes 524288 | tf_op jit(solution)/shard_map/all_to_all | solution.py:477
  (124 shorter events, 88.4 us)
Async XLA Ops:
  4.3 8.4 %collective-permute-start = (bf16[4,16,1280]{2,1,0:T(8,128)(2,1)S(1)}, bf16[4,16,1280]{2,1,0:T(8,128)(2,1)S(1)}, u32[]{:S(2)}, u32[]{:S(2)}) collective-permute-start(bf16[4,16,1280]{2,1,0:T(8,128)(2,1)S(1)} %pad_maximum_fusion.1.own_ref), channel_id=1, source_target_pairs={{0,64},{64,0},{1,65},{65,1},{2,66},{66,2},{3,67},{67,3},{4,68},{68... | collective-permute-start | bytes 491528 | tf_op jit(solution)/shard_map/ppermute | solution.py:517
  12.7 22.3 %collective-permute-start.1 = (bf16[1536,256]{1,0:T(8,128)(2,1)}, bf16[1536,256]{1,0:T(8,128)(2,1)S(1)}, u32[]{:S(2)}, u32[]{:S(2)}) collective-permute-start(bf16[1536,256]{1,0:T(8,128)(2,1)} %get-tuple-element.63), channel_id=1, source_target_pairs={{0,64},{64,0},{1,65},{65,1},{2,66},{66,2},{3,67},{67,3},{4,68},{68... | collective-permute-start | bytes 2359304 | tf_op jit(solution)/shard_map/ppermute | solution.py:521
  14.9 34.0 %collective-permute-start.2 = (bf16[1536,256]{1,0:T(8,128)(2,1)}, bf16[1536,256]{1,0:T(8,128)(2,1)S(1)}, u32[]{:S(2)}, u32[]{:S(2)}) collective-permute-start(bf16[1536,256]{1,0:T(8,128)(2,1)} %get-tuple-element.64), channel_id=1, source_target_pairs={{0,72},{72,0},{8,64},{64,8},{1,73},{73,1},{9,65},{65,9},{2,74},{74... | collective-permute-start | bytes 2359304 | tf_op jit(solution)/shard_map/ppermute | solution.py:522
  15.8 6.9 %collective-permute-start.3 = (bf16[2,16,1280]{2,1,0:T(8,128)(2,1)S(1)}, bf16[2,16,1280]{2,1,0:T(8,128)(2,1)S(1)}, u32[]{:S(2)}, u32[]{:S(2)}) collective-permute-start(bf16[2,16,1280]{2,1,0:T(8,128)(2,1)S(1)} %get-tuple-element.67), channel_id=1, source_target_pairs={{0,16},{16,32},{32,48},{48,0},{1,17},{17,33},{33,49},{49,1},{2,18}... | collective-permute-start | bytes 245768 | tf_op jit(solution)/shard_map/ppermute | solution.py:495
  17.8 8.4 %collective-permute-start.4 = (bf16[2,16,1280]{2,1,0:T(8,128)(2,1)S(1)}, bf16[2,16,1280]{2,1,0:T(8,128)(2,1)S(1)}, u32[]{:S(2)}, u32[]{:S(2)}) collective-permute-start(bf16[2,16,1280]{2,1,0:T(8,128)(2,1)S(1)} %get-tuple-element.68), channel_id=1, source_target_pairs={{0,32},{16,48},{32,0},{48,16},{1,33},{17,49},{33,1},{49,17},{2,34}... | collective-permute-start | bytes 245768 | tf_op jit(solution)/shard_map/ppermute | solution.py:495
  26.4 7.0 %collective-permute-start.6 = (bf16[4,2,16,1280]{3,2,1,0:T(8,128)(2,1)S(1)}, bf16[4,2,16,1280]{3,2,1,0:T(8,128)(2,1)S(1)}, u32[]{:S(2)}, u32[]{:S(2)}) collective-permute-start(bf16[4,2,16,1280]{3,2,1,0:T(8,128)(2,1)S(1)} %pad_maximum_fusion.own_ref), channel_id=1, source_target_pairs={{0,8},{8,0},{1,9},{9,1},{2,10},{10,2},{3,11},{11,3},{4,12},{12,4},... | collective-permute-start | bytes 983048 | tf_op jit(solution)/shard_map/ppermute | solution.py:491
  50.2 23.6 %collective-permute-start.14 = (bf16[768,256]{1,0:T(8,128)(2,1)}, bf16[768,256]{1,0:T(8,128)(2,1)S(1)}, u32[]{:S(2)}, u32[]{:S(2)}) collective-permute-start(bf16[768,256]{1,0:T(8,128)(2,1)} %get-tuple-element.84), channel_id=1, source_target_pairs={{0,64},{64,0},{1,65},{65,1},{2,66},{66,2},{3,67},{67,3},{4,68},{68... | collective-permute-start | bytes 1179656 | tf_op jit(solution)/shard_map/ppermute | solution.py:531
  51.7 22.1 %collective-permute-start.15 = (bf16[768,256]{1,0:T(8,128)(2,1)}, bf16[768,256]{1,0:T(8,128)(2,1)S(1)}, u32[]{:S(2)}, u32[]{:S(2)}) collective-permute-start(bf16[768,256]{1,0:T(8,128)(2,1)} %get-tuple-element.85), channel_id=1, source_target_pairs={{0,72},{72,0},{8,64},{64,8},{1,73},{73,1},{9,65},{65,9},{2,74},{74... | collective-permute-start | bytes 1179656 | tf_op jit(solution)/shard_map/ppermute | solution.py:532
  56.5 8.7 %collective-permute-start.8 = (bf16[192,384]{1,0:T(8,128)(2,1)S(1)}, bf16[192,384]{1,0:T(8,128)(2,1)S(1)}, u32[]{:S(2)}, u32[]{:S(2)}) collective-permute-start(bf16[192,384]{1,0:T(8,128)(2,1)S(1)} %get-tuple-element.81), channel_id=1, source_target_pairs={{0,16},{16,32},{32,48},{48,0},{1,17},{17,33},{33,49},{49,1},{2,18}... | collective-permute-start | bytes 442376 | tf_op jit(solution)/shard_map/ppermute | solution.py:495
  58.5 11.3 %collective-permute-start.9 = (bf16[192,384]{1,0:T(8,128)(2,1)S(1)}, bf16[192,384]{1,0:T(8,128)(2,1)S(1)}, u32[]{:S(2)}, u32[]{:S(2)}) collective-permute-start(bf16[192,384]{1,0:T(8,128)(2,1)S(1)} %get-tuple-element.82), channel_id=1, source_target_pairs={{0,32},{16,48},{32,0},{48,16},{1,33},{17,49},{33,1},{49,17},{2,34}... | collective-permute-start | bytes 442376 | tf_op jit(solution)/shard_map/ppermute | solution.py:495
  62.1 7.7 %collective-permute-start.10 = (bf16[192,384]{1,0:T(8,128)(2,1)S(1)}, bf16[192,384]{1,0:T(8,128)(2,1)S(1)}, u32[]{:S(2)}, u32[]{:S(2)}) collective-permute-start(bf16[192,384]{1,0:T(8,128)(2,1)S(1)} %get-tuple-element.83), channel_id=1, source_target_pairs={{0,48},{16,0},{32,16},{48,32},{1,49},{17,1},{33,17},{49,33},{2,50}... | collective-permute-start | bytes 442376 | tf_op jit(solution)/shard_map/ppermute | solution.py:495
  112.3 10.3 %collective-permute-start.18 = (bf16[192,384]{1,0:T(8,128)(2,1)S(1)}, bf16[192,384]{1,0:T(8,128)(2,1)S(1)}, u32[]{:S(2)}, u32[]{:S(2)}) collective-permute-start(bf16[192,384]{1,0:T(8,128)(2,1)S(1)} %get-tuple-element.91), channel_id=1, source_target_pairs={{0,16},{16,32},{32,48},{48,0},{1,17},{17,33},{33,49},{49,1},{2,18}... | collective-permute-start | bytes 442376 | tf_op jit(solution)/shard_map/ppermute | solution.py:495
  112.3 10.3 %collective-permute-start.19 = (bf16[192,384]{1,0:T(8,128)(2,1)S(1)}, bf16[192,384]{1,0:T(8,128)(2,1)S(1)}, u32[]{:S(2)}, u32[]{:S(2)}) collective-permute-start(bf16[192,384]{1,0:T(8,128)(2,1)S(1)} %get-tuple-element.92), channel_id=1, source_target_pairs={{0,32},{16,48},{32,0},{48,16},{1,33},{17,49},{33,1},{49,17},{2,34}... | collective-permute-start | bytes 442376 | tf_op jit(solution)/shard_map/ppermute | solution.py:495
  114.4 8.9 %collective-permute-start.20 = (bf16[192,384]{1,0:T(8,128)(2,1)S(1)}, bf16[192,384]{1,0:T(8,128)(2,1)S(1)}, u32[]{:S(2)}, u32[]{:S(2)}) collective-permute-start(bf16[192,384]{1,0:T(8,128)(2,1)S(1)} %get-tuple-element.93), channel_id=1, source_target_pairs={{0,48},{16,0},{32,16},{48,32},{1,49},{17,1},{33,17},{49,33},{2,50}... | collective-permute-start | bytes 442376 | tf_op jit(solution)/shard_map/ppermute | solution.py:495
  126.0 6.3 %collective-permute-start.21 = (bf16[88,384]{1,0:T(8,128)(2,1)S(1)}, bf16[88,384]{1,0:T(8,128)(2,1)S(1)}, u32[]{:S(2)}, u32[]{:S(2)}) collective-permute-start(bf16[88,384]{1,0:T(8,128)(2,1)S(1)} %activate.5.refs_1_), channel_id=1, source_target_pairs={{0,16},{16,32},{32,48},{48,0},{1,17},{17,33},{33,49},{49,1},{2,18}... | collective-permute-start | bytes 202760 | tf_op jit(solution)/shard_map/ppermute | solution.py:495
  163.6 10.3 %collective-permute-start.26 = (bf16[192,384]{1,0:T(8,128)(2,1)S(1)}, bf16[192,384]{1,0:T(8,128)(2,1)S(1)}, u32[]{:S(2)}, u32[]{:S(2)}) collective-permute-start(bf16[192,384]{1,0:T(8,128)(2,1)S(1)} %get-tuple-element.99), channel_id=1, source_target_pairs={{0,16},{16,32},{32,48},{48,0},{1,17},{17,33},{33,49},{49,1},{2,18}... | collective-permute-start | bytes 442376 | tf_op jit(solution)/shard_map/ppermute | solution.py:495
  163.7 10.3 %collective-permute-start.27 = (bf16[192,384]{1,0:T(8,128)(2,1)S(1)}, bf16[192,384]{1,0:T(8,128)(2,1)S(1)}, u32[]{:S(2)}, u32[]{:S(2)}) collective-permute-start(bf16[192,384]{1,0:T(8,128)(2,1)S(1)} %get-tuple-element.100), channel_id=1, source_target_pairs={{0,32},{16,48},{32,0},{48,16},{1,33},{17,49},{33,1},{49,17},{2,34}... | collective-permute-start | bytes 442376 | tf_op jit(solution)/shard_map/ppermute | solution.py:495
  166.0 8.6 %collective-permute-start.28 = (bf16[192,384]{1,0:T(8,128)(2,1)S(1)}, bf16[192,384]{1,0:T(8,128)(2,1)S(1)}, u32[]{:S(2)}, u32[]{:S(2)}) collective-permute-start(bf16[192,384]{1,0:T(8,128)(2,1)S(1)} %get-tuple-element.101), channel_id=1, source_target_pairs={{0,48},{16,0},{32,16},{48,32},{1,49},{17,1},{33,17},{49,33},{2,50}... | collective-permute-start | bytes 442376 | tf_op jit(solution)/shard_map/ppermute | solution.py:495
  177.5 6.1 %collective-permute-start.30 = (bf16[88,384]{1,0:T(8,128)(2,1)S(1)}, bf16[88,384]{1,0:T(8,128)(2,1)S(1)}, u32[]{:S(2)}, u32[]{:S(2)}) collective-permute-start(bf16[88,384]{1,0:T(8,128)(2,1)S(1)} %activate.6.refs_1_), channel_id=1, source_target_pairs={{0,32},{16,48},{32,0},{48,16},{1,33},{17,49},{33,1},{49,17},{2,34}... | collective-permute-start | bytes 202760 | tf_op jit(solution)/shard_map/ppermute | solution.py:495
  177.8 6.2 %collective-permute-start.29 = (bf16[88,384]{1,0:T(8,128)(2,1)S(1)}, bf16[88,384]{1,0:T(8,128)(2,1)S(1)}, u32[]{:S(2)}, u32[]{:S(2)}) collective-permute-start(bf16[88,384]{1,0:T(8,128)(2,1)S(1)} %activate.6.refs_1_), channel_id=1, source_target_pairs={{0,16},{16,32},{32,48},{48,0},{1,17},{17,33},{33,49},{49,1},{2,18}... | collective-permute-start | bytes 202760 | tf_op jit(solution)/shard_map/ppermute | solution.py:495
  215.6 10.3 %collective-permute-start.34 = (bf16[192,384]{1,0:T(8,128)(2,1)S(1)}, bf16[192,384]{1,0:T(8,128)(2,1)S(1)}, u32[]{:S(2)}, u32[]{:S(2)}) collective-permute-start(bf16[192,384]{1,0:T(8,128)(2,1)S(1)} %get-tuple-element.107), channel_id=1, source_target_pairs={{0,16},{16,32},{32,48},{48,0},{1,17},{17,33},{33,49},{49,1},{2,18}... | collective-permute-start | bytes 442376 | tf_op jit(solution)/shard_map/ppermute | solution.py:495
  215.7 10.3 %collective-permute-start.35 = (bf16[192,384]{1,0:T(8,128)(2,1)S(1)}, bf16[192,384]{1,0:T(8,128)(2,1)S(1)}, u32[]{:S(2)}, u32[]{:S(2)}) collective-permute-start(bf16[192,384]{1,0:T(8,128)(2,1)S(1)} %get-tuple-element.108), channel_id=1, source_target_pairs={{0,32},{16,48},{32,0},{48,16},{1,33},{17,49},{33,1},{49,17},{2,34}... | collective-permute-start | bytes 442376 | tf_op jit(solution)/shard_map/ppermute | solution.py:495
  217.9 8.7 %collective-permute-start.36 = (bf16[192,384]{1,0:T(8,128)(2,1)S(1)}, bf16[192,384]{1,0:T(8,128)(2,1)S(1)}, u32[]{:S(2)}, u32[]{:S(2)}) collective-permute-start(bf16[192,384]{1,0:T(8,128)(2,1)S(1)} %get-tuple-element.109), channel_id=1, source_target_pairs={{0,48},{16,0},{32,16},{48,32},{1,49},{17,1},{33,17},{49,33},{2,50}... | collective-permute-start | bytes 442376 | tf_op jit(solution)/shard_map/ppermute | solution.py:495
  229.6 6.4 %collective-permute-start.37 = (bf16[88,384]{1,0:T(8,128)(2,1)S(1)}, bf16[88,384]{1,0:T(8,128)(2,1)S(1)}, u32[]{:S(2)}, u32[]{:S(2)}) collective-permute-start(bf16[88,384]{1,0:T(8,128)(2,1)S(1)} %activate.7.refs_1_), channel_id=1, source_target_pairs={{0,16},{16,32},{32,48},{48,0},{1,17},{17,33},{33,49},{49,1},{2,18}... | collective-permute-start | bytes 202760 | tf_op jit(solution)/shard_map/ppermute | solution.py:495
  (23 other events, 112.1 us)

commit v3 on v2

--- a/solution.py
+++ b/solution.py
@@ -19,7 +19,7 @@
 WIDTH = 1024
 HALF = 256
 UNITS = 192
-PAY = 192
+PAY = 184
 EXT = 1152
 FIRST = 1280
 
@@ -63,8 +63,9 @@
 
 
 def quant_block(tile):
+    top = jnp.max(jnp.abs(tile), axis=0, keepdims=True).astype(f32)
+    top = jnp.max(top, axis=1, keepdims=True) + scale_eps
     tile = tile.astype(f32)
-    top = jnp.max(jnp.abs(tile), axis=(0, 1), keepdims=True) + scale_eps
     scale = top / code_limit
     return (float_code(tile * (1.0 / scale)) * scale).astype(bf16)
 
@@ -177,6 +178,53 @@
         compiler_params=pltpu.CompilerParams(vmem_limit_bytes=60 << 20),
         name="quantize_rest",
     )(ids, w)
+
+
+def first_kernel(*refs):
+    sources, (out_ref, table), held, sem = refs[:3], refs[3:5], refs[5:8], refs[8]
+    copies = [pltpu.make_async_copy(a, b, sem.at[i]) for i, (a, b) in enumerate(zip(sources, held))]
+    for copy in copies:
+        copy.start()
+    for copy in copies:
+        copy.wait()
+    hidden_ref, routing_ref, gates_ref = held
+    hidden = hidden_ref[...].astype(f32)
+    mean = jnp.sum(hidden * hidden, axis=1, keepdims=True) * (1.0 / D)
+    hi, mid, low = split3(lax.rsqrt(mean + norm_eps))
+    lane = lax.broadcasted_iota(jnp.int32, (ROWS_DEV, 128), 1)
+    rs = jnp.where(
+        lane == 0,
+        hi.astype(f32),
+        jnp.where(lane == 1, mid.astype(f32), jnp.where(lane == 2, low.astype(f32), 0.0)),
+    ).astype(bf16)
+    table[...] = jnp.zeros((128, 128), f32)
+    table[0:32, :ROWS_DEV] = routing_ref[...].astype(f32)
+    for i, part in enumerate(split3(gates_ref[...])):
+        table[32 + 32 * i : 64 + 32 * i, :ROWS_DEV] = part.astype(f32)
+    named = table[...].T[:ROWS_DEV].astype(bf16)
+    for z in range(4):
+        for half in range(2):
+            at = half * 2048 + z * 512
+            out_ref[z, :, half * 512 : half * 512 + 512] = hidden_ref[:, at : at + 512]
+        out_ref[z, :, WIDTH : WIDTH + 128] = named
+        out_ref[z, :, WIDTH + 128 :] = rs
+
+
+def first_rows(hidden, routing, gates):
+    return pl.pallas_call(
+        first_kernel,
+        in_specs=[pl.BlockSpec(memory_space=pltpu.HBM)] * 3,
+        out_shape=jax.ShapeDtypeStruct((4, ROWS_DEV, FIRST), bf16),
+        scratch_shapes=[
+            pltpu.VMEM((128, 128), f32),
+            pltpu.VMEM((ROWS_DEV, D), bf16),
+            pltpu.VMEM((STEPS * TOPK, ROWS_DEV), jnp.int32),
+            pltpu.VMEM((STEPS * TOPK, ROWS_DEV), f32),
+            pltpu.SemaphoreType.DMA((3,)),
+        ],
+        compiler_params=pltpu.CompilerParams(vmem_limit_bytes=60 << 20),
+        name="first_rows",
+    )(hidden, routing, gates)
 
 
 def spread_kernel(ids_ref, own_ref, far_ref, *out_refs):
@@ -437,54 +485,47 @@
     )(p, stream, gain)
 
 
-def last_kernel(p_ref, stream_ref, new_ref):
+def last_kernel(p_ref, stream_ref, before_ref, change_ref):
     total = p_ref[0].astype(f32)
     for j in range(1, 16):
         total = total + p_ref[j].astype(f32)
-    new_ref[...] = stream_ref[...] + total
-
-
-def last(p, stream):
+    change_ref[...] = (stream_ref[...] - before_ref[...] + total).astype(bf16)
+
+
+def last(p, stream, before):
     return pl.pallas_call(
         last_kernel,
-        out_shape=jax.ShapeDtypeStruct((8, WIDTH), f32),
+        out_shape=jax.ShapeDtypeStruct((8, WIDTH), bf16),
         compiler_params=pltpu.CompilerParams(vmem_limit_bytes=4 << 20),
         name="last",
-    )(p, stream)
-
-
-def place_kernel(ids_ref, whole_ref, out_ref):
+    )(p, stream, before)
+
+
+def place_kernel(ids_ref, whole_ref, hidden_ref, out_ref):
     z = ids_ref[4]
     for a in range(4):
         for h in range(2):
-            block = whole_ref[((a + z) % 4) * 2 + h]
+            block = whole_ref[((a + z) % 4) * 2 + h].astype(f32)
             for far in range(2):
                 to = far * 2048 + a * 512
-                out_ref[h * 8 : h * 8 + 8, to : to + 512] = block[:, far * 512 : far * 512 + 512]
-
-
-def place_rows(ids, whole):
+                rows = hidden_ref[:, to : to + 512].astype(f32)[h * 8 : h * 8 + 8]
+                out_ref[h * 8 : h * 8 + 8, to : to + 512] = (
+                    rows + block[:, far * 512 : far * 512 + 512]
+                )
+
+
+def place_rows(ids, whole, hidden):
     return pl.pallas_call(
         place_kernel,
-        in_specs=[pl.BlockSpec(memory_space=pltpu.SMEM), pl.BlockSpec()],
+        in_specs=[pl.BlockSpec(memory_space=pltpu.SMEM), pl.BlockSpec(), pl.BlockSpec()],
         out_shape=jax.ShapeDtypeStruct((ROWS_DEV, D), f32),
         compiler_params=pltpu.CompilerParams(vmem_limit_bytes=4 << 20),
         name="place_rows",
-    )(ids, whole)
+    )(ids, whole, hidden)
 
 
 def exchange(x, axes):
     return lax.all_to_all(x, axes, split_axis=0, concat_axis=0, tiled=True)
-
-
-def reduced(v):
-    return lax.reduce_precision(v, exponent_bits=8, mantissa_bits=7)
-
-
-def parts3(v):
-    hi = reduced(v)
-    mid = reduced(v - hi)
-    return [hi, mid, v - hi - mid]
 
 
 def swap(x):
@@ -502,18 +543,8 @@
     gain = lax.dynamic_index_in_dim(norm_gain.reshape(2, 4, 512), z, 1, keepdims=False)
     gain = gain.reshape(1, WIDTH)
 
-    hidden = hidden_in.astype(f32)
-    rs = lax.rsqrt(jnp.mean(hidden * hidden, axis=-1, keepdims=True) + norm_eps)
-    flat = lambda v: jnp.transpose(v, (1, 0, 2)).reshape(ROWS_DEV, STEPS * TOPK)
-    extra = jnp.concatenate(
-        [flat(routing).astype(f32)] + parts3(flat(gate_weights)) + parts3(rs)
-        + [jnp.zeros((ROWS_DEV, 125), f32)],
-        axis=1,
-    ).astype(bf16)
-    pieces = jnp.transpose(hidden_in.reshape(ROWS_DEV, 2, 4, 512), (2, 0, 1, 3))
-    pieces = pieces.reshape(4, ROWS_DEV, WIDTH)
-    extra = jnp.broadcast_to(extra[None], (4, ROWS_DEV, FIRST - WIDTH))
-    pieces = jnp.concatenate([pieces, extra], axis=2)
+    lines = lambda v: jnp.transpose(v, (0, 2, 1)).reshape(STEPS * TOPK, ROWS_DEV)
+    pieces = first_rows(hidden_in, lines(routing), lines(gate_weights))
     pieces_far = lax.ppermute(pieces, "xh", [(0, 1), (1, 0)])
 
     near_out, diag_out = quantize_far(ids, trainer_weights)
@@ -531,7 +562,7 @@
     down_near = lax.ppermute(near_out, "xh", [(0, 1), (1, 0)])
     down_diag = lax.ppermute(diag_out, ("xh", "c"), [(0, 3), (3, 0), (1, 2), (2, 1)])
 
-    x = [x]
+    x, before = [x], stream
     for step in range(STEPS):
         part = gate_up(step, ids, x, tab, [own, other, gu_near, gu_diag])
         part = [part[0]] + [around(part[d], d) for d in (1, 2, 3)]
@@ -544,12 +575,12 @@
             rows = exchange(rows, XT).reshape(128, EXT)
             x = [rows, swap(rows)]
         else:
-            stream = last(sums, stream)
+            change = last(sums, stream, before)
 
     turn = [(a * 8 + t, ((t // 2 - a) % 4) * 8 + t) for a in range(4) for t in range(8)]
-    mine = lax.ppermute(stream, ("z", "xl", "y"), turn)
+    mine = lax.ppermute(change, ("z", "xl", "y"), turn)
     whole = exchange(jnp.broadcast_to(mine[None], (8, 8, WIDTH)), T)
-    return place_rows(ids, whole)
+    return place_rows(ids, whole, hidden_in)
 
 
 def solution(mesh):

time: 270 us -> 265 us (0.981)
  no operation moved by 1% of the time
where the time goes in v3:
time: 265 us
  blocking collectives  103 us (39%)
  waiting for transfers between devices  77.2 us (29%)
  starting transfers between devices  50.9 us (19%)
  Pallas kernels  31.6 us (12%)
    all_to_all x8, blocking collectives, exchange(): return lax.all_to_all(x, axes, split_axis=0, concat_axis=0, tiled=True)  103 us
    ppermute x27, waiting for transfers between devices, around(): return lax.ppermute(x, 'z', [(i, (i + d) % 4) for i in range(4)])  52 us
    ppermute x27, starting transfers between devices, around(): return lax.ppermute(x, 'z', [(i, (i + d) % 4) for i in range(4)])  39.7 us
    ppermute x2, waiting for transfers between devices, body(): lax.ppermute(diag_out, ('xh', 'c'), [(0, 3), (3, 0), (1, 2), (2, 1)])  13.9 us
    ppermute x9, waiting for transfers between devices, swap(): return lax.ppermute(x, 'c', [(0, 1), (1, 0)])  10.8 us
    pallas_call x4, Pallas kernels, gate_up(): pl.pallas_call(lambda *refs: gate_up_kernel(step, *refs), in_specs=[pl.Bl...  8.6 us
    pallas_call x1, Pallas kernels, quantize_rest(): pl.pallas_call(quant_rest_kernel, in_specs=[pl.BlockSpec(memory_space=plt...  6.48 us
    pallas_call x4, Pallas kernels, down(): pl.pallas_call(lambda *refs: down_kernel(step, *refs), in_specs=[pl.Block...  5.61 us
  transfers between devices with their start and end apart: 42, of which 32 were waited for; matrix products, arithmetic and copies ran while one was open for 0% of the time, Pallas kernels for 6%

profile of v3, /device:TPU:0, one launch (start us, length us, event | category | flops | bytes accessed | tf_op | source)
XLA Modules:
  0.0 264.6 jit_solution(14183048007898670645)
XLA Ops:
  1.7 3.2 %collective-permute-start = (bf16[4,16,1280]{2,1,0:T(8,128)(2,1)}, bf16[4,16,1280]{2,1,0:T(8,128)(2,1)S(1)}, u32[]{:S(2)}, u32[]{:S(2)}) collective-permute-start(bf16[4,16,1280]{2,1,0:T(8,128)(2,1)} %first_rows.1.own_ref), channel_id=1, source_target_pairs={{0,64},{64,0},{1,65},{65,1},{2,66},{66,2},{3,67},{67,3},{4,68},{68... | collective-permute-start | bytes 491528 | tf_op jit(solution)/shard_map/ppermute | solution.py:548
  5.6 4.4 %quantize_far.1 = (bf16[1536,256]{1,0:T(8,128)(2,1)}, bf16[1536,256]{1,0:T(8,128)(2,1)}) custom-call(s32[6]{0:T(128)} %stack.42.ids_ref.refs_0_, bf16[2,3,1536,256]{3,2,1,0:T(8,128)(2,1)} %w_ref.3), custom_call_target="tpu_custom_call" | custom-call | tf_op jit(solution)/shard_map/quantize_far/pallas_call | solution.py:119
  15.2 3.6 %collective-permute-start.4 = (bf16[2,16,1280]{2,1,0:T(8,128)(2,1)S(1)}, bf16[2,16,1280]{2,1,0:T(8,128)(2,1)S(1)}, u32[]{:S(2)}, u32[]{:S(2)}) collective-permute-start(bf16[2,16,1280]{2,1,0:T(8,128)(2,1)S(1)} %get-tuple-element.68), channel_id=1, source_target_pairs={{0,32},{16,48},{32,0},{48,16},{1,33},{17,49},{33,1},{49,17},{2,34}... | collective-permute-start | bytes 245768 | tf_op jit(solution)/shard_map/ppermute | solution.py:536
  20.2 3.4 %collective-permute-done.4 = bf16[2,16,1280]{2,1,0:T(8,128)(2,1)S(1)} collective-permute-done((bf16[2,16,1280]{2,1,0:T(8,128)(2,1)S(1)}, bf16[2,16,1280]{2,1,0:T(8,128)(2,1)S(1)}, u32[]{:S(2)}, u32[]{:S(2)}) %collective-permute-start.4) | collective-permute-done | bytes 81952 | tf_op jit(solution)/shard_map/ppermute | solution.py:536
  24.1 6.5 %quantize_rest.1 = (bf16[2304,256]{1,0:T(8,128)(2,1)}, bf16[2304,256]{1,0:T(8,128)(2,1)}, bf16[768,256]{1,0:T(8,128)(2,1)}, bf16[768,256]{1,0:T(8,128)(2,1)}) custom-call(s32[6]{0:T(128)} %stack.42.ids_ref.refs_0_, bf16[2,3,1536,256]{3,2,1,0:T(8,128)(2,1)} %w_ref.3), custom_call_target="tpu_custom_call" | custom-call | tf_op jit(solution)/shard_map/quantize_rest/pallas_call | solution.py:165
  32.3 13.9 %collective-permute-done.2.refs_6_.refs_7_ = bf16[1536,256]{1,0:T(8,128)(2,1)S(1)} collective-permute-done((bf16[1536,256]{1,0:T(8,128)(2,1)}, bf16[1536,256]{1,0:T(8,128)(2,1)S(1)}, u32[]{:S(2)}, u32[]{:S(2)}) %collective-permute-start.2) | collective-permute-done | bytes 786464 | tf_op jit(solution)/shard_map/ppermute | solution.py:553
  55.8 3.6 %collective-permute-start.9 = (bf16[184,384]{1,0:T(8,128)(2,1)S(1)}, bf16[184,384]{1,0:T(8,128)(2,1)S(1)}, u32[]{:S(2)}, u32[]{:S(2)}) collective-permute-start(bf16[184,384]{1,0:T(8,128)(2,1)S(1)} %get-tuple-element.82), channel_id=1, source_target_pairs={{0,32},{16,48},{32,0},{48,16},{1,33},{17,49},{33,1},{49,17},{2,34}... | collective-permute-start | bytes 423944 | tf_op jit(solution)/shard_map/ppermute | solution.py:536
  62.4 4.4 %collective-permute-done.9.refs_2_ = bf16[184,384]{1,0:T(8,128)(2,1)S(1)} collective-permute-done((bf16[184,384]{1,0:T(8,128)(2,1)S(1)}, bf16[184,384]{1,0:T(8,128)(2,1)S(1)}, u32[]{:S(2)}, u32[]{:S(2)}) %collective-permute-start.9) | collective-permute-done | bytes 141344 | tf_op jit(solution)/shard_map/ppermute | solution.py:536
  72.3 2.9 %collective-permute-done.12.refs_3_ = bf16[88,384]{1,0:T(8,128)(2,1)S(1)} collective-permute-done((bf16[88,384]{1,0:T(8,128)(2,1)S(1)}, bf16[88,384]{1,0:T(8,128)(2,1)S(1)}, u32[]{:S(2)}, u32[]{:S(2)}) %collective-permute-start.12) | collective-permute-done | bytes 67616 | tf_op jit(solution)/shard_map/ppermute | solution.py:536
  79.0 14.5 %all_to_all.40.p_ref = bf16[16,8,1024]{2,1,0:T(8,128)(2,1)S(1)} all-to-all(bf16[16,8,1024]{2,1,0:T(8,128)(2,1)S(1)} %bitcast.24), channel_id=1, replica_groups=mesh['xh'=2,'z'=4,'c'=2,'xl'=2,'y'=4] {'xh','xl','y'}, dimensions={0} | all-to-all | bytes 524288 | tf_op jit(solution)/shard_map/all_to_all | solution.py:528
  93.6 12.1 %all_to_all.41 = bf16[16,8,1152]{2,1,0:T(8,128)(2,1)S(1)} all-to-all(bf16[16,8,1152]{2,1,0:T(8,128)(2,1)S(1)} %get-tuple-element.89), channel_id=1, replica_groups=mesh['xh'=2,'z'=4,'c'=2,'xl'=2,'y'=4] {'xh','xl','y'}, dimensions={0} | all-to-all | bytes 589824 | tf_op jit(solution)/shard_map/all_to_all | solution.py:528
  113.2 6.3 %collective-permute-done.18.refs_1_ = bf16[184,384]{1,0:T(8,128)(2,1)S(1)} collective-permute-done((bf16[184,384]{1,0:T(8,128)(2,1)S(1)}, bf16[184,384]{1,0:T(8,128)(2,1)S(1)}, u32[]{:S(2)}, u32[]{:S(2)}) %collective-permute-start.18) | collective-permute-done | bytes 141344 | tf_op jit(solution)/shard_map/ppermute | solution.py:536
  125.9 3.0 %collective-permute-done.22.refs_3_ = bf16[88,384]{1,0:T(8,128)(2,1)S(1)} collective-permute-done((bf16[88,384]{1,0:T(8,128)(2,1)S(1)}, bf16[88,384]{1,0:T(8,128)(2,1)S(1)}, u32[]{:S(2)}, u32[]{:S(2)}) %collective-permute-start.22) | collective-permute-done | bytes 67616 | tf_op jit(solution)/shard_map/ppermute | solution.py:536
  132.4 12.2 %all_to_all.42.p_ref = bf16[16,8,1024]{2,1,0:T(8,128)(2,1)S(1)} all-to-all(bf16[16,8,1024]{2,1,0:T(8,128)(2,1)S(1)} %bitcast.25), channel_id=1, replica_groups=mesh['xh'=2,'z'=4,'c'=2,'xl'=2,'y'=4] {'xh','xl','y'}, dimensions={0} | all-to-all | bytes 524288 | tf_op jit(solution)/shard_map/all_to_all | solution.py:528
  144.8 12.1 %all_to_all.43 = bf16[16,8,1152]{2,1,0:T(8,128)(2,1)S(1)} all-to-all(bf16[16,8,1152]{2,1,0:T(8,128)(2,1)S(1)} %get-tuple-element.97), channel_id=1, replica_groups=mesh['xh'=2,'z'=4,'c'=2,'xl'=2,'y'=4] {'xh','xl','y'}, dimensions={0} | all-to-all | bytes 589824 | tf_op jit(solution)/shard_map/all_to_all | solution.py:528
  164.8 5.9 %collective-permute-done.26.refs_1_ = bf16[184,384]{1,0:T(8,128)(2,1)S(1)} collective-permute-done((bf16[184,384]{1,0:T(8,128)(2,1)S(1)}, bf16[184,384]{1,0:T(8,128)(2,1)S(1)}, u32[]{:S(2)}, u32[]{:S(2)}) %collective-permute-start.26) | collective-permute-done | bytes 141344 | tf_op jit(solution)/shard_map/ppermute | solution.py:536
  171.5 2.7 %collective-permute-start.31 = (bf16[88,384]{1,0:T(8,128)(2,1)S(1)}, bf16[88,384]{1,0:T(8,128)(2,1)S(1)}, u32[]{:S(2)}, u32[]{:S(2)}) collective-permute-start(bf16[88,384]{1,0:T(8,128)(2,1)S(1)} %activate.6.refs_1_), channel_id=1, source_target_pairs={{0,48},{16,0},{32,16},{48,32},{1,49},{17,1},{33,17},{49,33},{2,50}... | collective-permute-start | bytes 202760 | tf_op jit(solution)/shard_map/ppermute | solution.py:536
  177.3 3.0 %collective-permute-done.30.refs_3_ = bf16[88,384]{1,0:T(8,128)(2,1)S(1)} collective-permute-done((bf16[88,384]{1,0:T(8,128)(2,1)S(1)}, bf16[88,384]{1,0:T(8,128)(2,1)S(1)}, u32[]{:S(2)}, u32[]{:S(2)}) %collective-permute-start.30) | collective-permute-done | bytes 67616 | tf_op jit(solution)/shard_map/ppermute | solution.py:536
  183.8 12.2 %all_to_all.44.p_ref = bf16[16,8,1024]{2,1,0:T(8,128)(2,1)S(1)} all-to-all(bf16[16,8,1024]{2,1,0:T(8,128)(2,1)S(1)} %bitcast.26), channel_id=1, replica_groups=mesh['xh'=2,'z'=4,'c'=2,'xl'=2,'y'=4] {'xh','xl','y'}, dimensions={0} | all-to-all | bytes 524288 | tf_op jit(solution)/shard_map/all_to_all | solution.py:528
  196.2 12.1 %all_to_all.45 = bf16[16,8,1152]{2,1,0:T(8,128)(2,1)S(1)} all-to-all(bf16[16,8,1152]{2,1,0:T(8,128)(2,1)S(1)} %get-tuple-element.105), channel_id=1, replica_groups=mesh['xh'=2,'z'=4,'c'=2,'xl'=2,'y'=4] {'xh','xl','y'}, dimensions={0} | all-to-all | bytes 589824 | tf_op jit(solution)/shard_map/all_to_all | solution.py:528
  216.1 6.1 %collective-permute-done.34.refs_1_ = bf16[184,384]{1,0:T(8,128)(2,1)S(1)} collective-permute-done((bf16[184,384]{1,0:T(8,128)(2,1)S(1)}, bf16[184,384]{1,0:T(8,128)(2,1)S(1)}, u32[]{:S(2)}, u32[]{:S(2)}) %collective-permute-start.34) | collective-permute-done | bytes 141344 | tf_op jit(solution)/shard_map/ppermute | solution.py:536
  228.7 3.0 %collective-permute-done.38.refs_3_ = bf16[88,384]{1,0:T(8,128)(2,1)S(1)} collective-permute-done((bf16[88,384]{1,0:T(8,128)(2,1)S(1)}, bf16[88,384]{1,0:T(8,128)(2,1)S(1)}, u32[]{:S(2)}, u32[]{:S(2)}) %collective-permute-start.38) | collective-permute-done | bytes 67616 | tf_op jit(solution)/shard_map/ppermute | solution.py:536
  235.2 12.3 %all_to_all.46.p_ref = bf16[16,8,1024]{2,1,0:T(8,128)(2,1)S(1)} all-to-all(bf16[16,8,1024]{2,1,0:T(8,128)(2,1)S(1)} %bitcast.27), channel_id=1, replica_groups=mesh['xh'=2,'z'=4,'c'=2,'xl'=2,'y'=4] {'xh','xl','y'}, dimensions={0} | all-to-all | bytes 524288 | tf_op jit(solution)/shard_map/all_to_all | solution.py:528
  248.2 15.1 %all_to_all.47.whole_ref = bf16[8,8,1024]{2,1,0:T(8,128)(2,1)S(1)} all-to-all(bf16[8,8,1024]{2,1,0:T(8,128)(2,1)S(1)} %broadcast_in_dim.2), channel_id=1, replica_groups=mesh['xh'=2,'z'=4,'c'=2,'xl'=2,'y'=4] {'xl','y'}, dimensions={0} | all-to-all | bytes 262144 | tf_op jit(solution)/shard_map/all_to_all | solution.py:528
  (111 shorter events, 85.8 us)
Async XLA Ops:
  1.7 8.3 %collective-permute-start = (bf16[4,16,1280]{2,1,0:T(8,128)(2,1)}, bf16[4,16,1280]{2,1,0:T(8,128)(2,1)S(1)}, u32[]{:S(2)}, u32[]{:S(2)}) collective-permute-start(bf16[4,16,1280]{2,1,0:T(8,128)(2,1)} %first_rows.1.own_ref), channel_id=1, source_target_pairs={{0,64},{64,0},{1,65},{65,1},{2,66},{66,2},{3,67},{67,3},{4,68},{68... | collective-permute-start | bytes 491528 | tf_op jit(solution)/shard_map/ppermute | solution.py:548
  10.1 22.3 %collective-permute-start.1 = (bf16[1536,256]{1,0:T(8,128)(2,1)}, bf16[1536,256]{1,0:T(8,128)(2,1)S(1)}, u32[]{:S(2)}, u32[]{:S(2)}) collective-permute-start(bf16[1536,256]{1,0:T(8,128)(2,1)} %get-tuple-element.63), channel_id=1, source_target_pairs={{0,64},{64,0},{1,65},{65,1},{2,66},{66,2},{3,67},{67,3},{4,68},{68... | collective-permute-start | bytes 2359304 | tf_op jit(solution)/shard_map/ppermute | solution.py:552
  12.6 33.6 %collective-permute-start.2 = (bf16[1536,256]{1,0:T(8,128)(2,1)}, bf16[1536,256]{1,0:T(8,128)(2,1)S(1)}, u32[]{:S(2)}, u32[]{:S(2)}) collective-permute-start(bf16[1536,256]{1,0:T(8,128)(2,1)} %get-tuple-element.64), channel_id=1, source_target_pairs={{0,72},{72,0},{8,64},{64,8},{1,73},{73,1},{9,65},{65,9},{2,74},{74... | collective-permute-start | bytes 2359304 | tf_op jit(solution)/shard_map/ppermute | solution.py:553
  13.2 7.0 %collective-permute-start.3 = (bf16[2,16,1280]{2,1,0:T(8,128)(2,1)S(1)}, bf16[2,16,1280]{2,1,0:T(8,128)(2,1)S(1)}, u32[]{:S(2)}, u32[]{:S(2)}) collective-permute-start(bf16[2,16,1280]{2,1,0:T(8,128)(2,1)S(1)} %get-tuple-element.67), channel_id=1, source_target_pairs={{0,16},{16,32},{32,48},{48,0},{1,17},{17,33},{33,49},{49,1},{2,18}... | collective-permute-start | bytes 245768 | tf_op jit(solution)/shard_map/ppermute | solution.py:536
  15.2 8.4 %collective-permute-start.4 = (bf16[2,16,1280]{2,1,0:T(8,128)(2,1)S(1)}, bf16[2,16,1280]{2,1,0:T(8,128)(2,1)S(1)}, u32[]{:S(2)}, u32[]{:S(2)}) collective-permute-start(bf16[2,16,1280]{2,1,0:T(8,128)(2,1)S(1)} %get-tuple-element.68), channel_id=1, source_target_pairs={{0,32},{16,48},{32,0},{48,16},{1,33},{17,49},{33,1},{49,17},{2,34}... | collective-permute-start | bytes 245768 | tf_op jit(solution)/shard_map/ppermute | solution.py:536
  23.8 6.8 %collective-permute-start.6 = (bf16[4,2,16,1280]{3,2,1,0:T(8,128)(2,1)S(1)}, bf16[4,2,16,1280]{3,2,1,0:T(8,128)(2,1)S(1)}, u32[]{:S(2)}, u32[]{:S(2)}) collective-permute-start(bf16[4,2,16,1280]{3,2,1,0:T(8,128)(2,1)S(1)} %pad_maximum_fusion.own_ref), channel_id=1, source_target_pairs={{0,8},{8,0},{1,9},{9,1},{2,10},{10,2},{3,11},{11,3},{4,12},{12,4},... | collective-permute-start | bytes 983048 | tf_op jit(solution)/shard_map/ppermute | solution.py:532
  47.5 23.2 %collective-permute-start.14 = (bf16[768,256]{1,0:T(8,128)(2,1)}, bf16[768,256]{1,0:T(8,128)(2,1)S(1)}, u32[]{:S(2)}, u32[]{:S(2)}) collective-permute-start(bf16[768,256]{1,0:T(8,128)(2,1)} %get-tuple-element.84), channel_id=1, source_target_pairs={{0,64},{64,0},{1,65},{65,1},{2,66},{66,2},{3,67},{67,3},{4,68},{68... | collective-permute-start | bytes 1179656 | tf_op jit(solution)/shard_map/ppermute | solution.py:562
  49.4 21.3 %collective-permute-start.15 = (bf16[768,256]{1,0:T(8,128)(2,1)}, bf16[768,256]{1,0:T(8,128)(2,1)S(1)}, u32[]{:S(2)}, u32[]{:S(2)}) collective-permute-start(bf16[768,256]{1,0:T(8,128)(2,1)} %get-tuple-element.85), channel_id=1, source_target_pairs={{0,72},{72,0},{8,64},{64,8},{1,73},{73,1},{9,65},{65,9},{2,74},{74... | collective-permute-start | bytes 1179656 | tf_op jit(solution)/shard_map/ppermute | solution.py:563
  53.8 8.6 %collective-permute-start.8 = (bf16[184,384]{1,0:T(8,128)(2,1)S(1)}, bf16[184,384]{1,0:T(8,128)(2,1)S(1)}, u32[]{:S(2)}, u32[]{:S(2)}) collective-permute-start(bf16[184,384]{1,0:T(8,128)(2,1)S(1)} %get-tuple-element.81), channel_id=1, source_target_pairs={{0,16},{16,32},{32,48},{48,0},{1,17},{17,33},{33,49},{49,1},{2,18}... | collective-permute-start | bytes 423944 | tf_op jit(solution)/shard_map/ppermute | solution.py:536
  55.8 11.0 %collective-permute-start.9 = (bf16[184,384]{1,0:T(8,128)(2,1)S(1)}, bf16[184,384]{1,0:T(8,128)(2,1)S(1)}, u32[]{:S(2)}, u32[]{:S(2)}) collective-permute-start(bf16[184,384]{1,0:T(8,128)(2,1)S(1)} %get-tuple-element.82), channel_id=1, source_target_pairs={{0,32},{16,48},{32,0},{48,16},{1,33},{17,49},{33,1},{49,17},{2,34}... | collective-permute-start | bytes 423944 | tf_op jit(solution)/shard_map/ppermute | solution.py:536
  59.4 7.4 %collective-permute-start.10 = (bf16[184,384]{1,0:T(8,128)(2,1)S(1)}, bf16[184,384]{1,0:T(8,128)(2,1)S(1)}, u32[]{:S(2)}, u32[]{:S(2)}) collective-permute-start(bf16[184,384]{1,0:T(8,128)(2,1)S(1)} %get-tuple-element.83), channel_id=1, source_target_pairs={{0,48},{16,0},{32,16},{48,32},{1,49},{17,1},{33,17},{49,33},{2,50}... | collective-permute-start | bytes 423944 | tf_op jit(solution)/shard_map/ppermute | solution.py:536
  109.5 10.1 %collective-permute-start.18 = (bf16[184,384]{1,0:T(8,128)(2,1)S(1)}, bf16[184,384]{1,0:T(8,128)(2,1)S(1)}, u32[]{:S(2)}, u32[]{:S(2)}) collective-permute-start(bf16[184,384]{1,0:T(8,128)(2,1)S(1)} %get-tuple-element.91), channel_id=1, source_target_pairs={{0,16},{16,32},{32,48},{48,0},{1,17},{17,33},{33,49},{49,1},{2,18}... | collective-permute-start | bytes 423944 | tf_op jit(solution)/shard_map/ppermute | solution.py:536
  109.6 10.0 %collective-permute-start.19 = (bf16[184,384]{1,0:T(8,128)(2,1)S(1)}, bf16[184,384]{1,0:T(8,128)(2,1)S(1)}, u32[]{:S(2)}, u32[]{:S(2)}) collective-permute-start(bf16[184,384]{1,0:T(8,128)(2,1)S(1)} %get-tuple-element.92), channel_id=1, source_target_pairs={{0,32},{16,48},{32,0},{48,16},{1,33},{17,49},{33,1},{49,17},{2,34}... | collective-permute-start | bytes 423944 | tf_op jit(solution)/shard_map/ppermute | solution.py:536
  111.6 8.6 %collective-permute-start.20 = (bf16[184,384]{1,0:T(8,128)(2,1)S(1)}, bf16[184,384]{1,0:T(8,128)(2,1)S(1)}, u32[]{:S(2)}, u32[]{:S(2)}) collective-permute-start(bf16[184,384]{1,0:T(8,128)(2,1)S(1)} %get-tuple-element.93), channel_id=1, source_target_pairs={{0,48},{16,0},{32,16},{48,32},{1,49},{17,1},{33,17},{49,33},{2,50}... | collective-permute-start | bytes 423944 | tf_op jit(solution)/shard_map/ppermute | solution.py:536
  123.0 6.3 %collective-permute-start.21 = (bf16[88,384]{1,0:T(8,128)(2,1)S(1)}, bf16[88,384]{1,0:T(8,128)(2,1)S(1)}, u32[]{:S(2)}, u32[]{:S(2)}) collective-permute-start(bf16[88,384]{1,0:T(8,128)(2,1)S(1)} %activate.5.refs_1_), channel_id=1, source_target_pairs={{0,16},{16,32},{32,48},{48,0},{1,17},{17,33},{33,49},{49,1},{2,18}... | collective-permute-start | bytes 202760 | tf_op jit(solution)/shard_map/ppermute | solution.py:536
  160.6 10.1 %collective-permute-start.26 = (bf16[184,384]{1,0:T(8,128)(2,1)S(1)}, bf16[184,384]{1,0:T(8,128)(2,1)S(1)}, u32[]{:S(2)}, u32[]{:S(2)}) collective-permute-start(bf16[184,384]{1,0:T(8,128)(2,1)S(1)} %get-tuple-element.99), channel_id=1, source_target_pairs={{0,16},{16,32},{32,48},{48,0},{1,17},{17,33},{33,49},{49,1},{2,18}... | collective-permute-start | bytes 423944 | tf_op jit(solution)/shard_map/ppermute | solution.py:536
  160.7 10.0 %collective-permute-start.27 = (bf16[184,384]{1,0:T(8,128)(2,1)S(1)}, bf16[184,384]{1,0:T(8,128)(2,1)S(1)}, u32[]{:S(2)}, u32[]{:S(2)}) collective-permute-start(bf16[184,384]{1,0:T(8,128)(2,1)S(1)} %get-tuple-element.100), channel_id=1, source_target_pairs={{0,32},{16,48},{32,0},{48,16},{1,33},{17,49},{33,1},{49,17},{2,34}... | collective-permute-start | bytes 423944 | tf_op jit(solution)/shard_map/ppermute | solution.py:536
  163.0 8.3 %collective-permute-start.28 = (bf16[184,384]{1,0:T(8,128)(2,1)S(1)}, bf16[184,384]{1,0:T(8,128)(2,1)S(1)}, u32[]{:S(2)}, u32[]{:S(2)}) collective-permute-start(bf16[184,384]{1,0:T(8,128)(2,1)S(1)} %get-tuple-element.101), channel_id=1, source_target_pairs={{0,48},{16,0},{32,16},{48,32},{1,49},{17,1},{33,17},{49,33},{2,50}... | collective-permute-start | bytes 423944 | tf_op jit(solution)/shard_map/ppermute | solution.py:536
  174.2 6.1 %collective-permute-start.30 = (bf16[88,384]{1,0:T(8,128)(2,1)S(1)}, bf16[88,384]{1,0:T(8,128)(2,1)S(1)}, u32[]{:S(2)}, u32[]{:S(2)}) collective-permute-start(bf16[88,384]{1,0:T(8,128)(2,1)S(1)} %activate.6.refs_1_), channel_id=1, source_target_pairs={{0,32},{16,48},{32,0},{48,16},{1,33},{17,49},{33,1},{49,17},{2,34}... | collective-permute-start | bytes 202760 | tf_op jit(solution)/shard_map/ppermute | solution.py:536
  174.5 6.2 %collective-permute-start.29 = (bf16[88,384]{1,0:T(8,128)(2,1)S(1)}, bf16[88,384]{1,0:T(8,128)(2,1)S(1)}, u32[]{:S(2)}, u32[]{:S(2)}) collective-permute-start(bf16[88,384]{1,0:T(8,128)(2,1)S(1)} %activate.6.refs_1_), channel_id=1, source_target_pairs={{0,16},{16,32},{32,48},{48,0},{1,17},{17,33},{33,49},{49,1},{2,18}... | collective-permute-start | bytes 202760 | tf_op jit(solution)/shard_map/ppermute | solution.py:536
  212.0 10.1 %collective-permute-start.34 = (bf16[184,384]{1,0:T(8,128)(2,1)S(1)}, bf16[184,384]{1,0:T(8,128)(2,1)S(1)}, u32[]{:S(2)}, u32[]{:S(2)}) collective-permute-start(bf16[184,384]{1,0:T(8,128)(2,1)S(1)} %get-tuple-element.107), channel_id=1, source_target_pairs={{0,16},{16,32},{32,48},{48,0},{1,17},{17,33},{33,49},{49,1},{2,18}... | collective-permute-start | bytes 423944 | tf_op jit(solution)/shard_map/ppermute | solution.py:536
  212.1 10.0 %collective-permute-start.35 = (bf16[184,384]{1,0:T(8,128)(2,1)S(1)}, bf16[184,384]{1,0:T(8,128)(2,1)S(1)}, u32[]{:S(2)}, u32[]{:S(2)}) collective-permute-start(bf16[184,384]{1,0:T(8,128)(2,1)S(1)} %get-tuple-element.108), channel_id=1, source_target_pairs={{0,32},{16,48},{32,0},{48,16},{1,33},{17,49},{33,1},{49,17},{2,34}... | collective-permute-start | bytes 423944 | tf_op jit(solution)/shard_map/ppermute | solution.py:536
  214.4 8.4 %collective-permute-start.36 = (bf16[184,384]{1,0:T(8,128)(2,1)S(1)}, bf16[184,384]{1,0:T(8,128)(2,1)S(1)}, u32[]{:S(2)}, u32[]{:S(2)}) collective-permute-start(bf16[184,384]{1,0:T(8,128)(2,1)S(1)} %get-tuple-element.109), channel_id=1, source_target_pairs={{0,48},{16,0},{32,16},{48,32},{1,49},{17,1},{33,17},{49,33},{2,50}... | collective-permute-start | bytes 423944 | tf_op jit(solution)/shard_map/ppermute | solution.py:536
  225.8 6.3 %collective-permute-start.37 = (bf16[88,384]{1,0:T(8,128)(2,1)S(1)}, bf16[88,384]{1,0:T(8,128)(2,1)S(1)}, u32[]{:S(2)}, u32[]{:S(2)}) collective-permute-start(bf16[88,384]{1,0:T(8,128)(2,1)S(1)} %activate.7.refs_1_), channel_id=1, source_target_pairs={{0,16},{16,32},{32,48},{48,0},{1,17},{17,33},{33,49},{49,1},{2,18}... | collective-permute-start | bytes 202760 | tf_op jit(solution)/shard_map/ppermute | solution.py:536
  (24 other events, 125.2 us)

commit v4 on v3

--- a/solution.py
+++ b/solution.py
@@ -43,8 +43,8 @@
     return lax.dot_general(a, b, dims, preferred_element_type=f32)
 
 
-def busy(us):
-    return pl.CostEstimate(flops=int(us * 1.15e9), bytes_accessed=0, transcendentals=0)
+def busy(us, moved=0):
+    return pl.CostEstimate(flops=int(us * 1.15e9), bytes_accessed=moved, transcendentals=0)
 
 
 def split3(v):
@@ -130,7 +130,7 @@
 
 
 def quant_rest_kernel(
-    ids_ref, w_ref, own_ref, other_ref, near_ref, diag_ref, buf, sem, down_buf, down_sem
+    ids_ref, w_ref, pair_ref, near_ref, diag_ref, buf, sem, down_buf, down_sem
 ):
     core, half = ids_ref[0], ids_ref[3]
     copies = []
@@ -149,7 +149,7 @@
     for copy in copies + down_copies:
         copy.start()
     for p in range(2):
-        out_ref = other_ref if p else own_ref
+        out_ref = pair_ref.at[1 - core if p else core]
         for g in range(2):
             copies[p * 2 + g].wait()
             quant_gate_up(buf.at[p * 2 + g], out_ref, g)
@@ -159,8 +159,21 @@
         quant_down(down_buf.at[p], diag_ref if p else near_ref, 0, 6)
 
 
+def keep_kernel(mixed_ref, out_ref):
+    out_ref[...] = mixed_ref[...]
+
+
+def hold(mixed):
+    return pl.pallas_call(
+        keep_kernel,
+        out_shape=jax.ShapeDtypeStruct(mixed.shape, bf16),
+        compiler_params=pltpu.CompilerParams(vmem_limit_bytes=12 << 20),
+        name="hold",
+    )(mixed)
+
+
 def quantize_rest(ids, w):
-    whole = jax.ShapeDtypeStruct((3 * UNIT_HALF, HALF), bf16)
+    whole = jax.ShapeDtypeStruct((2, 3 * UNIT_HALF, HALF), bf16)
     third = jax.ShapeDtypeStruct((UNIT_HALF, HALF), bf16)
     return pl.pallas_call(
         quant_rest_kernel,
@@ -168,14 +181,14 @@
             pl.BlockSpec(memory_space=pltpu.SMEM),
             pl.BlockSpec(memory_space=pltpu.HBM),
         ],
-        out_shape=[whole, whole, third, third],
+        out_shape=[whole, third, third],
         scratch_shapes=[
             pltpu.VMEM((4, 3, 384, HALF), bf16),
             pltpu.SemaphoreType.DMA((4,)),
             pltpu.VMEM((2, UNIT_HALF, HALF), bf16),
             pltpu.SemaphoreType.DMA((2,)),
         ],
-        compiler_params=pltpu.CompilerParams(vmem_limit_bytes=60 << 20),
+        compiler_params=pltpu.CompilerParams(vmem_limit_bytes=16 << 20),
         name="quantize_rest",
     )(ids, w)
 
@@ -318,9 +331,10 @@
     else:
         own_ref, other_ref, *refs = refs
     tab_ref, *refs = refs
-    w_refs, p_refs, xs = refs[:4], refs[4:8], refs[8]
+    w_refs, p_refs, xs = refs[:3], refs[3:7], refs[7]
+    w_refs = [w_refs[0].at[core], w_refs[0].at[1 - core], *w_refs[1:]]
     if not first:
-        x_ref = refs[9]
+        x_ref = refs[8]
         x_ref[pl.ds(pl.multiple_of(core * 128, 128), 128), :] = own_ref[...]
         x_ref[pl.ds(pl.multiple_of((1 - core) * 128, 128), 128), :] = other_ref[...]
     hot = one_hot(tab_ref, step)
@@ -356,11 +370,11 @@
         scratch.append(pltpu.VMEM((ROWS, EXT), bf16))
     return pl.pallas_call(
         lambda *refs: gate_up_kernel(step, *refs),
-        in_specs=[pl.BlockSpec(memory_space=pltpu.SMEM)] + [pl.BlockSpec()] * (len(x) + 5),
+        in_specs=[pl.BlockSpec(memory_space=pltpu.SMEM)] + [pl.BlockSpec()] * (len(x) + 4),
         out_shape=[jax.ShapeDtypeStruct((PAY, 384), bf16)] * 4,
         scratch_shapes=scratch,
-        compiler_params=pltpu.CompilerParams(vmem_limit_bytes=16 << 20),
-        cost_estimate=busy(2.2),
+        compiler_params=pltpu.CompilerParams(vmem_limit_bytes=10 << 20),
+        cost_estimate=busy(2.2, 4600000),
         name="gate_up",
     )(ids, *x, tab, *weights)
 
@@ -399,8 +413,9 @@
 
 def down_kernel(step, ids_ref, *refs):
     core, z = ids_ref[0], ids_ref[4]
-    a_refs, tab_ref, w_refs = refs[:4], refs[4], refs[5:9]
-    send_ref, keep_ref, ys = refs[9:]
+    a_refs, tab_ref, w_refs = refs[:4], refs[4], refs[5:8]
+    w_refs = [w_refs[0].at[core], w_refs[0].at[1 - core], *w_refs[1:]]
+    send_ref, keep_ref, ys = refs[8:]
     half = SLOTS // 2
     lane = lax.broadcasted_iota(jnp.int32, (half, 128), 1)
     sums = [jnp.zeros((SLOTS, HALF), f32)] * 4
@@ -430,14 +445,14 @@
 def down(step, ids, acts, tab, weights):
     return pl.pallas_call(
         lambda *refs: down_kernel(step, *refs),
-        in_specs=[pl.BlockSpec(memory_space=pltpu.SMEM)] + [pl.BlockSpec()] * 9,
+        in_specs=[pl.BlockSpec(memory_space=pltpu.SMEM)] + [pl.BlockSpec()] * 8,
         out_shape=[
             jax.ShapeDtypeStruct((128, WIDTH), bf16),
             jax.ShapeDtypeStruct((128, WIDTH), f32),
         ],
         scratch_shapes=[pltpu.VMEM((4, SLOTS, HALF), bf16)],
-        compiler_params=pltpu.CompilerParams(vmem_limit_bytes=16 << 20),
-        cost_estimate=busy(1.9),
+        compiler_params=pltpu.CompilerParams(vmem_limit_bytes=10 << 20),
+        cost_estimate=busy(1.9, 3000000),
         name="down",
     )(ids, *acts, tab, *weights)
 
@@ -553,22 +568,26 @@
     gu_diag = lax.ppermute(diag_out, ("xh", "c"), [(0, 3), (3, 0), (1, 2), (2, 1)])
     rows = spread(ids, pieces, pieces_far)
     rows = jnp.stack([rows[0]] + [around(rows[d], d) for d in (1, 2, 3)])
-    x, stream, tab = prepare(ids, rows, swap(rows), gain)
-    own, other_out, near_out, diag_out = quantize_rest(ids, trainer_weights)
-    near_out, diag_out, gu_near, gu_diag, x, stream, tab, other_out = lax.optimization_barrier(
-        (near_out, diag_out, gu_near, gu_diag, x, stream, tab, other_out)
+    mixed, near_out, diag_out = quantize_rest(ids, trainer_weights)
+    here, rows_other = lax.optimization_barrier((hold(exchange(mixed, "c")), swap(rows)))
+    x, stream, tab = prepare(ids, rows, rows_other, gain)
+
+    near_out, diag_out, gu_near, gu_diag, x, stream, tab = lax.optimization_barrier(
+        (near_out, diag_out, gu_near, gu_diag, x, stream, tab)
     )
-    other = swap(other_out)
     down_near = lax.ppermute(near_out, "xh", [(0, 1), (1, 0)])
     down_diag = lax.ppermute(diag_out, ("xh", "c"), [(0, 3), (3, 0), (1, 2), (2, 1)])
 
     x, before = [x], stream
     for step in range(STEPS):
-        part = gate_up(step, ids, x, tab, [own, other, gu_near, gu_diag])
+        part = gate_up(step, ids, x, tab, [here, gu_near, gu_diag])
+        if step == 0:
+            gu_near, gu_diag, *part = lax.optimization_barrier((gu_near, gu_diag, *part))
+            gu_near, gu_diag = hold(gu_near), hold(gu_diag)
         part = [part[0]] + [around(part[d], d) for d in (1, 2, 3)]
         act = activate(step == 0, part)
         acts = [act] + [around(act, d) for d in (1, 2, 3)]
-        send, keep = down(step, ids, acts, tab, [own, other, down_near, down_diag])
+        send, keep = down(step, ids, acts, tab, [here, down_near, down_diag])
         sums = exchange(pair(keep, swap(send)).reshape(16, 8, WIDTH), XT)
         if step < STEPS - 1:
             stream, rows = residual(sums, stream, gain)

time: 265 us -> 261 us (0.985)
  waiting for transfers between devices: 77.2 us -> 61.9 us
  starting transfers between devices: 50.9 us -> 57.4 us
  local copies, waits for them, and re-layouts: 2.01 us -> 5.97 us
    ppermute x2, waiting for transfers between devices: 13.9 us -> 1.99 us  [body(): lax.ppermute(diag_out, ('xh', 'c'), [(0, 3), (3, 0), (1, 2), (2, 1)])]
    ppermute x27, waiting for transfers between devices: 52 us -> 47.3 us  [around(): return lax.ppermute(x, 'z', [(i, (i + d) % 4) for i in range(4)])]
    unnamed x12 -> x20, local copies, waits for them, and re-layouts: 1.29 us -> 5.27 us
    all_to_all x0 -> x1, starting transfers between devices: none -> 3.94 us  [exchange(): return lax.all_to_all(x, axes, split_axis=0, concat_axis=0, tiled=True)]
    all_to_all x0 -> x1, waiting for transfers between devices: none -> 3.01 us  [exchange(): return lax.all_to_all(x, axes, split_axis=0, concat_axis=0, tiled=True)]
    ppermute x9 -> x8, waiting for transfers between devices: 10.8 us -> 9.59 us  [swap(): return lax.ppermute(x, 'c', [(0, 1), (1, 0)])]
where the time goes in v4:
time: 261 us; the launch traced here: 260 us
  blocking collectives  102 us (39%)
  waiting for transfers between devices  61.9 us (24%)
  starting transfers between devices  57.4 us (22%)
  Pallas kernels  32 us (12%)
  local copies, waits for them, and re-layouts  5.97 us (2%)
    all_to_all x8, blocking collectives, exchange(): return lax.all_to_all(x, axes, split_axis=0, concat_axis=0, tiled=True)  102 us
    ppermute x27, waiting for transfers between devices, around(): return lax.ppermute(x, 'z', [(i, (i + d) % 4) for i in range(4)])  47.3 us
    ppermute x27, starting transfers between devices, around(): return lax.ppermute(x, 'z', [(i, (i + d) % 4) for i in range(4)])  42.3 us
    ppermute x8, waiting for transfers between devices, swap(): return lax.ppermute(x, 'c', [(0, 1), (1, 0)])  9.59 us
    pallas_call x4, Pallas kernels, gate_up(): pl.pallas_call(lambda *refs: gate_up_kernel(step, *refs), in_specs=[pl.Bl...  9.21 us
    pallas_call x4, Pallas kernels, down(): pl.pallas_call(lambda *refs: down_kernel(step, *refs), in_specs=[pl.Block...  5.59 us
    unnamed x20, local copies, waits for them, and re-layouts  5.27 us
  transfers between devices with their start and end apart: 42, of which 32 were waited for; matrix products, arithmetic and copies ran while one was open for 0% of the time, Pallas kernels for 6%

profile of v4, /device:TPU:0, one launch (start us, length us, event | category | flops | bytes accessed | tf_op | source)
XLA Modules:
  0.0 259.8 jit_solution(8634629565444555612)
XLA Ops:
  1.7 3.2 %collective-permute-start = (bf16[4,16,1280]{2,1,0:T(8,128)(2,1)}, bf16[4,16,1280]{2,1,0:T(8,128)(2,1)S(1)}, u32[]{:S(2)}, u32[]{:S(2)}) collective-permute-start(bf16[4,16,1280]{2,1,0:T(8,128)(2,1)} %first_rows.1.own_ref), channel_id=1, source_target_pairs={{0,64},{64,0},{1,65},{65,1},{2,66},{66,2},{3,67},{67,3},{4,68},{68... | collective-permute-start | bytes 491528 | tf_op jit(solution)/shard_map/ppermute | solution.py:563
  5.6 4.5 %quantize_far.1 = (bf16[1536,256]{1,0:T(8,128)(2,1)}, bf16[1536,256]{1,0:T(8,128)(2,1)}) custom-call(s32[6]{0:T(128)} %stack.42.ids_ref.refs_0_, bf16[2,3,1536,256]{3,2,1,0:T(8,128)(2,1)} %w_ref.3), custom_call_target="tpu_custom_call" | custom-call | tf_op jit(solution)/shard_map/quantize_far/pallas_call | solution.py:119
  13.2 4.1 %collective-permute-start.5 = (bf16[2,16,1280]{2,1,0:T(8,128)(2,1)S(1)}, bf16[2,16,1280]{2,1,0:T(8,128)(2,1)S(1)}, u32[]{:S(2)}, u32[]{:S(2)}) collective-permute-start(bf16[2,16,1280]{2,1,0:T(8,128)(2,1)S(1)} %get-tuple-element.75), channel_id=1, source_target_pairs={{0,48},{16,0},{32,16},{48,32},{1,49},{17,1},{33,17},{49,33},{2,50}... | collective-permute-start | bytes 245768 | tf_op jit(solution)/shard_map/ppermute | solution.py:551
  28.0 4.4 %quantize_rest.1 = (bf16[2,2304,256]{2,1,0:T(8,128)(2,1)S(1)}, bf16[768,256]{1,0:T(8,128)(2,1)S(1)}, bf16[768,256]{1,0:T(8,128)(2,1)S(1)}) custom-call(s32[6]{0:T(128)S(1)} %copy-done.4, bf16[2,3,1536,256]{3,2,1,0:T(8,128)(2,1)S(1)} %copy-done), custom_call_target="tpu_custom_call" | custom-call | tf_op jit(solution)/shard_map/quantize_rest/pallas_call | solution.py:178
  35.4 3.9 %all-to-all-start = ((bf16[2,2304,256]{2,1,0:T(8,128)(2,1)}), bf16[2,2304,256]{2,1,0:T(8,128)(2,1)S(1)}, u32[]{:S(2)}, u32[]{:S(2)}) async-start(bf16[2,2304,256]{2,1,0:T(8,128)(2,1)} %copy-done.1), calls=%async_computation | async-start | bytes 4718592 | tf_op jit(solution)/shard_map/all_to_all | solution.py:543
  39.4 3.0 %all-to-all-done.mixed_ref = bf16[2,2304,256]{2,1,0:T(8,128)(2,1)S(1)} async-done(((bf16[2,2304,256]{2,1,0:T(8,128)(2,1)}), bf16[2,2304,256]{2,1,0:T(8,128)(2,1)S(1)}, u32[]{:S(2)}, u32[]{:S(2)}) %all-to-all-start) | async-done | bytes 2359328 | tf_op jit(solution)/shard_map/all_to_all | solution.py:543
  55.3 3.6 %collective-permute-start.8 = (bf16[184,384]{1,0:T(8,128)(2,1)S(1)}, bf16[184,384]{1,0:T(8,128)(2,1)S(1)}, u32[]{:S(2)}, u32[]{:S(2)}) collective-permute-start(bf16[184,384]{1,0:T(8,128)(2,1)S(1)} %get-tuple-element.92), channel_id=1, source_target_pairs={{0,32},{16,48},{32,0},{48,16},{1,33},{17,49},{33,1},{49,17},{2,34}... | collective-permute-start | bytes 423944 | tf_op jit(solution)/shard_map/ppermute | solution.py:551
  61.1 3.8 %collective-permute-done.8.refs_2_ = bf16[184,384]{1,0:T(8,128)(2,1)S(1)} collective-permute-done((bf16[184,384]{1,0:T(8,128)(2,1)S(1)}, bf16[184,384]{1,0:T(8,128)(2,1)S(1)}, u32[]{:S(2)}, u32[]{:S(2)}) %collective-permute-start.8) | collective-permute-done | bytes 141344 | tf_op jit(solution)/shard_map/ppermute | solution.py:551
  76.4 14.0 %all_to_all.45.p_ref = bf16[16,8,1024]{2,1,0:T(8,128)(2,1)S(1)} all-to-all(bf16[16,8,1024]{2,1,0:T(8,128)(2,1)S(1)} %bitcast.24), channel_id=1, replica_groups=mesh['xh'=2,'z'=4,'c'=2,'xl'=2,'y'=4] {'xh','xl','y'}, dimensions={0} | all-to-all | bytes 524288 | tf_op jit(solution)/shard_map/all_to_all | solution.py:543
  90.5 12.1 %all_to_all.46 = bf16[16,8,1152]{2,1,0:T(8,128)(2,1)S(1)} all-to-all(bf16[16,8,1152]{2,1,0:T(8,128)(2,1)S(1)} %get-tuple-element.99), channel_id=1, replica_groups=mesh['xh'=2,'z'=4,'c'=2,'xl'=2,'y'=4] {'xh','xl','y'}, dimensions={0} | all-to-all | bytes 589824 | tf_op jit(solution)/shard_map/all_to_all | solution.py:543
  107.0 3.1 %collective-permute-start.18 = (bf16[184,384]{1,0:T(8,128)(2,1)S(1)}, bf16[184,384]{1,0:T(8,128)(2,1)S(1)}, u32[]{:S(2)}, u32[]{:S(2)}) collective-permute-start(bf16[184,384]{1,0:T(8,128)(2,1)S(1)} %get-tuple-element.104), channel_id=1, source_target_pairs={{0,32},{16,48},{32,0},{48,16},{1,33},{17,49},{33,1},{49,17},{2,34}... | collective-permute-start | bytes 423944 | tf_op jit(solution)/shard_map/ppermute | solution.py:551
  110.5 3.1 %collective-permute-done.17.refs_1_ = bf16[184,384]{1,0:T(8,128)(2,1)S(1)} collective-permute-done((bf16[184,384]{1,0:T(8,128)(2,1)S(1)}, bf16[184,384]{1,0:T(8,128)(2,1)S(1)}, u32[]{:S(2)}, u32[]{:S(2)}) %collective-permute-start.17) | collective-permute-done | bytes 141344 | tf_op jit(solution)/shard_map/ppermute | solution.py:551
  113.6 3.4 %collective-permute-done.18.refs_2_ = bf16[184,384]{1,0:T(8,128)(2,1)S(1)} collective-permute-done((bf16[184,384]{1,0:T(8,128)(2,1)S(1)}, bf16[184,384]{1,0:T(8,128)(2,1)S(1)}, u32[]{:S(2)}, u32[]{:S(2)}) %collective-permute-start.18) | collective-permute-done | bytes 141344 | tf_op jit(solution)/shard_map/ppermute | solution.py:551
  118.2 3.2 %collective-permute-start.21 = (bf16[88,384]{1,0:T(8,128)(2,1)S(1)}, bf16[88,384]{1,0:T(8,128)(2,1)S(1)}, u32[]{:S(2)}, u32[]{:S(2)}) collective-permute-start(bf16[88,384]{1,0:T(8,128)(2,1)S(1)} %activate.5.refs_1_), channel_id=1, source_target_pairs={{0,32},{16,48},{32,0},{48,16},{1,33},{17,49},{33,1},{49,17},{2,34}... | collective-permute-start | bytes 202760 | tf_op jit(solution)/shard_map/ppermute | solution.py:551
  128.8 12.3 %all_to_all.47.p_ref = bf16[16,8,1024]{2,1,0:T(8,128)(2,1)S(1)} all-to-all(bf16[16,8,1024]{2,1,0:T(8,128)(2,1)S(1)} %bitcast.25), channel_id=1, replica_groups=mesh['xh'=2,'z'=4,'c'=2,'xl'=2,'y'=4] {'xh','xl','y'}, dimensions={0} | all-to-all | bytes 524288 | tf_op jit(solution)/shard_map/all_to_all | solution.py:543
  141.2 12.1 %all_to_all.48 = bf16[16,8,1152]{2,1,0:T(8,128)(2,1)S(1)} all-to-all(bf16[16,8,1152]{2,1,0:T(8,128)(2,1)S(1)} %get-tuple-element.109), channel_id=1, replica_groups=mesh['xh'=2,'z'=4,'c'=2,'xl'=2,'y'=4] {'xh','xl','y'}, dimensions={0} | all-to-all | bytes 589824 | tf_op jit(solution)/shard_map/all_to_all | solution.py:543
  161.2 5.8 %collective-permute-done.25.refs_1_ = bf16[184,384]{1,0:T(8,128)(2,1)S(1)} collective-permute-done((bf16[184,384]{1,0:T(8,128)(2,1)S(1)}, bf16[184,384]{1,0:T(8,128)(2,1)S(1)}, u32[]{:S(2)}, u32[]{:S(2)}) %collective-permute-start.25) | collective-permute-done | bytes 141344 | tf_op jit(solution)/shard_map/ppermute | solution.py:551
  168.9 3.2 %collective-permute-start.29 = (bf16[88,384]{1,0:T(8,128)(2,1)S(1)}, bf16[88,384]{1,0:T(8,128)(2,1)S(1)}, u32[]{:S(2)}, u32[]{:S(2)}) collective-permute-start(bf16[88,384]{1,0:T(8,128)(2,1)S(1)} %activate.6.refs_1_), channel_id=1, source_target_pairs={{0,32},{16,48},{32,0},{48,16},{1,33},{17,49},{33,1},{49,17},{2,34}... | collective-permute-start | bytes 202760 | tf_op jit(solution)/shard_map/ppermute | solution.py:551
  179.7 12.3 %all_to_all.49.p_ref = bf16[16,8,1024]{2,1,0:T(8,128)(2,1)S(1)} all-to-all(bf16[16,8,1024]{2,1,0:T(8,128)(2,1)S(1)} %bitcast.26), channel_id=1, replica_groups=mesh['xh'=2,'z'=4,'c'=2,'xl'=2,'y'=4] {'xh','xl','y'}, dimensions={0} | all-to-all | bytes 524288 | tf_op jit(solution)/shard_map/all_to_all | solution.py:543
  192.1 12.1 %all_to_all.50 = bf16[16,8,1152]{2,1,0:T(8,128)(2,1)S(1)} all-to-all(bf16[16,8,1152]{2,1,0:T(8,128)(2,1)S(1)} %get-tuple-element.117), channel_id=1, replica_groups=mesh['xh'=2,'z'=4,'c'=2,'xl'=2,'y'=4] {'xh','xl','y'}, dimensions={0} | all-to-all | bytes 589824 | tf_op jit(solution)/shard_map/all_to_all | solution.py:543
  212.1 5.9 %collective-permute-done.33.refs_1_ = bf16[184,384]{1,0:T(8,128)(2,1)S(1)} collective-permute-done((bf16[184,384]{1,0:T(8,128)(2,1)S(1)}, bf16[184,384]{1,0:T(8,128)(2,1)S(1)}, u32[]{:S(2)}, u32[]{:S(2)}) %collective-permute-start.33) | collective-permute-done | bytes 141344 | tf_op jit(solution)/shard_map/ppermute | solution.py:551
  219.8 3.2 %collective-permute-start.37 = (bf16[88,384]{1,0:T(8,128)(2,1)S(1)}, bf16[88,384]{1,0:T(8,128)(2,1)S(1)}, u32[]{:S(2)}, u32[]{:S(2)}) collective-permute-start(bf16[88,384]{1,0:T(8,128)(2,1)S(1)} %activate.7.refs_1_), channel_id=1, source_target_pairs={{0,32},{16,48},{32,0},{48,16},{1,33},{17,49},{33,1},{49,17},{2,34}... | collective-permute-start | bytes 202760 | tf_op jit(solution)/shard_map/ppermute | solution.py:551
  230.4 12.3 %all_to_all.51.p_ref = bf16[16,8,1024]{2,1,0:T(8,128)(2,1)S(1)} all-to-all(bf16[16,8,1024]{2,1,0:T(8,128)(2,1)S(1)} %bitcast.27), channel_id=1, replica_groups=mesh['xh'=2,'z'=4,'c'=2,'xl'=2,'y'=4] {'xh','xl','y'}, dimensions={0} | all-to-all | bytes 524288 | tf_op jit(solution)/shard_map/all_to_all | solution.py:543
  243.4 15.1 %all_to_all.52.whole_ref = bf16[8,8,1024]{2,1,0:T(8,128)(2,1)S(1)} all-to-all(bf16[8,8,1024]{2,1,0:T(8,128)(2,1)S(1)} %broadcast_in_dim.2), channel_id=1, replica_groups=mesh['xh'=2,'z'=4,'c'=2,'xl'=2,'y'=4] {'xl','y'}, dimensions={0} | all-to-all | bytes 262144 | tf_op jit(solution)/shard_map/all_to_all | solution.py:543
  (122 shorter events, 95.9 us)
Async XLA Ops:
  1.7 8.3 %collective-permute-start = (bf16[4,16,1280]{2,1,0:T(8,128)(2,1)}, bf16[4,16,1280]{2,1,0:T(8,128)(2,1)S(1)}, u32[]{:S(2)}, u32[]{:S(2)}) collective-permute-start(bf16[4,16,1280]{2,1,0:T(8,128)(2,1)} %first_rows.1.own_ref), channel_id=1, source_target_pairs={{0,64},{64,0},{1,65},{65,1},{2,66},{66,2},{3,67},{67,3},{4,68},{68... | collective-permute-start | bytes 491528 | tf_op jit(solution)/shard_map/ppermute | solution.py:563
  10.1 34.3 %collective-permute-start.1 = (bf16[1536,256]{1,0:T(8,128)(2,1)}, bf16[1536,256]{1,0:T(8,128)(2,1)S(1)}, u32[]{:S(2)}, u32[]{:S(2)}) collective-permute-start(bf16[1536,256]{1,0:T(8,128)(2,1)} %get-tuple-element.69), channel_id=1, source_target_pairs={{0,64},{64,0},{1,65},{65,1},{2,66},{66,2},{3,67},{67,3},{4,68},{68... | collective-permute-start | bytes 2359304 | tf_op jit(solution)/shard_map/ppermute | solution.py:567
  12.6 33.8 %collective-permute-start.2 = (bf16[1536,256]{1,0:T(8,128)(2,1)}, bf16[1536,256]{1,0:T(8,128)(2,1)}, u32[]{:S(2)}, u32[]{:S(2)}) collective-permute-start(bf16[1536,256]{1,0:T(8,128)(2,1)} %get-tuple-element.70), channel_id=1, source_target_pairs={{0,72},{72,0},{8,64},{64,8},{1,73},{73,1},{9,65},{65,9},{2,74},{74... | collective-permute-start | bytes 2359304 | tf_op jit(solution)/shard_map/ppermute | solution.py:568
  13.2 8.3 %collective-permute-start.5 = (bf16[2,16,1280]{2,1,0:T(8,128)(2,1)S(1)}, bf16[2,16,1280]{2,1,0:T(8,128)(2,1)S(1)}, u32[]{:S(2)}, u32[]{:S(2)}) collective-permute-start(bf16[2,16,1280]{2,1,0:T(8,128)(2,1)S(1)} %get-tuple-element.75), channel_id=1, source_target_pairs={{0,48},{16,0},{32,16},{48,32},{1,49},{17,1},{33,17},{49,33},{2,50}... | collective-permute-start | bytes 245768 | tf_op jit(solution)/shard_map/ppermute | solution.py:551
  17.3 6.9 %collective-permute-start.4 = (bf16[2,16,1280]{2,1,0:T(8,128)(2,1)S(1)}, bf16[2,16,1280]{2,1,0:T(8,128)(2,1)S(1)}, u32[]{:S(2)}, u32[]{:S(2)}) collective-permute-start(bf16[2,16,1280]{2,1,0:T(8,128)(2,1)S(1)} %get-tuple-element.74), channel_id=1, source_target_pairs={{0,32},{16,48},{32,0},{48,16},{1,33},{17,49},{33,1},{49,17},{2,34}... | collective-permute-start | bytes 245768 | tf_op jit(solution)/shard_map/ppermute | solution.py:551
  17.3 8.2 %collective-permute-start.3 = (bf16[2,16,1280]{2,1,0:T(8,128)(2,1)S(1)}, bf16[2,16,1280]{2,1,0:T(8,128)(2,1)S(1)}, u32[]{:S(2)}, u32[]{:S(2)}) collective-permute-start(bf16[2,16,1280]{2,1,0:T(8,128)(2,1)S(1)} %get-tuple-element.73), channel_id=1, source_target_pairs={{0,16},{16,32},{32,48},{48,0},{1,17},{17,33},{33,49},{49,1},{2,18}... | collective-permute-start | bytes 245768 | tf_op jit(solution)/shard_map/ppermute | solution.py:551
  25.6 17.0 %collective-permute-start.6 = (bf16[4,2,16,1280]{3,2,1,0:T(8,128)(2,1)S(1)}, bf16[4,2,16,1280]{3,2,1,0:T(8,128)(2,1)}, u32[]{:S(2)}, u32[]{:S(2)}) collective-permute-start(bf16[4,2,16,1280]{3,2,1,0:T(8,128)(2,1)S(1)} %pad_maximum_fusion.own_ref), channel_id=1, source_target_pairs={{0,8},{8,0},{1,9},{9,1},{2,10},{10,2},{3,11},{11,3},{4,12},{12,4},... | collective-permute-start | bytes 983048 | tf_op jit(solution)/shard_map/ppermute | solution.py:547
  35.4 7.0 %all-to-all-start = ((bf16[2,2304,256]{2,1,0:T(8,128)(2,1)}), bf16[2,2304,256]{2,1,0:T(8,128)(2,1)S(1)}, u32[]{:S(2)}, u32[]{:S(2)}) async-start(bf16[2,2304,256]{2,1,0:T(8,128)(2,1)} %copy-done.1), calls=%async_computation | async-start | bytes 4718592 | tf_op jit(solution)/shard_map/all_to_all | solution.py:543
  46.4 26.9 %collective-permute-start.13 = (bf16[768,256]{1,0:T(8,128)(2,1)S(1)}, bf16[768,256]{1,0:T(8,128)(2,1)S(1)}, u32[]{:S(2)}, u32[]{:S(2)}) collective-permute-start(bf16[768,256]{1,0:T(8,128)(2,1)S(1)} %copy-done.8), channel_id=1, source_target_pairs={{0,64},{64,0},{1,65},{65,1},{2,66},{66,2},{3,67},{67,3},{4,68},{68... | collective-permute-start | bytes 1179656 | tf_op jit(solution)/shard_map/ppermute | solution.py:578
  47.6 25.7 %collective-permute-start.14 = (bf16[768,256]{1,0:T(8,128)(2,1)S(1)}, bf16[768,256]{1,0:T(8,128)(2,1)S(1)}, u32[]{:S(2)}, u32[]{:S(2)}) collective-permute-start(bf16[768,256]{1,0:T(8,128)(2,1)S(1)} %copy-done.6), channel_id=1, source_target_pairs={{0,72},{72,0},{8,64},{64,8},{1,73},{73,1},{9,65},{65,9},{2,74},{74... | collective-permute-start | bytes 1179656 | tf_op jit(solution)/shard_map/ppermute | solution.py:579
  53.3 7.8 %collective-permute-start.7 = (bf16[184,384]{1,0:T(8,128)(2,1)S(1)}, bf16[184,384]{1,0:T(8,128)(2,1)S(1)}, u32[]{:S(2)}, u32[]{:S(2)}) collective-permute-start(bf16[184,384]{1,0:T(8,128)(2,1)S(1)} %get-tuple-element.91), channel_id=1, source_target_pairs={{0,16},{16,32},{32,48},{48,0},{1,17},{17,33},{33,49},{49,1},{2,18}... | collective-permute-start | bytes 423944 | tf_op jit(solution)/shard_map/ppermute | solution.py:551
  55.3 9.7 %collective-permute-start.8 = (bf16[184,384]{1,0:T(8,128)(2,1)S(1)}, bf16[184,384]{1,0:T(8,128)(2,1)S(1)}, u32[]{:S(2)}, u32[]{:S(2)}) collective-permute-start(bf16[184,384]{1,0:T(8,128)(2,1)S(1)} %get-tuple-element.92), channel_id=1, source_target_pairs={{0,32},{16,48},{32,0},{48,16},{1,33},{17,49},{33,1},{49,17},{2,34}... | collective-permute-start | bytes 423944 | tf_op jit(solution)/shard_map/ppermute | solution.py:551
  106.3 7.3 %collective-permute-start.17 = (bf16[184,384]{1,0:T(8,128)(2,1)S(1)}, bf16[184,384]{1,0:T(8,128)(2,1)S(1)}, u32[]{:S(2)}, u32[]{:S(2)}) collective-permute-start(bf16[184,384]{1,0:T(8,128)(2,1)S(1)} %get-tuple-element.103), channel_id=1, source_target_pairs={{0,16},{16,32},{32,48},{48,0},{1,17},{17,33},{33,49},{49,1},{2,18}... | collective-permute-start | bytes 423944 | tf_op jit(solution)/shard_map/ppermute | solution.py:551
  107.0 9.9 %collective-permute-start.18 = (bf16[184,384]{1,0:T(8,128)(2,1)S(1)}, bf16[184,384]{1,0:T(8,128)(2,1)S(1)}, u32[]{:S(2)}, u32[]{:S(2)}) collective-permute-start(bf16[184,384]{1,0:T(8,128)(2,1)S(1)} %get-tuple-element.104), channel_id=1, source_target_pairs={{0,32},{16,48},{32,0},{48,16},{1,33},{17,49},{33,1},{49,17},{2,34}... | collective-permute-start | bytes 423944 | tf_op jit(solution)/shard_map/ppermute | solution.py:551
  110.2 6.8 %collective-permute-start.19 = (bf16[184,384]{1,0:T(8,128)(2,1)S(1)}, bf16[184,384]{1,0:T(8,128)(2,1)S(1)}, u32[]{:S(2)}, u32[]{:S(2)}) collective-permute-start(bf16[184,384]{1,0:T(8,128)(2,1)S(1)} %get-tuple-element.105), channel_id=1, source_target_pairs={{0,48},{16,0},{32,16},{48,32},{1,49},{17,1},{33,17},{49,33},{2,50}... | collective-permute-start | bytes 423944 | tf_op jit(solution)/shard_map/ppermute | solution.py:551
  118.2 6.7 %collective-permute-start.21 = (bf16[88,384]{1,0:T(8,128)(2,1)S(1)}, bf16[88,384]{1,0:T(8,128)(2,1)S(1)}, u32[]{:S(2)}, u32[]{:S(2)}) collective-permute-start(bf16[88,384]{1,0:T(8,128)(2,1)S(1)} %activate.5.refs_1_), channel_id=1, source_target_pairs={{0,32},{16,48},{32,0},{48,16},{1,33},{17,49},{33,1},{49,17},{2,34}... | collective-permute-start | bytes 202760 | tf_op jit(solution)/shard_map/ppermute | solution.py:551
  157.0 10.1 %collective-permute-start.25 = (bf16[184,384]{1,0:T(8,128)(2,1)S(1)}, bf16[184,384]{1,0:T(8,128)(2,1)S(1)}, u32[]{:S(2)}, u32[]{:S(2)}) collective-permute-start(bf16[184,384]{1,0:T(8,128)(2,1)S(1)} %get-tuple-element.111), channel_id=1, source_target_pairs={{0,16},{16,32},{32,48},{48,0},{1,17},{17,33},{33,49},{49,1},{2,18}... | collective-permute-start | bytes 423944 | tf_op jit(solution)/shard_map/ppermute | solution.py:551
  157.1 10.0 %collective-permute-start.26 = (bf16[184,384]{1,0:T(8,128)(2,1)S(1)}, bf16[184,384]{1,0:T(8,128)(2,1)S(1)}, u32[]{:S(2)}, u32[]{:S(2)}) collective-permute-start(bf16[184,384]{1,0:T(8,128)(2,1)S(1)} %get-tuple-element.112), channel_id=1, source_target_pairs={{0,32},{16,48},{32,0},{48,16},{1,33},{17,49},{33,1},{49,17},{2,34}... | collective-permute-start | bytes 423944 | tf_op jit(solution)/shard_map/ppermute | solution.py:551
  160.0 7.7 %collective-permute-start.27 = (bf16[184,384]{1,0:T(8,128)(2,1)S(1)}, bf16[184,384]{1,0:T(8,128)(2,1)S(1)}, u32[]{:S(2)}, u32[]{:S(2)}) collective-permute-start(bf16[184,384]{1,0:T(8,128)(2,1)S(1)} %get-tuple-element.113), channel_id=1, source_target_pairs={{0,48},{16,0},{32,16},{48,32},{1,49},{17,1},{33,17},{49,33},{2,50}... | collective-permute-start | bytes 423944 | tf_op jit(solution)/shard_map/ppermute | solution.py:551
  168.9 6.7 %collective-permute-start.29 = (bf16[88,384]{1,0:T(8,128)(2,1)S(1)}, bf16[88,384]{1,0:T(8,128)(2,1)S(1)}, u32[]{:S(2)}, u32[]{:S(2)}) collective-permute-start(bf16[88,384]{1,0:T(8,128)(2,1)S(1)} %activate.6.refs_1_), channel_id=1, source_target_pairs={{0,32},{16,48},{32,0},{48,16},{1,33},{17,49},{33,1},{49,17},{2,34}... | collective-permute-start | bytes 202760 | tf_op jit(solution)/shard_map/ppermute | solution.py:551
  207.9 10.1 %collective-permute-start.33 = (bf16[184,384]{1,0:T(8,128)(2,1)S(1)}, bf16[184,384]{1,0:T(8,128)(2,1)S(1)}, u32[]{:S(2)}, u32[]{:S(2)}) collective-permute-start(bf16[184,384]{1,0:T(8,128)(2,1)S(1)} %get-tuple-element.119), channel_id=1, source_target_pairs={{0,16},{16,32},{32,48},{48,0},{1,17},{17,33},{33,49},{49,1},{2,18}... | collective-permute-start | bytes 423944 | tf_op jit(solution)/shard_map/ppermute | solution.py:551
  208.0 10.0 %collective-permute-start.34 = (bf16[184,384]{1,0:T(8,128)(2,1)S(1)}, bf16[184,384]{1,0:T(8,128)(2,1)S(1)}, u32[]{:S(2)}, u32[]{:S(2)}) collective-permute-start(bf16[184,384]{1,0:T(8,128)(2,1)S(1)} %get-tuple-element.120), channel_id=1, source_target_pairs={{0,32},{16,48},{32,0},{48,16},{1,33},{17,49},{33,1},{49,17},{2,34}... | collective-permute-start | bytes 423944 | tf_op jit(solution)/shard_map/ppermute | solution.py:551
  210.9 7.7 %collective-permute-start.35 = (bf16[184,384]{1,0:T(8,128)(2,1)S(1)}, bf16[184,384]{1,0:T(8,128)(2,1)S(1)}, u32[]{:S(2)}, u32[]{:S(2)}) collective-permute-start(bf16[184,384]{1,0:T(8,128)(2,1)S(1)} %get-tuple-element.121), channel_id=1, source_target_pairs={{0,48},{16,0},{32,16},{48,32},{1,49},{17,1},{33,17},{49,33},{2,50}... | collective-permute-start | bytes 423944 | tf_op jit(solution)/shard_map/ppermute | solution.py:551
  219.8 6.7 %collective-permute-start.37 = (bf16[88,384]{1,0:T(8,128)(2,1)S(1)}, bf16[88,384]{1,0:T(8,128)(2,1)S(1)}, u32[]{:S(2)}, u32[]{:S(2)}) collective-permute-start(bf16[88,384]{1,0:T(8,128)(2,1)S(1)} %activate.7.refs_1_), channel_id=1, source_target_pairs={{0,32},{16,48},{32,0},{48,16},{1,33},{17,49},{33,1},{49,17},{2,34}... | collective-permute-start | bytes 202760 | tf_op jit(solution)/shard_map/ppermute | solution.py:551
  (28 other events, 126.5 us)

commit v5 on v4

--- a/solution.py
+++ b/solution.py
@@ -572,8 +572,8 @@
     here, rows_other = lax.optimization_barrier((hold(exchange(mixed, "c")), swap(rows)))
     x, stream, tab = prepare(ids, rows, rows_other, gain)
 
-    near_out, diag_out, gu_near, gu_diag, x, stream, tab = lax.optimization_barrier(
-        (near_out, diag_out, gu_near, gu_diag, x, stream, tab)
+    near_out, diag_out, gu_near, x, stream, tab = lax.optimization_barrier(
+        (near_out, diag_out, gu_near, x, stream, tab)
     )
     down_near = lax.ppermute(near_out, "xh", [(0, 1), (1, 0)])
     down_diag = lax.ppermute(diag_out, ("xh", "c"), [(0, 3), (3, 0), (1, 2), (2, 1)])

time: 261 us -> 259 us (level)
  no operation moved by 1% of the time
where the time goes in v5:
time: 259 us; the launch traced here: 258 us
  blocking collectives  102 us (39%)
  waiting for transfers between devices  59.3 us (23%)
  starting transfers between devices  58.7 us (23%)
  Pallas kernels  32 us (12%)
  local copies, waits for them, and re-layouts  5.97 us (2%)
    all_to_all x8, blocking collectives, exchange(): return lax.all_to_all(x, axes, split_axis=0, concat_axis=0, tiled=True)  102 us
    ppermute x27, waiting for transfers between devices, around(): return lax.ppermute(x, 'z', [(i, (i + d) % 4) for i in range(4)])  46.7 us
    ppermute x27, starting transfers between devices, around(): return lax.ppermute(x, 'z', [(i, (i + d) % 4) for i in range(4)])  44.6 us
    ppermute x8, waiting for transfers between devices, swap(): return lax.ppermute(x, 'c', [(0, 1), (1, 0)])  9.59 us
    pallas_call x4, Pallas kernels, gate_up(): pl.pallas_call(lambda *refs: gate_up_kernel(step, *refs), in_specs=[pl.Bl...  9.19 us
    pallas_call x4, Pallas kernels, down(): pl.pallas_call(lambda *refs: down_kernel(step, *refs), in_specs=[pl.Block...  5.59 us
    unnamed x20, local copies, waits for them, and re-layouts  5.27 us
  transfers between devices with their start and end apart: 42, of which 32 were waited for; matrix products, arithmetic and copies ran while one was open for 0% of the time, Pallas kernels for 6%

profile of v5, /device:TPU:0, one launch (start us, length us, event | category | flops | bytes accessed | tf_op | source)
XLA Modules:
  0.0 258.1 jit_solution(9454863964076163674)
XLA Ops:
  1.7 3.2 %collective-permute-start = (bf16[4,16,1280]{2,1,0:T(8,128)(2,1)}, bf16[4,16,1280]{2,1,0:T(8,128)(2,1)S(1)}, u32[]{:S(2)}, u32[]{:S(2)}) collective-permute-start(bf16[4,16,1280]{2,1,0:T(8,128)(2,1)} %first_rows.1.own_ref), channel_id=1, source_target_pairs={{0,64},{64,0},{1,65},{65,1},{2,66},{66,2},{3,67},{67,3},{4,68},{68... | collective-permute-start | bytes 491528 | tf_op jit(solution)/shard_map/ppermute | solution.py:563
  5.6 4.5 %quantize_far.1 = (bf16[1536,256]{1,0:T(8,128)(2,1)}, bf16[1536,256]{1,0:T(8,128)(2,1)}) custom-call(s32[6]{0:T(128)} %stack.42.ids_ref.refs_0_, bf16[2,3,1536,256]{3,2,1,0:T(8,128)(2,1)} %w_ref.3), custom_call_target="tpu_custom_call" | custom-call | tf_op jit(solution)/shard_map/quantize_far/pallas_call | solution.py:119
  13.2 4.1 %collective-permute-start.4 = (bf16[2,16,1280]{2,1,0:T(8,128)(2,1)S(1)}, bf16[2,16,1280]{2,1,0:T(8,128)(2,1)S(1)}, u32[]{:S(2)}, u32[]{:S(2)}) collective-permute-start(bf16[2,16,1280]{2,1,0:T(8,128)(2,1)S(1)} %get-tuple-element.73), channel_id=1, source_target_pairs={{0,48},{16,0},{32,16},{48,32},{1,49},{17,1},{33,17},{49,33},{2,50}... | collective-permute-start | bytes 245768 | tf_op jit(solution)/shard_map/ppermute | solution.py:551
  18.6 3.0 %collective-permute-done.4 = bf16[2,16,1280]{2,1,0:T(8,128)(2,1)S(1)} collective-permute-done((bf16[2,16,1280]{2,1,0:T(8,128)(2,1)S(1)}, bf16[2,16,1280]{2,1,0:T(8,128)(2,1)S(1)}, u32[]{:S(2)}, u32[]{:S(2)}) %collective-permute-start.4) | collective-permute-done | bytes 81952 | tf_op jit(solution)/shard_map/ppermute | solution.py:551
  28.0 4.4 %quantize_rest.1 = (bf16[2,2304,256]{2,1,0:T(8,128)(2,1)S(1)}, bf16[768,256]{1,0:T(8,128)(2,1)S(1)}, bf16[768,256]{1,0:T(8,128)(2,1)S(1)}) custom-call(s32[6]{0:T(128)S(1)} %copy-done.4, bf16[2,3,1536,256]{3,2,1,0:T(8,128)(2,1)S(1)} %copy-done), custom_call_target="tpu_custom_call" | custom-call | tf_op jit(solution)/shard_map/quantize_rest/pallas_call | solution.py:178
  35.4 3.9 %all-to-all-start = ((bf16[2,2304,256]{2,1,0:T(8,128)(2,1)}), bf16[2,2304,256]{2,1,0:T(8,128)(2,1)S(1)}, u32[]{:S(2)}, u32[]{:S(2)}) async-start(bf16[2,2304,256]{2,1,0:T(8,128)(2,1)} %copy-done.1), calls=%async_computation | async-start | bytes 4718592 | tf_op jit(solution)/shard_map/all_to_all | solution.py:543
  39.4 3.0 %all-to-all-done.mixed_ref = bf16[2,2304,256]{2,1,0:T(8,128)(2,1)S(1)} async-done(((bf16[2,2304,256]{2,1,0:T(8,128)(2,1)}), bf16[2,2304,256]{2,1,0:T(8,128)(2,1)S(1)}, u32[]{:S(2)}, u32[]{:S(2)}) %all-to-all-start) | async-done | bytes 2359328 | tf_op jit(solution)/shard_map/all_to_all | solution.py:543
  52.4 3.6 %collective-permute-start.8 = (bf16[184,384]{1,0:T(8,128)(2,1)S(1)}, bf16[184,384]{1,0:T(8,128)(2,1)S(1)}, u32[]{:S(2)}, u32[]{:S(2)}) collective-permute-start(bf16[184,384]{1,0:T(8,128)(2,1)S(1)} %get-tuple-element.90), channel_id=1, source_target_pairs={{0,32},{16,48},{32,0},{48,16},{1,33},{17,49},{33,1},{49,17},{2,34}... | collective-permute-start | bytes 423944 | tf_op jit(solution)/shard_map/ppermute | solution.py:551
  58.4 4.8 %collective-permute-done.8.refs_2_ = bf16[184,384]{1,0:T(8,128)(2,1)S(1)} collective-permute-done((bf16[184,384]{1,0:T(8,128)(2,1)S(1)}, bf16[184,384]{1,0:T(8,128)(2,1)S(1)}, u32[]{:S(2)}, u32[]{:S(2)}) %collective-permute-start.8) | collective-permute-done | bytes 141344 | tf_op jit(solution)/shard_map/ppermute | solution.py:551
  75.0 13.6 %all_to_all.45.p_ref = bf16[16,8,1024]{2,1,0:T(8,128)(2,1)S(1)} all-to-all(bf16[16,8,1024]{2,1,0:T(8,128)(2,1)S(1)} %bitcast.24), channel_id=1, replica_groups=mesh['xh'=2,'z'=4,'c'=2,'xl'=2,'y'=4] {'xh','xl','y'}, dimensions={0} | all-to-all | bytes 524288 | tf_op jit(solution)/shard_map/all_to_all | solution.py:543
  88.8 12.1 %all_to_all.46 = bf16[16,8,1152]{2,1,0:T(8,128)(2,1)S(1)} all-to-all(bf16[16,8,1152]{2,1,0:T(8,128)(2,1)S(1)} %get-tuple-element.97), channel_id=1, replica_groups=mesh['xh'=2,'z'=4,'c'=2,'xl'=2,'y'=4] {'xh','xl','y'}, dimensions={0} | all-to-all | bytes 589824 | tf_op jit(solution)/shard_map/all_to_all | solution.py:543
  111.8 3.5 %collective-permute-done.18.refs_2_ = bf16[184,384]{1,0:T(8,128)(2,1)S(1)} collective-permute-done((bf16[184,384]{1,0:T(8,128)(2,1)S(1)}, bf16[184,384]{1,0:T(8,128)(2,1)S(1)}, u32[]{:S(2)}, u32[]{:S(2)}) %collective-permute-start.18) | collective-permute-done | bytes 141344 | tf_op jit(solution)/shard_map/ppermute | solution.py:551
  127.1 12.3 %all_to_all.47.p_ref = bf16[16,8,1024]{2,1,0:T(8,128)(2,1)S(1)} all-to-all(bf16[16,8,1024]{2,1,0:T(8,128)(2,1)S(1)} %bitcast.25), channel_id=1, replica_groups=mesh['xh'=2,'z'=4,'c'=2,'xl'=2,'y'=4] {'xh','xl','y'}, dimensions={0} | all-to-all | bytes 524288 | tf_op jit(solution)/shard_map/all_to_all | solution.py:543
  139.5 12.1 %all_to_all.48 = bf16[16,8,1152]{2,1,0:T(8,128)(2,1)S(1)} all-to-all(bf16[16,8,1152]{2,1,0:T(8,128)(2,1)S(1)} %get-tuple-element.107), channel_id=1, replica_groups=mesh['xh'=2,'z'=4,'c'=2,'xl'=2,'y'=4] {'xh','xl','y'}, dimensions={0} | all-to-all | bytes 589824 | tf_op jit(solution)/shard_map/all_to_all | solution.py:543
  155.7 3.1 %collective-permute-start.26 = (bf16[184,384]{1,0:T(8,128)(2,1)S(1)}, bf16[184,384]{1,0:T(8,128)(2,1)S(1)}, u32[]{:S(2)}, u32[]{:S(2)}) collective-permute-start(bf16[184,384]{1,0:T(8,128)(2,1)S(1)} %get-tuple-element.110), channel_id=1, source_target_pairs={{0,32},{16,48},{32,0},{48,16},{1,33},{17,49},{33,1},{49,17},{2,34}... | collective-permute-start | bytes 423944 | tf_op jit(solution)/shard_map/ppermute | solution.py:551
  159.6 3.5 %collective-permute-done.25.refs_1_ = bf16[184,384]{1,0:T(8,128)(2,1)S(1)} collective-permute-done((bf16[184,384]{1,0:T(8,128)(2,1)S(1)}, bf16[184,384]{1,0:T(8,128)(2,1)S(1)}, u32[]{:S(2)}, u32[]{:S(2)}) %collective-permute-start.25) | collective-permute-done | bytes 141344 | tf_op jit(solution)/shard_map/ppermute | solution.py:551
  167.2 3.2 %collective-permute-start.29 = (bf16[88,384]{1,0:T(8,128)(2,1)S(1)}, bf16[88,384]{1,0:T(8,128)(2,1)S(1)}, u32[]{:S(2)}, u32[]{:S(2)}) collective-permute-start(bf16[88,384]{1,0:T(8,128)(2,1)S(1)} %activate.6.refs_1_), channel_id=1, source_target_pairs={{0,32},{16,48},{32,0},{48,16},{1,33},{17,49},{33,1},{49,17},{2,34}... | collective-permute-start | bytes 202760 | tf_op jit(solution)/shard_map/ppermute | solution.py:551
  178.0 12.3 %all_to_all.49.p_ref = bf16[16,8,1024]{2,1,0:T(8,128)(2,1)S(1)} all-to-all(bf16[16,8,1024]{2,1,0:T(8,128)(2,1)S(1)} %bitcast.26), channel_id=1, replica_groups=mesh['xh'=2,'z'=4,'c'=2,'xl'=2,'y'=4] {'xh','xl','y'}, dimensions={0} | all-to-all | bytes 524288 | tf_op jit(solution)/shard_map/all_to_all | solution.py:543
  190.4 12.1 %all_to_all.50 = bf16[16,8,1152]{2,1,0:T(8,128)(2,1)S(1)} all-to-all(bf16[16,8,1152]{2,1,0:T(8,128)(2,1)S(1)} %get-tuple-element.115), channel_id=1, replica_groups=mesh['xh'=2,'z'=4,'c'=2,'xl'=2,'y'=4] {'xh','xl','y'}, dimensions={0} | all-to-all | bytes 589824 | tf_op jit(solution)/shard_map/all_to_all | solution.py:543
  206.3 2.9 %collective-permute-start.34 = (bf16[184,384]{1,0:T(8,128)(2,1)S(1)}, bf16[184,384]{1,0:T(8,128)(2,1)S(1)}, u32[]{:S(2)}, u32[]{:S(2)}) collective-permute-start(bf16[184,384]{1,0:T(8,128)(2,1)S(1)} %get-tuple-element.118), channel_id=1, source_target_pairs={{0,32},{16,48},{32,0},{48,16},{1,33},{17,49},{33,1},{49,17},{2,34}... | collective-permute-start | bytes 423944 | tf_op jit(solution)/shard_map/ppermute | solution.py:551
  210.5 5.9 %collective-permute-done.33.refs_1_ = bf16[184,384]{1,0:T(8,128)(2,1)S(1)} collective-permute-done((bf16[184,384]{1,0:T(8,128)(2,1)S(1)}, bf16[184,384]{1,0:T(8,128)(2,1)S(1)}, u32[]{:S(2)}, u32[]{:S(2)}) %collective-permute-start.33) | collective-permute-done | bytes 141344 | tf_op jit(solution)/shard_map/ppermute | solution.py:551
  218.1 3.2 %collective-permute-start.37 = (bf16[88,384]{1,0:T(8,128)(2,1)S(1)}, bf16[88,384]{1,0:T(8,128)(2,1)S(1)}, u32[]{:S(2)}, u32[]{:S(2)}) collective-permute-start(bf16[88,384]{1,0:T(8,128)(2,1)S(1)} %activate.7.refs_1_), channel_id=1, source_target_pairs={{0,32},{16,48},{32,0},{48,16},{1,33},{17,49},{33,1},{49,17},{2,34}... | collective-permute-start | bytes 202760 | tf_op jit(solution)/shard_map/ppermute | solution.py:551
  228.7 12.3 %all_to_all.51.p_ref = bf16[16,8,1024]{2,1,0:T(8,128)(2,1)S(1)} all-to-all(bf16[16,8,1024]{2,1,0:T(8,128)(2,1)S(1)} %bitcast.27), channel_id=1, replica_groups=mesh['xh'=2,'z'=4,'c'=2,'xl'=2,'y'=4] {'xh','xl','y'}, dimensions={0} | all-to-all | bytes 524288 | tf_op jit(solution)/shard_map/all_to_all | solution.py:543
  241.7 15.1 %all_to_all.52.whole_ref = bf16[8,8,1024]{2,1,0:T(8,128)(2,1)S(1)} all-to-all(bf16[8,8,1024]{2,1,0:T(8,128)(2,1)S(1)} %broadcast_in_dim.2), channel_id=1, replica_groups=mesh['xh'=2,'z'=4,'c'=2,'xl'=2,'y'=4] {'xl','y'}, dimensions={0} | all-to-all | bytes 262144 | tf_op jit(solution)/shard_map/all_to_all | solution.py:543
  (122 shorter events, 96.3 us)
Async XLA Ops:
  1.7 8.3 %collective-permute-start = (bf16[4,16,1280]{2,1,0:T(8,128)(2,1)}, bf16[4,16,1280]{2,1,0:T(8,128)(2,1)S(1)}, u32[]{:S(2)}, u32[]{:S(2)}) collective-permute-start(bf16[4,16,1280]{2,1,0:T(8,128)(2,1)} %first_rows.1.own_ref), channel_id=1, source_target_pairs={{0,64},{64,0},{1,65},{65,1},{2,66},{66,2},{3,67},{67,3},{4,68},{68... | collective-permute-start | bytes 491528 | tf_op jit(solution)/shard_map/ppermute | solution.py:563
  10.1 34.3 %collective-permute-start.1 = (bf16[1536,256]{1,0:T(8,128)(2,1)}, bf16[1536,256]{1,0:T(8,128)(2,1)S(1)}, u32[]{:S(2)}, u32[]{:S(2)}) collective-permute-start(bf16[1536,256]{1,0:T(8,128)(2,1)} %get-tuple-element.68), channel_id=1, source_target_pairs={{0,64},{64,0},{1,65},{65,1},{2,66},{66,2},{3,67},{67,3},{4,68},{68... | collective-permute-start | bytes 2359304 | tf_op jit(solution)/shard_map/ppermute | solution.py:567
  12.6 34.9 %collective-permute-start.6 = (bf16[1536,256]{1,0:T(8,128)(2,1)}, bf16[1536,256]{1,0:T(8,128)(2,1)}, u32[]{:S(2)}, u32[]{:S(2)}) collective-permute-start(bf16[1536,256]{1,0:T(8,128)(2,1)} %get-tuple-element.80), channel_id=1, source_target_pairs={{0,72},{72,0},{8,64},{64,8},{1,73},{73,1},{9,65},{65,9},{2,74},{74... | collective-permute-start | bytes 2359304 | tf_op jit(solution)/shard_map/ppermute | solution.py:568
  13.2 8.3 %collective-permute-start.4 = (bf16[2,16,1280]{2,1,0:T(8,128)(2,1)S(1)}, bf16[2,16,1280]{2,1,0:T(8,128)(2,1)S(1)}, u32[]{:S(2)}, u32[]{:S(2)}) collective-permute-start(bf16[2,16,1280]{2,1,0:T(8,128)(2,1)S(1)} %get-tuple-element.73), channel_id=1, source_target_pairs={{0,48},{16,0},{32,16},{48,32},{1,49},{17,1},{33,17},{49,33},{2,50}... | collective-permute-start | bytes 245768 | tf_op jit(solution)/shard_map/ppermute | solution.py:551
  17.3 6.9 %collective-permute-start.3 = (bf16[2,16,1280]{2,1,0:T(8,128)(2,1)S(1)}, bf16[2,16,1280]{2,1,0:T(8,128)(2,1)S(1)}, u32[]{:S(2)}, u32[]{:S(2)}) collective-permute-start(bf16[2,16,1280]{2,1,0:T(8,128)(2,1)S(1)} %get-tuple-element.72), channel_id=1, source_target_pairs={{0,32},{16,48},{32,0},{48,16},{1,33},{17,49},{33,1},{49,17},{2,34}... | collective-permute-start | bytes 245768 | tf_op jit(solution)/shard_map/ppermute | solution.py:551
  17.3 8.2 %collective-permute-start.2 = (bf16[2,16,1280]{2,1,0:T(8,128)(2,1)S(1)}, bf16[2,16,1280]{2,1,0:T(8,128)(2,1)S(1)}, u32[]{:S(2)}, u32[]{:S(2)}) collective-permute-start(bf16[2,16,1280]{2,1,0:T(8,128)(2,1)S(1)} %get-tuple-element.71), channel_id=1, source_target_pairs={{0,16},{16,32},{32,48},{48,0},{1,17},{17,33},{33,49},{49,1},{2,18}... | collective-permute-start | bytes 245768 | tf_op jit(solution)/shard_map/ppermute | solution.py:551
  25.6 17.0 %collective-permute-start.5 = (bf16[4,2,16,1280]{3,2,1,0:T(8,128)(2,1)S(1)}, bf16[4,2,16,1280]{3,2,1,0:T(8,128)(2,1)}, u32[]{:S(2)}, u32[]{:S(2)}) collective-permute-start(bf16[4,2,16,1280]{3,2,1,0:T(8,128)(2,1)S(1)} %pad_maximum_fusion.own_ref), channel_id=1, source_target_pairs={{0,8},{8,0},{1,9},{9,1},{2,10},{10,2},{3,11},{11,3},{4,12},{12,4},... | collective-permute-start | bytes 983048 | tf_op jit(solution)/shard_map/ppermute | solution.py:547
  35.4 7.0 %all-to-all-start = ((bf16[2,2304,256]{2,1,0:T(8,128)(2,1)}), bf16[2,2304,256]{2,1,0:T(8,128)(2,1)S(1)}, u32[]{:S(2)}, u32[]{:S(2)}) async-start(bf16[2,2304,256]{2,1,0:T(8,128)(2,1)} %copy-done.1), calls=%async_computation | async-start | bytes 4718592 | tf_op jit(solution)/shard_map/all_to_all | solution.py:543
  44.4 27.6 %collective-permute-start.13 = (bf16[768,256]{1,0:T(8,128)(2,1)S(1)}, bf16[768,256]{1,0:T(8,128)(2,1)S(1)}, u32[]{:S(2)}, u32[]{:S(2)}) collective-permute-start(bf16[768,256]{1,0:T(8,128)(2,1)S(1)} %copy-done.8), channel_id=1, source_target_pairs={{0,64},{64,0},{1,65},{65,1},{2,66},{66,2},{3,67},{67,3},{4,68},{68... | collective-permute-start | bytes 1179656 | tf_op jit(solution)/shard_map/ppermute | solution.py:578
  46.2 25.7 %collective-permute-start.14 = (bf16[768,256]{1,0:T(8,128)(2,1)S(1)}, bf16[768,256]{1,0:T(8,128)(2,1)S(1)}, u32[]{:S(2)}, u32[]{:S(2)}) collective-permute-start(bf16[768,256]{1,0:T(8,128)(2,1)S(1)} %copy-done.6), channel_id=1, source_target_pairs={{0,72},{72,0},{8,64},{64,8},{1,73},{73,1},{9,65},{65,9},{2,74},{74... | collective-permute-start | bytes 1179656 | tf_op jit(solution)/shard_map/ppermute | solution.py:579
  50.2 8.2 %collective-permute-start.7 = (bf16[184,384]{1,0:T(8,128)(2,1)S(1)}, bf16[184,384]{1,0:T(8,128)(2,1)S(1)}, u32[]{:S(2)}, u32[]{:S(2)}) collective-permute-start(bf16[184,384]{1,0:T(8,128)(2,1)S(1)} %get-tuple-element.89), channel_id=1, source_target_pairs={{0,16},{16,32},{32,48},{48,0},{1,17},{17,33},{33,49},{49,1},{2,18}... | collective-permute-start | bytes 423944 | tf_op jit(solution)/shard_map/ppermute | solution.py:551
  52.4 10.8 %collective-permute-start.8 = (bf16[184,384]{1,0:T(8,128)(2,1)S(1)}, bf16[184,384]{1,0:T(8,128)(2,1)S(1)}, u32[]{:S(2)}, u32[]{:S(2)}) collective-permute-start(bf16[184,384]{1,0:T(8,128)(2,1)S(1)} %get-tuple-element.90), channel_id=1, source_target_pairs={{0,32},{16,48},{32,0},{48,16},{1,33},{17,49},{33,1},{49,17},{2,34}... | collective-permute-start | bytes 423944 | tf_op jit(solution)/shard_map/ppermute | solution.py:551
  56.0 7.2 %collective-permute-start.9 = (bf16[184,384]{1,0:T(8,128)(2,1)S(1)}, bf16[184,384]{1,0:T(8,128)(2,1)S(1)}, u32[]{:S(2)}, u32[]{:S(2)}) collective-permute-start(bf16[184,384]{1,0:T(8,128)(2,1)S(1)} %get-tuple-element.91), channel_id=1, source_target_pairs={{0,48},{16,0},{32,16},{48,32},{1,49},{17,1},{33,17},{49,33},{2,50}... | collective-permute-start | bytes 423944 | tf_op jit(solution)/shard_map/ppermute | solution.py:551
  104.6 7.2 %collective-permute-start.17 = (bf16[184,384]{1,0:T(8,128)(2,1)S(1)}, bf16[184,384]{1,0:T(8,128)(2,1)S(1)}, u32[]{:S(2)}, u32[]{:S(2)}) collective-permute-start(bf16[184,384]{1,0:T(8,128)(2,1)S(1)} %get-tuple-element.101), channel_id=1, source_target_pairs={{0,16},{16,32},{32,48},{48,0},{1,17},{17,33},{33,49},{49,1},{2,18}... | collective-permute-start | bytes 423944 | tf_op jit(solution)/shard_map/ppermute | solution.py:551
  106.1 9.2 %collective-permute-start.18 = (bf16[184,384]{1,0:T(8,128)(2,1)S(1)}, bf16[184,384]{1,0:T(8,128)(2,1)S(1)}, u32[]{:S(2)}, u32[]{:S(2)}) collective-permute-start(bf16[184,384]{1,0:T(8,128)(2,1)S(1)} %get-tuple-element.102), channel_id=1, source_target_pairs={{0,32},{16,48},{32,0},{48,16},{1,33},{17,49},{33,1},{49,17},{2,34}... | collective-permute-start | bytes 423944 | tf_op jit(solution)/shard_map/ppermute | solution.py:551
  108.5 6.8 %collective-permute-start.19 = (bf16[184,384]{1,0:T(8,128)(2,1)S(1)}, bf16[184,384]{1,0:T(8,128)(2,1)S(1)}, u32[]{:S(2)}, u32[]{:S(2)}) collective-permute-start(bf16[184,384]{1,0:T(8,128)(2,1)S(1)} %get-tuple-element.103), channel_id=1, source_target_pairs={{0,48},{16,0},{32,16},{48,32},{1,49},{17,1},{33,17},{49,33},{2,50}... | collective-permute-start | bytes 423944 | tf_op jit(solution)/shard_map/ppermute | solution.py:551
  155.3 7.7 %collective-permute-start.25 = (bf16[184,384]{1,0:T(8,128)(2,1)S(1)}, bf16[184,384]{1,0:T(8,128)(2,1)S(1)}, u32[]{:S(2)}, u32[]{:S(2)}) collective-permute-start(bf16[184,384]{1,0:T(8,128)(2,1)S(1)} %get-tuple-element.109), channel_id=1, source_target_pairs={{0,16},{16,32},{32,48},{48,0},{1,17},{17,33},{33,49},{49,1},{2,18}... | collective-permute-start | bytes 423944 | tf_op jit(solution)/shard_map/ppermute | solution.py:551
  155.7 9.8 %collective-permute-start.26 = (bf16[184,384]{1,0:T(8,128)(2,1)S(1)}, bf16[184,384]{1,0:T(8,128)(2,1)S(1)}, u32[]{:S(2)}, u32[]{:S(2)}) collective-permute-start(bf16[184,384]{1,0:T(8,128)(2,1)S(1)} %get-tuple-element.110), channel_id=1, source_target_pairs={{0,32},{16,48},{32,0},{48,16},{1,33},{17,49},{33,1},{49,17},{2,34}... | collective-permute-start | bytes 423944 | tf_op jit(solution)/shard_map/ppermute | solution.py:551
  158.8 7.2 %collective-permute-start.27 = (bf16[184,384]{1,0:T(8,128)(2,1)S(1)}, bf16[184,384]{1,0:T(8,128)(2,1)S(1)}, u32[]{:S(2)}, u32[]{:S(2)}) collective-permute-start(bf16[184,384]{1,0:T(8,128)(2,1)S(1)} %get-tuple-element.111), channel_id=1, source_target_pairs={{0,48},{16,0},{32,16},{48,32},{1,49},{17,1},{33,17},{49,33},{2,50}... | collective-permute-start | bytes 423944 | tf_op jit(solution)/shard_map/ppermute | solution.py:551
  167.2 6.7 %collective-permute-start.29 = (bf16[88,384]{1,0:T(8,128)(2,1)S(1)}, bf16[88,384]{1,0:T(8,128)(2,1)S(1)}, u32[]{:S(2)}, u32[]{:S(2)}) collective-permute-start(bf16[88,384]{1,0:T(8,128)(2,1)S(1)} %activate.6.refs_1_), channel_id=1, source_target_pairs={{0,32},{16,48},{32,0},{48,16},{1,33},{17,49},{33,1},{49,17},{2,34}... | collective-permute-start | bytes 202760 | tf_op jit(solution)/shard_map/ppermute | solution.py:551
  206.3 10.1 %collective-permute-start.33 = (bf16[184,384]{1,0:T(8,128)(2,1)S(1)}, bf16[184,384]{1,0:T(8,128)(2,1)S(1)}, u32[]{:S(2)}, u32[]{:S(2)}) collective-permute-start(bf16[184,384]{1,0:T(8,128)(2,1)S(1)} %get-tuple-element.117), channel_id=1, source_target_pairs={{0,16},{16,32},{32,48},{48,0},{1,17},{17,33},{33,49},{49,1},{2,18}... | collective-permute-start | bytes 423944 | tf_op jit(solution)/shard_map/ppermute | solution.py:551
  206.3 10.0 %collective-permute-start.34 = (bf16[184,384]{1,0:T(8,128)(2,1)S(1)}, bf16[184,384]{1,0:T(8,128)(2,1)S(1)}, u32[]{:S(2)}, u32[]{:S(2)}) collective-permute-start(bf16[184,384]{1,0:T(8,128)(2,1)S(1)} %get-tuple-element.118), channel_id=1, source_target_pairs={{0,32},{16,48},{32,0},{48,16},{1,33},{17,49},{33,1},{49,17},{2,34}... | collective-permute-start | bytes 423944 | tf_op jit(solution)/shard_map/ppermute | solution.py:551
  209.2 7.7 %collective-permute-start.35 = (bf16[184,384]{1,0:T(8,128)(2,1)S(1)}, bf16[184,384]{1,0:T(8,128)(2,1)S(1)}, u32[]{:S(2)}, u32[]{:S(2)}) collective-permute-start(bf16[184,384]{1,0:T(8,128)(2,1)S(1)} %get-tuple-element.119), channel_id=1, source_target_pairs={{0,48},{16,0},{32,16},{48,32},{1,49},{17,1},{33,17},{49,33},{2,50}... | collective-permute-start | bytes 423944 | tf_op jit(solution)/shard_map/ppermute | solution.py:551
  218.1 6.7 %collective-permute-start.37 = (bf16[88,384]{1,0:T(8,128)(2,1)S(1)}, bf16[88,384]{1,0:T(8,128)(2,1)S(1)}, u32[]{:S(2)}, u32[]{:S(2)}) collective-permute-start(bf16[88,384]{1,0:T(8,128)(2,1)S(1)} %activate.7.refs_1_), channel_id=1, source_target_pairs={{0,32},{16,48},{32,0},{48,16},{1,33},{17,49},{33,1},{49,17},{2,34}... | collective-permute-start | bytes 202760 | tf_op jit(solution)/shard_map/ppermute | solution.py:551
  (28 other events, 123.2 us)

commit v6 on v5

--- a/solution.py
+++ b/solution.py
@@ -97,8 +97,8 @@
             out_ref[at + q * QB : at + (q + 1) * QB, cols] = back
 
 
-def quant_far_kernel(ids_ref, w_ref, near_ref, diag_ref, buf, sem):
-    core, half = ids_ref[0], 1 - ids_ref[3]
+def quant_far_kernel(w_ref, near_ref, diag_ref, buf, sem):
+    core, half = lax.axis_index("c"), 1 - lax.axis_index("xh")
     copies = []
     for p in range(2):
         for g in range(2):
@@ -114,19 +114,16 @@
             quant_gate_up(buf.at[p * 2 + g], diag_ref if p else near_ref, g)
 
 
-def quantize_far(ids, w):
+def quantize_far(w):
     out = jax.ShapeDtypeStruct((2 * UNIT_HALF, HALF), bf16)
     return pl.pallas_call(
         quant_far_kernel,
-        in_specs=[
-            pl.BlockSpec(memory_space=pltpu.SMEM),
-            pl.BlockSpec(memory_space=pltpu.HBM),
-        ],
+        in_specs=[pl.BlockSpec(memory_space=pltpu.HBM)],
         out_shape=[out, out],
         scratch_shapes=[pltpu.VMEM((4, 2, 384, HALF), bf16), pltpu.SemaphoreType.DMA((4,))],
         compiler_params=pltpu.CompilerParams(vmem_limit_bytes=60 << 20),
         name="quantize_far",
-    )(ids, w)
+    )(w)
 
 
 def quant_rest_kernel(
@@ -191,6 +188,59 @@
         compiler_params=pltpu.CompilerParams(vmem_limit_bytes=16 << 20),
         name="quantize_rest",
     )(ids, w)
+
+
+def side_by_side(refs, ids_ref, out_ref, put):
+    core, half = ids_ref[0], ids_ref[3]
+    far = 1 - half
+    at = [half * 2 + core, half * 2 + 1 - core, far * 2 + core, far * 2 + 1 - core]
+    for ref, b in zip(refs, at):
+        put(ref, out_ref, pl.ds(pl.multiple_of(b * HALF, HALF), HALF))
+
+
+def gate_up_side_kernel(ids_ref, here_ref, near_ref, diag_ref, out_ref):
+    core = ids_ref[0]
+
+    def put(ref, out_ref, cols):
+        out_ref[:, cols] = ref[: 2 * UNIT_HALF, :]
+
+    refs = [here_ref.at[core], here_ref.at[1 - core], near_ref, diag_ref]
+    side_by_side(refs, ids_ref, out_ref, put)
+
+
+def gate_up_side(ids, here, near, diag):
+    return pl.pallas_call(
+        gate_up_side_kernel,
+        in_specs=[pl.BlockSpec(memory_space=pltpu.SMEM)] + [pl.BlockSpec()] * 3,
+        out_shape=jax.ShapeDtypeStruct((2 * UNIT_HALF, WIDTH), bf16),
+        compiler_params=pltpu.CompilerParams(vmem_limit_bytes=12 << 20),
+        name="gate_up_side",
+    )(ids, here, near, diag)
+
+
+def down_side_kernel(ids_ref, here_ref, near_ref, diag_ref, out_ref):
+    core = ids_ref[0]
+
+    def put(ref, out_ref, cols):
+        for j in range(4):
+            out_ref[j * HALF : j * HALF + UNITS, cols] = ref[j * UNITS : (j + 1) * UNITS, :]
+            out_ref[j * HALF + UNITS : (j + 1) * HALF, cols] = ref[
+                j * UNITS + 128 : (j + 1) * UNITS, :
+            ]
+
+    rows = pl.ds(2 * UNIT_HALF, UNIT_HALF)
+    refs = [here_ref.at[core, rows], here_ref.at[1 - core, rows], near_ref, diag_ref]
+    side_by_side(refs, ids_ref, out_ref, put)
+
+
+def down_side(ids, here, near, diag):
+    return pl.pallas_call(
+        down_side_kernel,
+        in_specs=[pl.BlockSpec(memory_space=pltpu.SMEM)] + [pl.BlockSpec()] * 3,
+        out_shape=jax.ShapeDtypeStruct((4 * HALF, WIDTH), bf16),
+        compiler_params=pltpu.CompilerParams(vmem_limit_bytes=12 << 20),
+        name="down_side",
+    )(ids, here, near, diag)
 
 
 def first_kernel(*refs):
@@ -331,17 +381,18 @@
     else:
         own_ref, other_ref, *refs = refs
     tab_ref, *refs = refs
-    w_refs, p_refs, xs = refs[:3], refs[3:7], refs[7]
-    w_refs = [w_refs[0].at[core], w_refs[0].at[1 - core], *w_refs[1:]]
-    if not first:
-        x_ref = refs[8]
+    if first:
+        w_refs, p_refs, xs = refs[:3], refs[3:7], refs[7]
+        w_refs = [w_refs[0].at[core], w_refs[0].at[1 - core], *w_refs[1:]]
+    else:
+        w_ref, p_refs, x_ref = refs[0], refs[1:5], refs[5]
         x_ref[pl.ds(pl.multiple_of(core * 128, 128), 128), :] = own_ref[...]
         x_ref[pl.ds(pl.multiple_of((1 - core) * 128, 128), 128), :] = other_ref[...]
     hot = one_hot(tab_ref, step)
     picked = dot(hot.T[:SLOTS].astype(bf16), x_ref[:, :WIDTH]).astype(bf16)
-    for b in range(4):
-        xs[b] = picked[:, b * HALF : (b + 1) * HALF]
     if first:
+        for b in range(4):
+            xs[b] = picked[:, b * HALF : (b + 1) * HALF]
         tail = jnp.zeros((PAY - SLOTS, 384), bf16)
     else:
         squares = jnp.sum(x_ref[:, WIDTH:].astype(f32), axis=1, keepdims=True)
@@ -354,25 +405,27 @@
             hi.astype(f32),
             jnp.where(at == 1, mid.astype(f32), jnp.where(at == 2, low.astype(f32), 0.0)),
         ).astype(bf16)
-    ours = [xs[at] for at in block_at(ids_ref)]
+    ours = [xs[at] for at in block_at(ids_ref)] if first else None
     for d in range(4):
         at = pl.multiple_of(((z + d) % 4) * 384, 128)
-        part = dot(ours[0], w_refs[0][pl.ds(at, 384), :], NT)
-        for b in range(1, 4):
-            part = part + dot(ours[b], w_refs[b][pl.ds(at, 384), :], NT)
+        if first:
+            part = dot(ours[0], w_refs[0][pl.ds(at, 384), :], NT)
+            for b in range(1, 4):
+                part = part + dot(ours[b], w_refs[b][pl.ds(at, 384), :], NT)
+        else:
+            part = dot(picked, w_ref[pl.ds(at, 384), :], NT)
         p_refs[d][:SLOTS, :] = part.astype(bf16)
         p_refs[d][SLOTS:, :] = tail
 
 
 def gate_up(step, ids, x, tab, weights):
-    scratch = [pltpu.VMEM((4, SLOTS, HALF), bf16)]
-    if step > 0:
-        scratch.append(pltpu.VMEM((ROWS, EXT), bf16))
+    first = step == 0
+    scratch = pltpu.VMEM((4, SLOTS, HALF) if first else (ROWS, EXT), bf16)
     return pl.pallas_call(
         lambda *refs: gate_up_kernel(step, *refs),
-        in_specs=[pl.BlockSpec(memory_space=pltpu.SMEM)] + [pl.BlockSpec()] * (len(x) + 4),
+        in_specs=[pl.BlockSpec(memory_space=pltpu.SMEM)] + [pl.BlockSpec()] * (len(x) + 1 + len(weights)),
         out_shape=[jax.ShapeDtypeStruct((PAY, 384), bf16)] * 4,
-        scratch_shapes=scratch,
+        scratch_shapes=[scratch],
         compiler_params=pltpu.CompilerParams(vmem_limit_bytes=10 << 20),
         cost_estimate=busy(2.2, 4600000),
         name="gate_up",
@@ -413,44 +466,77 @@
 
 def down_kernel(step, ids_ref, *refs):
     core, z = ids_ref[0], ids_ref[4]
-    a_refs, tab_ref, w_refs = refs[:4], refs[4], refs[5:8]
-    w_refs = [w_refs[0].at[core], w_refs[0].at[1 - core], *w_refs[1:]]
-    send_ref, keep_ref, ys = refs[8:]
+    first = step == 0
+    a_refs, tab_ref, refs = refs[:4], refs[4], refs[5:]
+    if first:
+        w_refs = [refs[0].at[core], refs[0].at[1 - core], *refs[1:3]]
+        send_ref, ys = refs[3:]
+        sums = [jnp.zeros((SLOTS, HALF), f32)] * 4
+    else:
+        w_ref, send_ref, ys, acts = refs
     half = SLOTS // 2
     lane = lax.broadcasted_iota(jnp.int32, (half, 128), 1)
-    sums = [jnp.zeros((SLOTS, HALF), f32)] * 4
     for d in range(4):
         block = a_refs[d][...].astype(f32)
         middle = block[:, 128:256]
         low = jnp.concatenate([block[:, :128], jnp.where(lane < 64, middle, 0.0)], axis=1)
         high = jnp.concatenate([block[:, 256:], jnp.where(lane < 64, 0.0, middle)], axis=1)
         act = jnp.concatenate([low, high], axis=0).astype(bf16)
+        source = (z - d + 4) % 4
+        if not first:
+            acts[:, pl.ds(pl.multiple_of(source * HALF, HALF), HALF)] = act
+            continue
         for b in range(4):
             start = 2 * UNIT_HALF if b < 2 else 0
-            at = pl.multiple_of(((z - d + 4) % 4) * UNITS + start, 64)
-            after = pl.multiple_of(((z - d + 4) % 4) * UNITS + start + 128, 64)
+            at = pl.multiple_of(source * UNITS + start, 64)
+            after = pl.multiple_of(source * UNITS + start + 128, 64)
             w = jnp.concatenate([w_refs[b][pl.ds(at, UNITS), :], w_refs[b][pl.ds(after, 64), :]], axis=0)
             sums[b] = sums[b] + dot(act, w)
-    for b, at in enumerate(block_at(ids_ref)):
-        ys[at] = sums[b].astype(bf16)
+    if first:
+        for b, at in enumerate(block_at(ids_ref)):
+            ys[at] = sums[b].astype(bf16)
+        result = [ys[b] for b in range(4)]
+    else:
+        total = [dot(acts[...], w_ref[:, b * HALF : (b + 1) * HALF]) for b in range(4)]
+        result = [t.astype(bf16) for t in total]
+        for b in range(4):
+            ys[b] = result[b]
+    place_part(step, 1 - core, tab_ref, result, send_ref)
+
+
+def place_part(step, part, tab_ref, result, out_ref):
     slot = lax.broadcasted_iota(jnp.int32, (128, HALF), 1).astype(f32)
-    for ref, part in ((send_ref, 1 - core), (keep_ref, core)):
-        tab = tab_ref[pl.ds(pl.multiple_of(part * 128, 128), 128), :]
-        hot = jnp.where(slot == tab[:, 64 + step : 65 + step], 1.0, 0.0)[:, :SLOTS].astype(bf16)
-        for b in range(4):
-            rows = dot(hot, ys[b]) * tab[:, step : step + 1]
-            ref[:, b * HALF : (b + 1) * HALF] = rows.astype(ref.dtype)
+    tab = tab_ref[pl.ds(pl.multiple_of(part * 128, 128), 128), :]
+    hot = jnp.where(slot == tab[:, 64 + step : 65 + step], 1.0, 0.0)[:, :SLOTS].astype(bf16)
+    for b in range(4):
+        rows = dot(hot, result[b]) * tab[:, step : step + 1]
+        out_ref[:, b * HALF : (b + 1) * HALF] = rows.astype(out_ref.dtype)
+
+
+def kept_kernel(step, ids_ref, ys_ref, tab_ref, out_ref):
+    place_part(step, ids_ref[0], tab_ref, [ys_ref[b] for b in range(4)], out_ref)
+
+
+def kept(step, ids, ys, tab):
+    return pl.pallas_call(
+        lambda *refs: kept_kernel(step, *refs),
+        in_specs=[pl.BlockSpec(memory_space=pltpu.SMEM)] + [pl.BlockSpec()] * 2,
+        out_shape=jax.ShapeDtypeStruct((128, WIDTH), f32),
+        compiler_params=pltpu.CompilerParams(vmem_limit_bytes=6 << 20),
+        cost_estimate=busy(0.4),
+        name="kept",
+    )(ids, ys, tab)
 
 
 def down(step, ids, acts, tab, weights):
     return pl.pallas_call(
         lambda *refs: down_kernel(step, *refs),
-        in_specs=[pl.BlockSpec(memory_space=pltpu.SMEM)] + [pl.BlockSpec()] * 8,
+        in_specs=[pl.BlockSpec(memory_space=pltpu.SMEM)] + [pl.BlockSpec()] * (5 + len(weights)),
         out_shape=[
             jax.ShapeDtypeStruct((128, WIDTH), bf16),
-            jax.ShapeDtypeStruct((128, WIDTH), f32),
+            jax.ShapeDtypeStruct((4, SLOTS, HALF), bf16),
         ],
-        scratch_shapes=[pltpu.VMEM((4, SLOTS, HALF), bf16)],
+        scratch_shapes=[] if step == 0 else [pltpu.VMEM((SLOTS, WIDTH), bf16)],
         compiler_params=pltpu.CompilerParams(vmem_limit_bytes=10 << 20),
         cost_estimate=busy(1.9, 3000000),
         name="down",
@@ -562,7 +648,7 @@
     pieces = first_rows(hidden_in, lines(routing), lines(gate_weights))
     pieces_far = lax.ppermute(pieces, "xh", [(0, 1), (1, 0)])
 
-    near_out, diag_out = quantize_far(ids, trainer_weights)
+    near_out, diag_out = quantize_far(trainer_weights)
     near_out, diag_out, pieces_far = lax.optimization_barrier((near_out, diag_out, pieces_far))
     gu_near = lax.ppermute(near_out, "xh", [(0, 1), (1, 0)])
     gu_diag = lax.ppermute(diag_out, ("xh", "c"), [(0, 3), (3, 0), (1, 2), (2, 1)])
@@ -579,16 +665,20 @@
     down_diag = lax.ppermute(diag_out, ("xh", "c"), [(0, 3), (3, 0), (1, 2), (2, 1)])
 
     x, before = [x], stream
+    gu_weights, down_weights = [here, gu_near, gu_diag], [here, down_near, down_diag]
     for step in range(STEPS):
-        part = gate_up(step, ids, x, tab, [here, gu_near, gu_diag])
+        part = gate_up(step, ids, x, tab, gu_weights)
         if step == 0:
             gu_near, gu_diag, *part = lax.optimization_barrier((gu_near, gu_diag, *part))
-            gu_near, gu_diag = hold(gu_near), hold(gu_diag)
+            gu_weights = [gate_up_side(ids, here, gu_near, gu_diag)]
         part = [part[0]] + [around(part[d], d) for d in (1, 2, 3)]
         act = activate(step == 0, part)
         acts = [act] + [around(act, d) for d in (1, 2, 3)]
-        send, keep = down(step, ids, acts, tab, [here, down_near, down_diag])
-        sums = exchange(pair(keep, swap(send)).reshape(16, 8, WIDTH), XT)
+        send, ys = down(step, ids, acts, tab, down_weights)
+        if step == 0:
+            send, down_near, down_diag = lax.optimization_barrier((send, down_near, down_diag))
+            down_weights = [down_side(ids, here, down_near, down_diag)]
+        sums = exchange(pair(kept(step, ids, ys, tab), swap(send)).reshape(16, 8, WIDTH), XT)
         if step < STEPS - 1:
             stream, rows = residual(sums, stream, gain)
             rows = exchange(rows, XT).reshape(128, EXT)

time: 259 us -> 258 us (level)
  waiting for transfers between devices: 59.3 us -> 55.9 us
  Pallas kernels: 32 us -> 34.6 us
    pallas_call x0 -> x6, Pallas kernels: none -> 5.65 us  [the longest x4 3.25 us: kept(): pl.pallas_call(lambda *refs: kept_kernel(step, *refs), in_specs=[pl.Block...]
    ppermute x8, waiting for transfers between devices: 9.59 us -> 5.98 us  [swap(): return lax.ppermute(x, 'c', [(0, 1), (1, 0)])]
    unnamed x20 -> x18, local copies, waits for them, and re-layouts: 5.27 us -> 5.28 us
  transfers between devices with their start and end apart: 42 -> 42, of which waited for: 32 -> 32; matrix products, arithmetic and copies ran while one was open for 0% -> 0% of each run, Pallas kernels for 6% -> 7%
where the time goes in v6:
time: 258 us; the launch traced here: 257 us
  blocking collectives  102 us (40%)
  starting transfers between devices  58.7 us (23%)
  waiting for transfers between devices  55.9 us (22%)
  Pallas kernels  34.6 us (13%)
  local copies, waits for them, and re-layouts  5.4 us (2%)
    all_to_all x8, blocking collectives, exchange(): return lax.all_to_all(x, axes, split_axis=0, concat_axis=0, tiled=True)  102 us
    ppermute x27, waiting for transfers between devices, around(): return lax.ppermute(x, 'z', [(i, (i + d) % 4) for i in range(4)])  46.1 us
    ppermute x27, starting transfers between devices, around(): return lax.ppermute(x, 'z', [(i, (i + d) % 4) for i in range(4)])  43.9 us
    pallas_call x4, Pallas kernels, gate_up(): pl.pallas_call(lambda *refs: gate_up_kernel(step, *refs), in_specs=[pl.Bl...  8.58 us
    ppermute x8, waiting for transfers between devices, swap(): return lax.ppermute(x, 'c', [(0, 1), (1, 0)])  5.98 us
    unnamed x18, local copies, waits for them, and re-layouts  5.28 us
    pallas_call x4, Pallas kernels, down(): pl.pallas_call(lambda *refs: down_kernel(step, *refs), in_specs=[pl.Block...  5.23 us
  transfers between devices with their start and end apart: 42, of which 32 were waited for; matrix products, arithmetic and copies ran while one was open for 0% of the time, Pallas kernels for 7%

profile of v6, /device:TPU:0, one launch (start us, length us, event | category | flops | bytes accessed | tf_op | source)
XLA Modules:
  0.0 257.1 jit_solution(16434598218496330854)
XLA Ops:
  1.8 3.2 %collective-permute-start = (bf16[4,16,1280]{2,1,0:T(8,128)(2,1)}, bf16[4,16,1280]{2,1,0:T(8,128)(2,1)S(1)}, u32[]{:S(2)}, u32[]{:S(2)}) collective-permute-start(bf16[4,16,1280]{2,1,0:T(8,128)(2,1)} %first_rows.1.own_ref), channel_id=1, source_target_pairs={{0,64},{64,0},{1,65},{65,1},{2,66},{66,2},{3,67},{67,3},{4,68},{68... | collective-permute-start | bytes 491528 | tf_op jit(solution)/shard_map/ppermute | solution.py:649
  4.9 3.6 %quantize_far.1 = (bf16[1536,256]{1,0:T(8,128)(2,1)}, bf16[1536,256]{1,0:T(8,128)(2,1)}) custom-call(bf16[2,3,1536,256]{3,2,1,0:T(8,128)(2,1)} %w_ref.3), custom_call_target="tpu_custom_call" | custom-call | tf_op jit(solution)/shard_map/quantize_far/pallas_call | solution.py:119
  9.4 3.2 %collective-permute-start.1 = (bf16[1536,256]{1,0:T(8,128)(2,1)}, bf16[1536,256]{1,0:T(8,128)(2,1)S(1)}, u32[]{:S(2)}, u32[]{:S(2)}) collective-permute-start(bf16[1536,256]{1,0:T(8,128)(2,1)} %get-tuple-element.71), channel_id=1, source_target_pairs={{0,64},{64,0},{1,65},{65,1},{2,66},{66,2},{3,67},{67,3},{4,68},{68... | collective-permute-start | bytes 2359304 | tf_op jit(solution)/shard_map/ppermute | solution.py:653
  13.3 4.1 %collective-permute-start.4 = (bf16[2,16,1280]{2,1,0:T(8,128)(2,1)S(1)}, bf16[2,16,1280]{2,1,0:T(8,128)(2,1)S(1)}, u32[]{:S(2)}, u32[]{:S(2)}) collective-permute-start(bf16[2,16,1280]{2,1,0:T(8,128)(2,1)S(1)} %get-tuple-element.76), channel_id=1, source_target_pairs={{0,48},{16,0},{32,16},{48,32},{1,49},{17,1},{33,17},{49,33},{2,50}... | collective-permute-start | bytes 245768 | tf_op jit(solution)/shard_map/ppermute | solution.py:637
  18.6 3.0 %collective-permute-done.4 = bf16[2,16,1280]{2,1,0:T(8,128)(2,1)S(1)} collective-permute-done((bf16[2,16,1280]{2,1,0:T(8,128)(2,1)S(1)}, bf16[2,16,1280]{2,1,0:T(8,128)(2,1)S(1)}, u32[]{:S(2)}, u32[]{:S(2)}) %collective-permute-start.4) | collective-permute-done | bytes 81952 | tf_op jit(solution)/shard_map/ppermute | solution.py:637
  27.5 4.4 %quantize_rest.1 = (bf16[2,2304,256]{2,1,0:T(8,128)(2,1)S(1)}, bf16[768,256]{1,0:T(8,128)(2,1)S(1)}, bf16[768,256]{1,0:T(8,128)(2,1)S(1)}) custom-call(s32[6]{0:T(128)S(1)} %stack.42.ids_ref.refs_0_, bf16[2,3,1536,256]{3,2,1,0:T(8,128)(2,1)S(1)} %copy-done), custom_call_target="tpu_custom_call" | custom-call | tf_op jit(solution)/shard_map/quantize_rest/pallas_call | solution.py:175
  34.9 3.9 %all-to-all-start = ((bf16[2,2304,256]{2,1,0:T(8,128)(2,1)}), bf16[2,2304,256]{2,1,0:T(8,128)(2,1)S(1)}, u32[]{:S(2)}, u32[]{:S(2)}) async-start(bf16[2,2304,256]{2,1,0:T(8,128)(2,1)} %copy-done.1), calls=%async_computation | async-start | bytes 4718592 | tf_op jit(solution)/shard_map/all_to_all | solution.py:629
  38.8 3.0 %all-to-all-done.mixed_ref = bf16[2,2304,256]{2,1,0:T(8,128)(2,1)S(1)} async-done(((bf16[2,2304,256]{2,1,0:T(8,128)(2,1)}), bf16[2,2304,256]{2,1,0:T(8,128)(2,1)S(1)}, u32[]{:S(2)}, u32[]{:S(2)}) %all-to-all-start) | async-done | bytes 2359328 | tf_op jit(solution)/shard_map/all_to_all | solution.py:629
  52.3 3.6 %collective-permute-start.8 = (bf16[184,384]{1,0:T(8,128)(2,1)S(1)}, bf16[184,384]{1,0:T(8,128)(2,1)S(1)}, u32[]{:S(2)}, u32[]{:S(2)}) collective-permute-start(bf16[184,384]{1,0:T(8,128)(2,1)S(1)} %get-tuple-element.93), channel_id=1, source_target_pairs={{0,32},{16,48},{32,0},{48,16},{1,33},{17,49},{33,1},{49,17},{2,34}... | collective-permute-start | bytes 423944 | tf_op jit(solution)/shard_map/ppermute | solution.py:637
  58.7 4.2 %collective-permute-done.8.refs_2_ = bf16[184,384]{1,0:T(8,128)(2,1)S(1)} collective-permute-done((bf16[184,384]{1,0:T(8,128)(2,1)S(1)}, bf16[184,384]{1,0:T(8,128)(2,1)S(1)}, u32[]{:S(2)}, u32[]{:S(2)}) %collective-permute-start.8) | collective-permute-done | bytes 141344 | tf_op jit(solution)/shard_map/ppermute | solution.py:637
  74.2 13.9 %all_to_all.45.p_ref = bf16[16,8,1024]{2,1,0:T(8,128)(2,1)S(1)} all-to-all(bf16[16,8,1024]{2,1,0:T(8,128)(2,1)S(1)} %bitcast.24), channel_id=1, replica_groups=mesh['xh'=2,'z'=4,'c'=2,'xl'=2,'y'=4] {'xh','xl','y'}, dimensions={0} | all-to-all | bytes 524288 | tf_op jit(solution)/shard_map/all_to_all | solution.py:629
  88.3 12.1 %all_to_all.46 = bf16[16,8,1152]{2,1,0:T(8,128)(2,1)S(1)} all-to-all(bf16[16,8,1152]{2,1,0:T(8,128)(2,1)S(1)} %get-tuple-element.101), channel_id=1, replica_groups=mesh['xh'=2,'z'=4,'c'=2,'xl'=2,'y'=4] {'xh','xl','y'}, dimensions={0} | all-to-all | bytes 589824 | tf_op jit(solution)/shard_map/all_to_all | solution.py:629
  111.3 3.8 %collective-permute-done.18.refs_2_ = bf16[184,384]{1,0:T(8,128)(2,1)S(1)} collective-permute-done((bf16[184,384]{1,0:T(8,128)(2,1)S(1)}, bf16[184,384]{1,0:T(8,128)(2,1)S(1)}, u32[]{:S(2)}, u32[]{:S(2)}) %collective-permute-start.18) | collective-permute-done | bytes 141344 | tf_op jit(solution)/shard_map/ppermute | solution.py:637
  126.7 12.3 %all_to_all.47.p_ref = bf16[16,8,1024]{2,1,0:T(8,128)(2,1)S(1)} all-to-all(bf16[16,8,1024]{2,1,0:T(8,128)(2,1)S(1)} %bitcast.25), channel_id=1, replica_groups=mesh['xh'=2,'z'=4,'c'=2,'xl'=2,'y'=4] {'xh','xl','y'}, dimensions={0} | all-to-all | bytes 524288 | tf_op jit(solution)/shard_map/all_to_all | solution.py:629
  139.1 12.1 %all_to_all.48 = bf16[16,8,1152]{2,1,0:T(8,128)(2,1)S(1)} all-to-all(bf16[16,8,1152]{2,1,0:T(8,128)(2,1)S(1)} %get-tuple-element.113), channel_id=1, replica_groups=mesh['xh'=2,'z'=4,'c'=2,'xl'=2,'y'=4] {'xh','xl','y'}, dimensions={0} | all-to-all | bytes 589824 | tf_op jit(solution)/shard_map/all_to_all | solution.py:629
  154.9 3.2 %collective-permute-start.26 = (bf16[184,384]{1,0:T(8,128)(2,1)S(1)}, bf16[184,384]{1,0:T(8,128)(2,1)S(1)}, u32[]{:S(2)}, u32[]{:S(2)}) collective-permute-start(bf16[184,384]{1,0:T(8,128)(2,1)S(1)} %get-tuple-element.116), channel_id=1, source_target_pairs={{0,32},{16,48},{32,0},{48,16},{1,33},{17,49},{33,1},{49,17},{2,34}... | collective-permute-start | bytes 423944 | tf_op jit(solution)/shard_map/ppermute | solution.py:637
  158.9 3.6 %collective-permute-done.25.refs_1_ = bf16[184,384]{1,0:T(8,128)(2,1)S(1)} collective-permute-done((bf16[184,384]{1,0:T(8,128)(2,1)S(1)}, bf16[184,384]{1,0:T(8,128)(2,1)S(1)}, u32[]{:S(2)}, u32[]{:S(2)}) %collective-permute-start.25) | collective-permute-done | bytes 141344 | tf_op jit(solution)/shard_map/ppermute | solution.py:637
  166.6 3.2 %collective-permute-start.29 = (bf16[88,384]{1,0:T(8,128)(2,1)S(1)}, bf16[88,384]{1,0:T(8,128)(2,1)S(1)}, u32[]{:S(2)}, u32[]{:S(2)}) collective-permute-start(bf16[88,384]{1,0:T(8,128)(2,1)S(1)} %activate.6.refs_1_), channel_id=1, source_target_pairs={{0,32},{16,48},{32,0},{48,16},{1,33},{17,49},{33,1},{49,17},{2,34}... | collective-permute-start | bytes 202760 | tf_op jit(solution)/shard_map/ppermute | solution.py:637
  177.3 12.3 %all_to_all.49.p_ref = bf16[16,8,1024]{2,1,0:T(8,128)(2,1)S(1)} all-to-all(bf16[16,8,1024]{2,1,0:T(8,128)(2,1)S(1)} %bitcast.26), channel_id=1, replica_groups=mesh['xh'=2,'z'=4,'c'=2,'xl'=2,'y'=4] {'xh','xl','y'}, dimensions={0} | all-to-all | bytes 524288 | tf_op jit(solution)/shard_map/all_to_all | solution.py:629
  189.7 12.1 %all_to_all.50 = bf16[16,8,1152]{2,1,0:T(8,128)(2,1)S(1)} all-to-all(bf16[16,8,1152]{2,1,0:T(8,128)(2,1)S(1)} %get-tuple-element.121), channel_id=1, replica_groups=mesh['xh'=2,'z'=4,'c'=2,'xl'=2,'y'=4] {'xh','xl','y'}, dimensions={0} | all-to-all | bytes 589824 | tf_op jit(solution)/shard_map/all_to_all | solution.py:629
  209.5 5.9 %collective-permute-done.33.refs_1_ = bf16[184,384]{1,0:T(8,128)(2,1)S(1)} collective-permute-done((bf16[184,384]{1,0:T(8,128)(2,1)S(1)}, bf16[184,384]{1,0:T(8,128)(2,1)S(1)}, u32[]{:S(2)}, u32[]{:S(2)}) %collective-permute-start.33) | collective-permute-done | bytes 141344 | tf_op jit(solution)/shard_map/ppermute | solution.py:637
  217.2 3.2 %collective-permute-start.37 = (bf16[88,384]{1,0:T(8,128)(2,1)S(1)}, bf16[88,384]{1,0:T(8,128)(2,1)S(1)}, u32[]{:S(2)}, u32[]{:S(2)}) collective-permute-start(bf16[88,384]{1,0:T(8,128)(2,1)S(1)} %activate.7.refs_1_), channel_id=1, source_target_pairs={{0,32},{16,48},{32,0},{48,16},{1,33},{17,49},{33,1},{49,17},{2,34}... | collective-permute-start | bytes 202760 | tf_op jit(solution)/shard_map/ppermute | solution.py:637
  227.7 12.3 %all_to_all.51.p_ref = bf16[16,8,1024]{2,1,0:T(8,128)(2,1)S(1)} all-to-all(bf16[16,8,1024]{2,1,0:T(8,128)(2,1)S(1)} %bitcast.27), channel_id=1, replica_groups=mesh['xh'=2,'z'=4,'c'=2,'xl'=2,'y'=4] {'xh','xl','y'}, dimensions={0} | all-to-all | bytes 524288 | tf_op jit(solution)/shard_map/all_to_all | solution.py:629
  240.7 15.1 %all_to_all.52.whole_ref = bf16[8,8,1024]{2,1,0:T(8,128)(2,1)S(1)} all-to-all(bf16[8,8,1024]{2,1,0:T(8,128)(2,1)S(1)} %broadcast_in_dim.2), channel_id=1, replica_groups=mesh['xh'=2,'z'=4,'c'=2,'xl'=2,'y'=4] {'xl','y'}, dimensions={0} | all-to-all | bytes 262144 | tf_op jit(solution)/shard_map/all_to_all | solution.py:629
  (124 shorter events, 95.4 us)
Async XLA Ops:
  1.8 7.6 %collective-permute-start = (bf16[4,16,1280]{2,1,0:T(8,128)(2,1)}, bf16[4,16,1280]{2,1,0:T(8,128)(2,1)S(1)}, u32[]{:S(2)}, u32[]{:S(2)}) collective-permute-start(bf16[4,16,1280]{2,1,0:T(8,128)(2,1)} %first_rows.1.own_ref), channel_id=1, source_target_pairs={{0,64},{64,0},{1,65},{65,1},{2,66},{66,2},{3,67},{67,3},{4,68},{68... | collective-permute-start | bytes 491528 | tf_op jit(solution)/shard_map/ppermute | solution.py:649
  9.4 34.5 %collective-permute-start.1 = (bf16[1536,256]{1,0:T(8,128)(2,1)}, bf16[1536,256]{1,0:T(8,128)(2,1)S(1)}, u32[]{:S(2)}, u32[]{:S(2)}) collective-permute-start(bf16[1536,256]{1,0:T(8,128)(2,1)} %get-tuple-element.71), channel_id=1, source_target_pairs={{0,64},{64,0},{1,65},{65,1},{2,66},{66,2},{3,67},{67,3},{4,68},{68... | collective-permute-start | bytes 2359304 | tf_op jit(solution)/shard_map/ppermute | solution.py:653
  12.6 34.3 %collective-permute-start.6 = (bf16[1536,256]{1,0:T(8,128)(2,1)}, bf16[1536,256]{1,0:T(8,128)(2,1)}, u32[]{:S(2)}, u32[]{:S(2)}) collective-permute-start(bf16[1536,256]{1,0:T(8,128)(2,1)} %get-tuple-element.83), channel_id=1, source_target_pairs={{0,72},{72,0},{8,64},{64,8},{1,73},{73,1},{9,65},{65,9},{2,74},{74... | collective-permute-start | bytes 2359304 | tf_op jit(solution)/shard_map/ppermute | solution.py:654
  13.3 8.3 %collective-permute-start.4 = (bf16[2,16,1280]{2,1,0:T(8,128)(2,1)S(1)}, bf16[2,16,1280]{2,1,0:T(8,128)(2,1)S(1)}, u32[]{:S(2)}, u32[]{:S(2)}) collective-permute-start(bf16[2,16,1280]{2,1,0:T(8,128)(2,1)S(1)} %get-tuple-element.76), channel_id=1, source_target_pairs={{0,48},{16,0},{32,16},{48,32},{1,49},{17,1},{33,17},{49,33},{2,50}... | collective-permute-start | bytes 245768 | tf_op jit(solution)/shard_map/ppermute | solution.py:637
  17.4 6.8 %collective-permute-start.3 = (bf16[2,16,1280]{2,1,0:T(8,128)(2,1)S(1)}, bf16[2,16,1280]{2,1,0:T(8,128)(2,1)S(1)}, u32[]{:S(2)}, u32[]{:S(2)}) collective-permute-start(bf16[2,16,1280]{2,1,0:T(8,128)(2,1)S(1)} %get-tuple-element.75), channel_id=1, source_target_pairs={{0,32},{16,48},{32,0},{48,16},{1,33},{17,49},{33,1},{49,17},{2,34}... | collective-permute-start | bytes 245768 | tf_op jit(solution)/shard_map/ppermute | solution.py:637
  17.4 7.7 %collective-permute-start.2 = (bf16[2,16,1280]{2,1,0:T(8,128)(2,1)S(1)}, bf16[2,16,1280]{2,1,0:T(8,128)(2,1)S(1)}, u32[]{:S(2)}, u32[]{:S(2)}) collective-permute-start(bf16[2,16,1280]{2,1,0:T(8,128)(2,1)S(1)} %get-tuple-element.74), channel_id=1, source_target_pairs={{0,16},{16,32},{32,48},{48,0},{1,17},{17,33},{33,49},{49,1},{2,18}... | collective-permute-start | bytes 245768 | tf_op jit(solution)/shard_map/ppermute | solution.py:637
  25.1 17.0 %collective-permute-start.5 = (bf16[4,2,16,1280]{3,2,1,0:T(8,128)(2,1)S(1)}, bf16[4,2,16,1280]{3,2,1,0:T(8,128)(2,1)}, u32[]{:S(2)}, u32[]{:S(2)}) collective-permute-start(bf16[4,2,16,1280]{3,2,1,0:T(8,128)(2,1)S(1)} %pad_maximum_fusion.own_ref), channel_id=1, source_target_pairs={{0,8},{8,0},{1,9},{9,1},{2,10},{10,2},{3,11},{11,3},{4,12},{12,4},... | collective-permute-start | bytes 983048 | tf_op jit(solution)/shard_map/ppermute | solution.py:633
  34.9 7.0 %all-to-all-start = ((bf16[2,2304,256]{2,1,0:T(8,128)(2,1)}), bf16[2,2304,256]{2,1,0:T(8,128)(2,1)S(1)}, u32[]{:S(2)}, u32[]{:S(2)}) async-start(bf16[2,2304,256]{2,1,0:T(8,128)(2,1)} %copy-done.1), calls=%async_computation | async-start | bytes 4718592 | tf_op jit(solution)/shard_map/all_to_all | solution.py:629
  43.9 27.3 %collective-permute-start.13 = (bf16[768,256]{1,0:T(8,128)(2,1)S(1)}, bf16[768,256]{1,0:T(8,128)(2,1)S(1)}, u32[]{:S(2)}, u32[]{:S(2)}) collective-permute-start(bf16[768,256]{1,0:T(8,128)(2,1)S(1)} %copy-done.7), channel_id=1, source_target_pairs={{0,64},{64,0},{1,65},{65,1},{2,66},{66,2},{3,67},{67,3},{4,68},{68... | collective-permute-start | bytes 1179656 | tf_op jit(solution)/shard_map/ppermute | solution.py:664
  46.3 24.9 %collective-permute-start.14 = (bf16[768,256]{1,0:T(8,128)(2,1)S(1)}, bf16[768,256]{1,0:T(8,128)(2,1)S(1)}, u32[]{:S(2)}, u32[]{:S(2)}) collective-permute-start(bf16[768,256]{1,0:T(8,128)(2,1)S(1)} %copy-done.5), channel_id=1, source_target_pairs={{0,72},{72,0},{8,64},{64,8},{1,73},{73,1},{9,65},{65,9},{2,74},{74... | collective-permute-start | bytes 1179656 | tf_op jit(solution)/shard_map/ppermute | solution.py:665
  49.7 9.0 %collective-permute-start.7 = (bf16[184,384]{1,0:T(8,128)(2,1)S(1)}, bf16[184,384]{1,0:T(8,128)(2,1)S(1)}, u32[]{:S(2)}, u32[]{:S(2)}) collective-permute-start(bf16[184,384]{1,0:T(8,128)(2,1)S(1)} %get-tuple-element.92), channel_id=1, source_target_pairs={{0,16},{16,32},{32,48},{48,0},{1,17},{17,33},{33,49},{49,1},{2,18}... | collective-permute-start | bytes 423944 | tf_op jit(solution)/shard_map/ppermute | solution.py:637
  52.3 10.5 %collective-permute-start.8 = (bf16[184,384]{1,0:T(8,128)(2,1)S(1)}, bf16[184,384]{1,0:T(8,128)(2,1)S(1)}, u32[]{:S(2)}, u32[]{:S(2)}) collective-permute-start(bf16[184,384]{1,0:T(8,128)(2,1)S(1)} %get-tuple-element.93), channel_id=1, source_target_pairs={{0,32},{16,48},{32,0},{48,16},{1,33},{17,49},{33,1},{49,17},{2,34}... | collective-permute-start | bytes 423944 | tf_op jit(solution)/shard_map/ppermute | solution.py:637
  55.9 6.9 %collective-permute-start.9 = (bf16[184,384]{1,0:T(8,128)(2,1)S(1)}, bf16[184,384]{1,0:T(8,128)(2,1)S(1)}, u32[]{:S(2)}, u32[]{:S(2)}) collective-permute-start(bf16[184,384]{1,0:T(8,128)(2,1)S(1)} %get-tuple-element.94), channel_id=1, source_target_pairs={{0,48},{16,0},{32,16},{48,32},{1,49},{17,1},{33,17},{49,33},{2,50}... | collective-permute-start | bytes 423944 | tf_op jit(solution)/shard_map/ppermute | solution.py:637
  103.9 7.4 %collective-permute-start.17 = (bf16[184,384]{1,0:T(8,128)(2,1)S(1)}, bf16[184,384]{1,0:T(8,128)(2,1)S(1)}, u32[]{:S(2)}, u32[]{:S(2)}) collective-permute-start(bf16[184,384]{1,0:T(8,128)(2,1)S(1)} %get-tuple-element.105), channel_id=1, source_target_pairs={{0,16},{16,32},{32,48},{48,0},{1,17},{17,33},{33,49},{49,1},{2,18}... | collective-permute-start | bytes 423944 | tf_op jit(solution)/shard_map/ppermute | solution.py:637
  105.4 9.7 %collective-permute-start.18 = (bf16[184,384]{1,0:T(8,128)(2,1)S(1)}, bf16[184,384]{1,0:T(8,128)(2,1)S(1)}, u32[]{:S(2)}, u32[]{:S(2)}) collective-permute-start(bf16[184,384]{1,0:T(8,128)(2,1)S(1)} %get-tuple-element.106), channel_id=1, source_target_pairs={{0,32},{16,48},{32,0},{48,16},{1,33},{17,49},{33,1},{49,17},{2,34}... | collective-permute-start | bytes 423944 | tf_op jit(solution)/shard_map/ppermute | solution.py:637
  108.0 7.1 %collective-permute-start.19 = (bf16[184,384]{1,0:T(8,128)(2,1)S(1)}, bf16[184,384]{1,0:T(8,128)(2,1)S(1)}, u32[]{:S(2)}, u32[]{:S(2)}) collective-permute-start(bf16[184,384]{1,0:T(8,128)(2,1)S(1)} %get-tuple-element.107), channel_id=1, source_target_pairs={{0,48},{16,0},{32,16},{48,32},{1,49},{17,1},{33,17},{49,33},{2,50}... | collective-permute-start | bytes 423944 | tf_op jit(solution)/shard_map/ppermute | solution.py:637
  154.7 7.8 %collective-permute-start.25 = (bf16[184,384]{1,0:T(8,128)(2,1)S(1)}, bf16[184,384]{1,0:T(8,128)(2,1)S(1)}, u32[]{:S(2)}, u32[]{:S(2)}) collective-permute-start(bf16[184,384]{1,0:T(8,128)(2,1)S(1)} %get-tuple-element.115), channel_id=1, source_target_pairs={{0,16},{16,32},{32,48},{48,0},{1,17},{17,33},{33,49},{49,1},{2,18}... | collective-permute-start | bytes 423944 | tf_op jit(solution)/shard_map/ppermute | solution.py:637
  154.9 9.9 %collective-permute-start.26 = (bf16[184,384]{1,0:T(8,128)(2,1)S(1)}, bf16[184,384]{1,0:T(8,128)(2,1)S(1)}, u32[]{:S(2)}, u32[]{:S(2)}) collective-permute-start(bf16[184,384]{1,0:T(8,128)(2,1)S(1)} %get-tuple-element.116), channel_id=1, source_target_pairs={{0,32},{16,48},{32,0},{48,16},{1,33},{17,49},{33,1},{49,17},{2,34}... | collective-permute-start | bytes 423944 | tf_op jit(solution)/shard_map/ppermute | solution.py:637
  158.0 7.3 %collective-permute-start.27 = (bf16[184,384]{1,0:T(8,128)(2,1)S(1)}, bf16[184,384]{1,0:T(8,128)(2,1)S(1)}, u32[]{:S(2)}, u32[]{:S(2)}) collective-permute-start(bf16[184,384]{1,0:T(8,128)(2,1)S(1)} %get-tuple-element.117), channel_id=1, source_target_pairs={{0,48},{16,0},{32,16},{48,32},{1,49},{17,1},{33,17},{49,33},{2,50}... | collective-permute-start | bytes 423944 | tf_op jit(solution)/shard_map/ppermute | solution.py:637
  166.6 6.7 %collective-permute-start.29 = (bf16[88,384]{1,0:T(8,128)(2,1)S(1)}, bf16[88,384]{1,0:T(8,128)(2,1)S(1)}, u32[]{:S(2)}, u32[]{:S(2)}) collective-permute-start(bf16[88,384]{1,0:T(8,128)(2,1)S(1)} %activate.6.refs_1_), channel_id=1, source_target_pairs={{0,32},{16,48},{32,0},{48,16},{1,33},{17,49},{33,1},{49,17},{2,34}... | collective-permute-start | bytes 202760 | tf_op jit(solution)/shard_map/ppermute | solution.py:637
  205.3 10.1 %collective-permute-start.33 = (bf16[184,384]{1,0:T(8,128)(2,1)S(1)}, bf16[184,384]{1,0:T(8,128)(2,1)S(1)}, u32[]{:S(2)}, u32[]{:S(2)}) collective-permute-start(bf16[184,384]{1,0:T(8,128)(2,1)S(1)} %get-tuple-element.123), channel_id=1, source_target_pairs={{0,16},{16,32},{32,48},{48,0},{1,17},{17,33},{33,49},{49,1},{2,18}... | collective-permute-start | bytes 423944 | tf_op jit(solution)/shard_map/ppermute | solution.py:637
  205.4 10.0 %collective-permute-start.34 = (bf16[184,384]{1,0:T(8,128)(2,1)S(1)}, bf16[184,384]{1,0:T(8,128)(2,1)S(1)}, u32[]{:S(2)}, u32[]{:S(2)}) collective-permute-start(bf16[184,384]{1,0:T(8,128)(2,1)S(1)} %get-tuple-element.124), channel_id=1, source_target_pairs={{0,32},{16,48},{32,0},{48,16},{1,33},{17,49},{33,1},{49,17},{2,34}... | collective-permute-start | bytes 423944 | tf_op jit(solution)/shard_map/ppermute | solution.py:637
  208.3 7.7 %collective-permute-start.35 = (bf16[184,384]{1,0:T(8,128)(2,1)S(1)}, bf16[184,384]{1,0:T(8,128)(2,1)S(1)}, u32[]{:S(2)}, u32[]{:S(2)}) collective-permute-start(bf16[184,384]{1,0:T(8,128)(2,1)S(1)} %get-tuple-element.125), channel_id=1, source_target_pairs={{0,48},{16,0},{32,16},{48,32},{1,49},{17,1},{33,17},{49,33},{2,50}... | collective-permute-start | bytes 423944 | tf_op jit(solution)/shard_map/ppermute | solution.py:637
  217.2 6.7 %collective-permute-start.37 = (bf16[88,384]{1,0:T(8,128)(2,1)S(1)}, bf16[88,384]{1,0:T(8,128)(2,1)S(1)}, u32[]{:S(2)}, u32[]{:S(2)}) collective-permute-start(bf16[88,384]{1,0:T(8,128)(2,1)S(1)} %activate.7.refs_1_), channel_id=1, source_target_pairs={{0,32},{16,48},{32,0},{48,16},{1,33},{17,49},{33,1},{49,17},{2,34}... | collective-permute-start | bytes 202760 | tf_op jit(solution)/shard_map/ppermute | solution.py:637
  (27 other events, 121.4 us)

commit v7 on v6

--- a/solution.py
+++ b/solution.py
@@ -649,7 +649,6 @@
     pieces_far = lax.ppermute(pieces, "xh", [(0, 1), (1, 0)])
 
     near_out, diag_out = quantize_far(trainer_weights)
-    near_out, diag_out, pieces_far = lax.optimization_barrier((near_out, diag_out, pieces_far))
     gu_near = lax.ppermute(near_out, "xh", [(0, 1), (1, 0)])
     gu_diag = lax.ppermute(diag_out, ("xh", "c"), [(0, 3), (3, 0), (1, 2), (2, 1)])
     rows = spread(ids, pieces, pieces_far)

time: 258 us -> 257 us (level)
    ppermute x2, starting transfers between devices: 0.61 us -> 4.55 us  [body(): lax.ppermute(diag_out, ('xh', 'c'), [(0, 3), (3, 0), (1, 2), (2, 1)])]
    ppermute x1, starting transfers between devices: 3.24 us -> 0.5 us  [body(): gu_near = lax.ppermute(near_out, 'xh', [(0, 1), (1, 0)])]
where the time goes in v7:
time: 257 us; the launch traced here: 256 us
  blocking collectives  103 us (40%)
  starting transfers between devices  56.6 us (22%)
  waiting for transfers between devices  55.8 us (22%)
  Pallas kernels  34.6 us (13%)
  local copies, waits for them, and re-layouts  5.4 us (2%)
    all_to_all x8, blocking collectives, exchange(): return lax.all_to_all(x, axes, split_axis=0, concat_axis=0, tiled=True)  103 us
    ppermute x27, waiting for transfers between devices, around(): return lax.ppermute(x, 'z', [(i, (i + d) % 4) for i in range(4)])  46.8 us
    ppermute x27, starting transfers between devices, around(): return lax.ppermute(x, 'z', [(i, (i + d) % 4) for i in range(4)])  42.5 us
    pallas_call x4, Pallas kernels, gate_up(): pl.pallas_call(lambda *refs: gate_up_kernel(step, *refs), in_specs=[pl.Bl...  8.58 us
    ppermute x8, waiting for transfers between devices, swap(): return lax.ppermute(x, 'c', [(0, 1), (1, 0)])  5.98 us
    unnamed x18, local copies, waits for them, and re-layouts  5.28 us
    pallas_call x4, Pallas kernels, down(): pl.pallas_call(lambda *refs: down_kernel(step, *refs), in_specs=[pl.Block...  5.23 us
  transfers between devices with their start and end apart: 42, of which 32 were waited for; matrix products, arithmetic and copies ran while one was open for 0% of the time, Pallas kernels for 7%

profile of v7, /device:TPU:0, one launch (start us, length us, event | category | flops | bytes accessed | tf_op | source)
XLA Modules:
  0.0 256.0 jit_solution(12372016249608959651)
XLA Ops:
  1.8 3.2 %collective-permute-start.1 = (bf16[4,16,1280]{2,1,0:T(8,128)(2,1)}, bf16[4,16,1280]{2,1,0:T(8,128)(2,1)S(1)}, u32[]{:S(2)}, u32[]{:S(2)}) collective-permute-start(bf16[4,16,1280]{2,1,0:T(8,128)(2,1)} %first_rows.1.own_ref), channel_id=1, source_target_pairs={{0,64},{64,0},{1,65},{65,1},{2,66},{66,2},{3,67},{67,3},{4,68},{68... | collective-permute-start | bytes 491528 | tf_op jit(solution)/shard_map/ppermute | solution.py:649
  4.9 3.6 %quantize_far.1 = (bf16[1536,256]{1,0:T(8,128)(2,1)}, bf16[1536,256]{1,0:T(8,128)(2,1)}) custom-call(bf16[2,3,1536,256]{3,2,1,0:T(8,128)(2,1)} %w_ref.3), custom_call_target="tpu_custom_call" | custom-call | tf_op jit(solution)/shard_map/quantize_far/pallas_call | solution.py:119
  11.8 4.1 %collective-permute-start.4 = (bf16[2,16,1280]{2,1,0:T(8,128)(2,1)S(1)}, bf16[2,16,1280]{2,1,0:T(8,128)(2,1)S(1)}, u32[]{:S(2)}, u32[]{:S(2)}) collective-permute-start(bf16[2,16,1280]{2,1,0:T(8,128)(2,1)S(1)} %get-tuple-element.70), channel_id=1, source_target_pairs={{0,48},{16,0},{32,16},{48,32},{1,49},{17,1},{33,17},{49,33},{2,50}... | collective-permute-start | bytes 245768 | tf_op jit(solution)/shard_map/ppermute | solution.py:637
  17.1 2.9 %collective-permute-done.4 = bf16[2,16,1280]{2,1,0:T(8,128)(2,1)S(1)} collective-permute-done((bf16[2,16,1280]{2,1,0:T(8,128)(2,1)S(1)}, bf16[2,16,1280]{2,1,0:T(8,128)(2,1)S(1)}, u32[]{:S(2)}, u32[]{:S(2)}) %collective-permute-start.4) | collective-permute-done | bytes 81952 | tf_op jit(solution)/shard_map/ppermute | solution.py:637
  26.7 4.4 %quantize_rest.1 = (bf16[2,2304,256]{2,1,0:T(8,128)(2,1)S(1)}, bf16[768,256]{1,0:T(8,128)(2,1)S(1)}, bf16[768,256]{1,0:T(8,128)(2,1)S(1)}) custom-call(s32[6]{0:T(128)S(1)} %stack.42.ids_ref.refs_0_, bf16[2,3,1536,256]{3,2,1,0:T(8,128)(2,1)S(1)} %copy-done), custom_call_target="tpu_custom_call" | custom-call | tf_op jit(solution)/shard_map/quantize_rest/pallas_call | solution.py:175
  34.0 3.9 %all-to-all-start = ((bf16[2,2304,256]{2,1,0:T(8,128)(2,1)}), bf16[2,2304,256]{2,1,0:T(8,128)(2,1)S(1)}, u32[]{:S(2)}, u32[]{:S(2)}) async-start(bf16[2,2304,256]{2,1,0:T(8,128)(2,1)} %copy-done.1), calls=%async_computation | async-start | bytes 4718592 | tf_op jit(solution)/shard_map/all_to_all | solution.py:629
  38.0 3.0 %all-to-all-done.mixed_ref = bf16[2,2304,256]{2,1,0:T(8,128)(2,1)S(1)} async-done(((bf16[2,2304,256]{2,1,0:T(8,128)(2,1)}), bf16[2,2304,256]{2,1,0:T(8,128)(2,1)S(1)}, u32[]{:S(2)}, u32[]{:S(2)}) %all-to-all-start) | async-done | bytes 2359328 | tf_op jit(solution)/shard_map/all_to_all | solution.py:629
  49.6 3.6 %collective-permute-start.8 = (bf16[184,384]{1,0:T(8,128)(2,1)S(1)}, bf16[184,384]{1,0:T(8,128)(2,1)S(1)}, u32[]{:S(2)}, u32[]{:S(2)}) collective-permute-start(bf16[184,384]{1,0:T(8,128)(2,1)S(1)} %get-tuple-element.87), channel_id=1, source_target_pairs={{0,32},{16,48},{32,0},{48,16},{1,33},{17,49},{33,1},{49,17},{2,34}... | collective-permute-start | bytes 423944 | tf_op jit(solution)/shard_map/ppermute | solution.py:637
  55.2 3.7 %collective-permute-done.8.refs_2_ = bf16[184,384]{1,0:T(8,128)(2,1)S(1)} collective-permute-done((bf16[184,384]{1,0:T(8,128)(2,1)S(1)}, bf16[184,384]{1,0:T(8,128)(2,1)S(1)}, u32[]{:S(2)}, u32[]{:S(2)}) %collective-permute-start.8) | collective-permute-done | bytes 141344 | tf_op jit(solution)/shard_map/ppermute | solution.py:637
  59.9 3.1 %collective-permute-start.10 = (bf16[88,384]{1,0:T(8,128)(2,1)S(1)}, bf16[88,384]{1,0:T(8,128)(2,1)S(1)}, u32[]{:S(2)}, u32[]{:S(2)}) collective-permute-start(bf16[88,384]{1,0:T(8,128)(2,1)S(1)} %activate.4.refs_1_), channel_id=1, source_target_pairs={{0,16},{16,32},{32,48},{48,0},{1,17},{17,33},{33,49},{49,1},{2,18}... | collective-permute-start | bytes 202760 | tf_op jit(solution)/shard_map/ppermute | solution.py:637
  72.1 15.0 %all_to_all.45.p_ref = bf16[16,8,1024]{2,1,0:T(8,128)(2,1)S(1)} all-to-all(bf16[16,8,1024]{2,1,0:T(8,128)(2,1)S(1)} %bitcast.24), channel_id=1, replica_groups=mesh['xh'=2,'z'=4,'c'=2,'xl'=2,'y'=4] {'xh','xl','y'}, dimensions={0} | all-to-all | bytes 524288 | tf_op jit(solution)/shard_map/all_to_all | solution.py:629
  87.2 12.1 %all_to_all.46 = bf16[16,8,1152]{2,1,0:T(8,128)(2,1)S(1)} all-to-all(bf16[16,8,1152]{2,1,0:T(8,128)(2,1)S(1)} %get-tuple-element.95), channel_id=1, replica_groups=mesh['xh'=2,'z'=4,'c'=2,'xl'=2,'y'=4] {'xh','xl','y'}, dimensions={0} | all-to-all | bytes 589824 | tf_op jit(solution)/shard_map/all_to_all | solution.py:629
  110.2 3.7 %collective-permute-done.18.refs_2_ = bf16[184,384]{1,0:T(8,128)(2,1)S(1)} collective-permute-done((bf16[184,384]{1,0:T(8,128)(2,1)S(1)}, bf16[184,384]{1,0:T(8,128)(2,1)S(1)}, u32[]{:S(2)}, u32[]{:S(2)}) %collective-permute-start.18) | collective-permute-done | bytes 141344 | tf_op jit(solution)/shard_map/ppermute | solution.py:637
  125.6 12.2 %all_to_all.47.p_ref = bf16[16,8,1024]{2,1,0:T(8,128)(2,1)S(1)} all-to-all(bf16[16,8,1024]{2,1,0:T(8,128)(2,1)S(1)} %bitcast.25), channel_id=1, replica_groups=mesh['xh'=2,'z'=4,'c'=2,'xl'=2,'y'=4] {'xh','xl','y'}, dimensions={0} | all-to-all | bytes 524288 | tf_op jit(solution)/shard_map/all_to_all | solution.py:629
  137.9 12.1 %all_to_all.48 = bf16[16,8,1152]{2,1,0:T(8,128)(2,1)S(1)} all-to-all(bf16[16,8,1152]{2,1,0:T(8,128)(2,1)S(1)} %get-tuple-element.107), channel_id=1, replica_groups=mesh['xh'=2,'z'=4,'c'=2,'xl'=2,'y'=4] {'xh','xl','y'}, dimensions={0} | all-to-all | bytes 589824 | tf_op jit(solution)/shard_map/all_to_all | solution.py:629
  153.7 3.1 %collective-permute-start.26 = (bf16[184,384]{1,0:T(8,128)(2,1)S(1)}, bf16[184,384]{1,0:T(8,128)(2,1)S(1)}, u32[]{:S(2)}, u32[]{:S(2)}) collective-permute-start(bf16[184,384]{1,0:T(8,128)(2,1)S(1)} %get-tuple-element.110), channel_id=1, source_target_pairs={{0,32},{16,48},{32,0},{48,16},{1,33},{17,49},{33,1},{49,17},{2,34}... | collective-permute-start | bytes 423944 | tf_op jit(solution)/shard_map/ppermute | solution.py:637
  157.8 3.6 %collective-permute-done.25.refs_1_ = bf16[184,384]{1,0:T(8,128)(2,1)S(1)} collective-permute-done((bf16[184,384]{1,0:T(8,128)(2,1)S(1)}, bf16[184,384]{1,0:T(8,128)(2,1)S(1)}, u32[]{:S(2)}, u32[]{:S(2)}) %collective-permute-start.25) | collective-permute-done | bytes 141344 | tf_op jit(solution)/shard_map/ppermute | solution.py:637
  165.4 3.2 %collective-permute-start.29 = (bf16[88,384]{1,0:T(8,128)(2,1)S(1)}, bf16[88,384]{1,0:T(8,128)(2,1)S(1)}, u32[]{:S(2)}, u32[]{:S(2)}) collective-permute-start(bf16[88,384]{1,0:T(8,128)(2,1)S(1)} %activate.6.refs_1_), channel_id=1, source_target_pairs={{0,32},{16,48},{32,0},{48,16},{1,33},{17,49},{33,1},{49,17},{2,34}... | collective-permute-start | bytes 202760 | tf_op jit(solution)/shard_map/ppermute | solution.py:637
  176.2 12.2 %all_to_all.49.p_ref = bf16[16,8,1024]{2,1,0:T(8,128)(2,1)S(1)} all-to-all(bf16[16,8,1024]{2,1,0:T(8,128)(2,1)S(1)} %bitcast.26), channel_id=1, replica_groups=mesh['xh'=2,'z'=4,'c'=2,'xl'=2,'y'=4] {'xh','xl','y'}, dimensions={0} | all-to-all | bytes 524288 | tf_op jit(solution)/shard_map/all_to_all | solution.py:629
  188.6 12.1 %all_to_all.50 = bf16[16,8,1152]{2,1,0:T(8,128)(2,1)S(1)} all-to-all(bf16[16,8,1152]{2,1,0:T(8,128)(2,1)S(1)} %get-tuple-element.115), channel_id=1, replica_groups=mesh['xh'=2,'z'=4,'c'=2,'xl'=2,'y'=4] {'xh','xl','y'}, dimensions={0} | all-to-all | bytes 589824 | tf_op jit(solution)/shard_map/all_to_all | solution.py:629
  208.4 5.9 %collective-permute-done.33.refs_1_ = bf16[184,384]{1,0:T(8,128)(2,1)S(1)} collective-permute-done((bf16[184,384]{1,0:T(8,128)(2,1)S(1)}, bf16[184,384]{1,0:T(8,128)(2,1)S(1)}, u32[]{:S(2)}, u32[]{:S(2)}) %collective-permute-start.33) | collective-permute-done | bytes 141344 | tf_op jit(solution)/shard_map/ppermute | solution.py:637
  216.1 3.2 %collective-permute-start.37 = (bf16[88,384]{1,0:T(8,128)(2,1)S(1)}, bf16[88,384]{1,0:T(8,128)(2,1)S(1)}, u32[]{:S(2)}, u32[]{:S(2)}) collective-permute-start(bf16[88,384]{1,0:T(8,128)(2,1)S(1)} %activate.7.refs_1_), channel_id=1, source_target_pairs={{0,32},{16,48},{32,0},{48,16},{1,33},{17,49},{33,1},{49,17},{2,34}... | collective-permute-start | bytes 202760 | tf_op jit(solution)/shard_map/ppermute | solution.py:637
  226.6 12.3 %all_to_all.51.p_ref = bf16[16,8,1024]{2,1,0:T(8,128)(2,1)S(1)} all-to-all(bf16[16,8,1024]{2,1,0:T(8,128)(2,1)S(1)} %bitcast.27), channel_id=1, replica_groups=mesh['xh'=2,'z'=4,'c'=2,'xl'=2,'y'=4] {'xh','xl','y'}, dimensions={0} | all-to-all | bytes 524288 | tf_op jit(solution)/shard_map/all_to_all | solution.py:629
  239.6 15.1 %all_to_all.52.whole_ref = bf16[8,8,1024]{2,1,0:T(8,128)(2,1)S(1)} all-to-all(bf16[8,8,1024]{2,1,0:T(8,128)(2,1)S(1)} %broadcast_in_dim.2), channel_id=1, replica_groups=mesh['xh'=2,'z'=4,'c'=2,'xl'=2,'y'=4] {'xl','y'}, dimensions={0} | all-to-all | bytes 262144 | tf_op jit(solution)/shard_map/all_to_all | solution.py:629
  (124 shorter events, 94.1 us)
Async XLA Ops:
  1.8 9.4 %collective-permute-start.1 = (bf16[4,16,1280]{2,1,0:T(8,128)(2,1)}, bf16[4,16,1280]{2,1,0:T(8,128)(2,1)S(1)}, u32[]{:S(2)}, u32[]{:S(2)}) collective-permute-start(bf16[4,16,1280]{2,1,0:T(8,128)(2,1)} %first_rows.1.own_ref), channel_id=1, source_target_pairs={{0,64},{64,0},{1,65},{65,1},{2,66},{66,2},{3,67},{67,3},{4,68},{68... | collective-permute-start | bytes 491528 | tf_op jit(solution)/shard_map/ppermute | solution.py:649
  8.6 34.4 %collective-permute-start = (bf16[1536,256]{1,0:T(8,128)(2,1)}, bf16[1536,256]{1,0:T(8,128)(2,1)S(1)}, u32[]{:S(2)}, u32[]{:S(2)}) collective-permute-start(bf16[1536,256]{1,0:T(8,128)(2,1)} %get-tuple-element.66), channel_id=1, source_target_pairs={{0,64},{64,0},{1,65},{65,1},{2,66},{66,2},{3,67},{67,3},{4,68},{68... | collective-permute-start | bytes 2359304 | tf_op jit(solution)/shard_map/ppermute | solution.py:652
  9.1 37.0 %collective-permute-start.6 = (bf16[1536,256]{1,0:T(8,128)(2,1)}, bf16[1536,256]{1,0:T(8,128)(2,1)}, u32[]{:S(2)}, u32[]{:S(2)}) collective-permute-start(bf16[1536,256]{1,0:T(8,128)(2,1)} %get-tuple-element.77), channel_id=1, source_target_pairs={{0,72},{72,0},{8,64},{64,8},{1,73},{73,1},{9,65},{65,9},{2,74},{74... | collective-permute-start | bytes 2359304 | tf_op jit(solution)/shard_map/ppermute | solution.py:653
  11.8 8.3 %collective-permute-start.4 = (bf16[2,16,1280]{2,1,0:T(8,128)(2,1)S(1)}, bf16[2,16,1280]{2,1,0:T(8,128)(2,1)S(1)}, u32[]{:S(2)}, u32[]{:S(2)}) collective-permute-start(bf16[2,16,1280]{2,1,0:T(8,128)(2,1)S(1)} %get-tuple-element.70), channel_id=1, source_target_pairs={{0,48},{16,0},{32,16},{48,32},{1,49},{17,1},{33,17},{49,33},{2,50}... | collective-permute-start | bytes 245768 | tf_op jit(solution)/shard_map/ppermute | solution.py:637
  15.9 6.9 %collective-permute-start.3 = (bf16[2,16,1280]{2,1,0:T(8,128)(2,1)S(1)}, bf16[2,16,1280]{2,1,0:T(8,128)(2,1)S(1)}, u32[]{:S(2)}, u32[]{:S(2)}) collective-permute-start(bf16[2,16,1280]{2,1,0:T(8,128)(2,1)S(1)} %get-tuple-element.69), channel_id=1, source_target_pairs={{0,32},{16,48},{32,0},{48,16},{1,33},{17,49},{33,1},{49,17},{2,34}... | collective-permute-start | bytes 245768 | tf_op jit(solution)/shard_map/ppermute | solution.py:637
  15.9 8.3 %collective-permute-start.2 = (bf16[2,16,1280]{2,1,0:T(8,128)(2,1)S(1)}, bf16[2,16,1280]{2,1,0:T(8,128)(2,1)S(1)}, u32[]{:S(2)}, u32[]{:S(2)}) collective-permute-start(bf16[2,16,1280]{2,1,0:T(8,128)(2,1)S(1)} %get-tuple-element.68), channel_id=1, source_target_pairs={{0,16},{16,32},{32,48},{48,0},{1,17},{17,33},{33,49},{49,1},{2,18}... | collective-permute-start | bytes 245768 | tf_op jit(solution)/shard_map/ppermute | solution.py:637
  24.2 17.0 %collective-permute-start.5 = (bf16[4,2,16,1280]{3,2,1,0:T(8,128)(2,1)S(1)}, bf16[4,2,16,1280]{3,2,1,0:T(8,128)(2,1)}, u32[]{:S(2)}, u32[]{:S(2)}) collective-permute-start(bf16[4,2,16,1280]{3,2,1,0:T(8,128)(2,1)S(1)} %pad_maximum_fusion.own_ref), channel_id=1, source_target_pairs={{0,8},{8,0},{1,9},{9,1},{2,10},{10,2},{3,11},{11,3},{4,12},{12,4},... | collective-permute-start | bytes 983048 | tf_op jit(solution)/shard_map/ppermute | solution.py:633
  34.0 7.0 %all-to-all-start = ((bf16[2,2304,256]{2,1,0:T(8,128)(2,1)}), bf16[2,2304,256]{2,1,0:T(8,128)(2,1)S(1)}, u32[]{:S(2)}, u32[]{:S(2)}) async-start(bf16[2,2304,256]{2,1,0:T(8,128)(2,1)} %copy-done.1), calls=%async_computation | async-start | bytes 4718592 | tf_op jit(solution)/shard_map/all_to_all | solution.py:629
  43.0 26.0 %collective-permute-start.13 = (bf16[768,256]{1,0:T(8,128)(2,1)S(1)}, bf16[768,256]{1,0:T(8,128)(2,1)S(1)}, u32[]{:S(2)}, u32[]{:S(2)}) collective-permute-start(bf16[768,256]{1,0:T(8,128)(2,1)S(1)} %copy-done.7), channel_id=1, source_target_pairs={{0,64},{64,0},{1,65},{65,1},{2,66},{66,2},{3,67},{67,3},{4,68},{68... | collective-permute-start | bytes 1179656 | tf_op jit(solution)/shard_map/ppermute | solution.py:663
  43.6 25.5 %collective-permute-start.14 = (bf16[768,256]{1,0:T(8,128)(2,1)S(1)}, bf16[768,256]{1,0:T(8,128)(2,1)S(1)}, u32[]{:S(2)}, u32[]{:S(2)}) collective-permute-start(bf16[768,256]{1,0:T(8,128)(2,1)S(1)} %copy-done.5), channel_id=1, source_target_pairs={{0,72},{72,0},{8,64},{64,8},{1,73},{73,1},{9,65},{65,9},{2,74},{74... | collective-permute-start | bytes 1179656 | tf_op jit(solution)/shard_map/ppermute | solution.py:664
  48.9 6.4 %collective-permute-start.7 = (bf16[184,384]{1,0:T(8,128)(2,1)S(1)}, bf16[184,384]{1,0:T(8,128)(2,1)S(1)}, u32[]{:S(2)}, u32[]{:S(2)}) collective-permute-start(bf16[184,384]{1,0:T(8,128)(2,1)S(1)} %get-tuple-element.86), channel_id=1, source_target_pairs={{0,16},{16,32},{32,48},{48,0},{1,17},{17,33},{33,49},{49,1},{2,18}... | collective-permute-start | bytes 423944 | tf_op jit(solution)/shard_map/ppermute | solution.py:637
  49.6 9.3 %collective-permute-start.8 = (bf16[184,384]{1,0:T(8,128)(2,1)S(1)}, bf16[184,384]{1,0:T(8,128)(2,1)S(1)}, u32[]{:S(2)}, u32[]{:S(2)}) collective-permute-start(bf16[184,384]{1,0:T(8,128)(2,1)S(1)} %get-tuple-element.87), channel_id=1, source_target_pairs={{0,32},{16,48},{32,0},{48,16},{1,33},{17,49},{33,1},{49,17},{2,34}... | collective-permute-start | bytes 423944 | tf_op jit(solution)/shard_map/ppermute | solution.py:637
  53.2 6.6 %collective-permute-start.9 = (bf16[184,384]{1,0:T(8,128)(2,1)S(1)}, bf16[184,384]{1,0:T(8,128)(2,1)S(1)}, u32[]{:S(2)}, u32[]{:S(2)}) collective-permute-start(bf16[184,384]{1,0:T(8,128)(2,1)S(1)} %get-tuple-element.88), channel_id=1, source_target_pairs={{0,48},{16,0},{32,16},{48,32},{1,49},{17,1},{33,17},{49,33},{2,50}... | collective-permute-start | bytes 423944 | tf_op jit(solution)/shard_map/ppermute | solution.py:637
  102.8 7.4 %collective-permute-start.17 = (bf16[184,384]{1,0:T(8,128)(2,1)S(1)}, bf16[184,384]{1,0:T(8,128)(2,1)S(1)}, u32[]{:S(2)}, u32[]{:S(2)}) collective-permute-start(bf16[184,384]{1,0:T(8,128)(2,1)S(1)} %get-tuple-element.99), channel_id=1, source_target_pairs={{0,16},{16,32},{32,48},{48,0},{1,17},{17,33},{33,49},{49,1},{2,18}... | collective-permute-start | bytes 423944 | tf_op jit(solution)/shard_map/ppermute | solution.py:637
  104.0 9.9 %collective-permute-start.18 = (bf16[184,384]{1,0:T(8,128)(2,1)S(1)}, bf16[184,384]{1,0:T(8,128)(2,1)S(1)}, u32[]{:S(2)}, u32[]{:S(2)}) collective-permute-start(bf16[184,384]{1,0:T(8,128)(2,1)S(1)} %get-tuple-element.100), channel_id=1, source_target_pairs={{0,32},{16,48},{32,0},{48,16},{1,33},{17,49},{33,1},{49,17},{2,34}... | collective-permute-start | bytes 423944 | tf_op jit(solution)/shard_map/ppermute | solution.py:637
  106.8 7.1 %collective-permute-start.19 = (bf16[184,384]{1,0:T(8,128)(2,1)S(1)}, bf16[184,384]{1,0:T(8,128)(2,1)S(1)}, u32[]{:S(2)}, u32[]{:S(2)}) collective-permute-start(bf16[184,384]{1,0:T(8,128)(2,1)S(1)} %get-tuple-element.101), channel_id=1, source_target_pairs={{0,48},{16,0},{32,16},{48,32},{1,49},{17,1},{33,17},{49,33},{2,50}... | collective-permute-start | bytes 423944 | tf_op jit(solution)/shard_map/ppermute | solution.py:637
  153.6 7.8 %collective-permute-start.25 = (bf16[184,384]{1,0:T(8,128)(2,1)S(1)}, bf16[184,384]{1,0:T(8,128)(2,1)S(1)}, u32[]{:S(2)}, u32[]{:S(2)}) collective-permute-start(bf16[184,384]{1,0:T(8,128)(2,1)S(1)} %get-tuple-element.109), channel_id=1, source_target_pairs={{0,16},{16,32},{32,48},{48,0},{1,17},{17,33},{33,49},{49,1},{2,18}... | collective-permute-start | bytes 423944 | tf_op jit(solution)/shard_map/ppermute | solution.py:637
  153.7 9.9 %collective-permute-start.26 = (bf16[184,384]{1,0:T(8,128)(2,1)S(1)}, bf16[184,384]{1,0:T(8,128)(2,1)S(1)}, u32[]{:S(2)}, u32[]{:S(2)}) collective-permute-start(bf16[184,384]{1,0:T(8,128)(2,1)S(1)} %get-tuple-element.110), channel_id=1, source_target_pairs={{0,32},{16,48},{32,0},{48,16},{1,33},{17,49},{33,1},{49,17},{2,34}... | collective-permute-start | bytes 423944 | tf_op jit(solution)/shard_map/ppermute | solution.py:637
  156.9 7.4 %collective-permute-start.27 = (bf16[184,384]{1,0:T(8,128)(2,1)S(1)}, bf16[184,384]{1,0:T(8,128)(2,1)S(1)}, u32[]{:S(2)}, u32[]{:S(2)}) collective-permute-start(bf16[184,384]{1,0:T(8,128)(2,1)S(1)} %get-tuple-element.111), channel_id=1, source_target_pairs={{0,48},{16,0},{32,16},{48,32},{1,49},{17,1},{33,17},{49,33},{2,50}... | collective-permute-start | bytes 423944 | tf_op jit(solution)/shard_map/ppermute | solution.py:637
  165.4 6.7 %collective-permute-start.29 = (bf16[88,384]{1,0:T(8,128)(2,1)S(1)}, bf16[88,384]{1,0:T(8,128)(2,1)S(1)}, u32[]{:S(2)}, u32[]{:S(2)}) collective-permute-start(bf16[88,384]{1,0:T(8,128)(2,1)S(1)} %activate.6.refs_1_), channel_id=1, source_target_pairs={{0,32},{16,48},{32,0},{48,16},{1,33},{17,49},{33,1},{49,17},{2,34}... | collective-permute-start | bytes 202760 | tf_op jit(solution)/shard_map/ppermute | solution.py:637
  204.2 10.1 %collective-permute-start.33 = (bf16[184,384]{1,0:T(8,128)(2,1)S(1)}, bf16[184,384]{1,0:T(8,128)(2,1)S(1)}, u32[]{:S(2)}, u32[]{:S(2)}) collective-permute-start(bf16[184,384]{1,0:T(8,128)(2,1)S(1)} %get-tuple-element.117), channel_id=1, source_target_pairs={{0,16},{16,32},{32,48},{48,0},{1,17},{17,33},{33,49},{49,1},{2,18}... | collective-permute-start | bytes 423944 | tf_op jit(solution)/shard_map/ppermute | solution.py:637
  204.3 10.0 %collective-permute-start.34 = (bf16[184,384]{1,0:T(8,128)(2,1)S(1)}, bf16[184,384]{1,0:T(8,128)(2,1)S(1)}, u32[]{:S(2)}, u32[]{:S(2)}) collective-permute-start(bf16[184,384]{1,0:T(8,128)(2,1)S(1)} %get-tuple-element.118), channel_id=1, source_target_pairs={{0,32},{16,48},{32,0},{48,16},{1,33},{17,49},{33,1},{49,17},{2,34}... | collective-permute-start | bytes 423944 | tf_op jit(solution)/shard_map/ppermute | solution.py:637
  207.1 7.7 %collective-permute-start.35 = (bf16[184,384]{1,0:T(8,128)(2,1)S(1)}, bf16[184,384]{1,0:T(8,128)(2,1)S(1)}, u32[]{:S(2)}, u32[]{:S(2)}) collective-permute-start(bf16[184,384]{1,0:T(8,128)(2,1)S(1)} %get-tuple-element.119), channel_id=1, source_target_pairs={{0,48},{16,0},{32,16},{48,32},{1,49},{17,1},{33,17},{49,33},{2,50}... | collective-permute-start | bytes 423944 | tf_op jit(solution)/shard_map/ppermute | solution.py:637
  216.1 6.7 %collective-permute-start.37 = (bf16[88,384]{1,0:T(8,128)(2,1)S(1)}, bf16[88,384]{1,0:T(8,128)(2,1)S(1)}, u32[]{:S(2)}, u32[]{:S(2)}) collective-permute-start(bf16[88,384]{1,0:T(8,128)(2,1)S(1)} %activate.7.refs_1_), channel_id=1, source_target_pairs={{0,32},{16,48},{32,0},{48,16},{1,33},{17,49},{33,1},{49,17},{2,34}... | collective-permute-start | bytes 202760 | tf_op jit(solution)/shard_map/ppermute | solution.py:637
  (27 other events, 117.7 us)

commit v8 on v7

--- a/solution.py
+++ b/solution.py
@@ -185,7 +185,7 @@
             pltpu.VMEM((2, UNIT_HALF, HALF), bf16),
             pltpu.SemaphoreType.DMA((2,)),
         ],
-        compiler_params=pltpu.CompilerParams(vmem_limit_bytes=16 << 20),
+        compiler_params=pltpu.CompilerParams(vmem_limit_bytes=60 << 20),
         name="quantize_rest",
     )(ids, w)
 

time: 257 us -> 256 us (level)
  local copies, waits for them, and re-layouts: 5.4 us -> 0.15 us
  waiting for transfers between devices: 55.8 us -> 58.5 us
    unnamed x18 -> x14, local copies, waits for them, and re-layouts: 5.28 us -> 0.03 us
  transfers between devices with their start and end apart: 42 -> 42, of which waited for: 32 -> 33; matrix products, arithmetic and copies ran while one was open for 0% -> 0% of each run, Pallas kernels for 7% -> 8%
where the time goes in v8:
time: 256 us
  blocking collectives  103 us (40%)
  waiting for transfers between devices  58.5 us (23%)
  starting transfers between devices  57 us (22%)
  Pallas kernels  36.6 us (14%)
    all_to_all x8, blocking collectives, exchange(): return lax.all_to_all(x, axes, split_axis=0, concat_axis=0, tiled=True)  103 us
    ppermute x27, waiting for transfers between devices, around(): return lax.ppermute(x, 'z', [(i, (i + d) % 4) for i in range(4)])  47.3 us
    ppermute x27, starting transfers between devices, around(): return lax.ppermute(x, 'z', [(i, (i + d) % 4) for i in range(4)])  43 us
    pallas_call x4, Pallas kernels, gate_up(): pl.pallas_call(lambda *refs: gate_up_kernel(step, *refs), in_specs=[pl.Bl...  8.59 us
    pallas_call x1, Pallas kernels, quantize_rest(): pl.pallas_call(quant_rest_kernel, in_specs=[pl.BlockSpec(memory_space=plt...  6.31 us
    ppermute x8, waiting for transfers between devices, swap(): return lax.ppermute(x, 'c', [(0, 1), (1, 0)])  5.97 us
    pallas_call x4, Pallas kernels, down(): pl.pallas_call(lambda *refs: down_kernel(step, *refs), in_specs=[pl.Block...  5.3 us
  transfers between devices with their start and end apart: 42, of which 33 were waited for; matrix products, arithmetic and copies ran while one was open for 0% of the time, Pallas kernels for 8%

profile of v8, /device:TPU:0, one launch (start us, length us, event | category | flops | bytes accessed | tf_op | source)
XLA Modules:
  0.0 255.8 jit_solution(11086241712935875133)
XLA Ops:
  1.8 3.2 %collective-permute-start.1 = (bf16[4,16,1280]{2,1,0:T(8,128)(2,1)}, bf16[4,16,1280]{2,1,0:T(8,128)(2,1)S(1)}, u32[]{:S(2)}, u32[]{:S(2)}) collective-permute-start(bf16[4,16,1280]{2,1,0:T(8,128)(2,1)} %first_rows.1.own_ref), channel_id=1, source_target_pairs={{0,64},{64,0},{1,65},{65,1},{2,66},{66,2},{3,67},{67,3},{4,68},{68... | collective-permute-start | bytes 491528 | tf_op jit(solution)/shard_map/ppermute | solution.py:649
  4.9 3.7 %quantize_far.1 = (bf16[1536,256]{1,0:T(8,128)(2,1)}, bf16[1536,256]{1,0:T(8,128)(2,1)}) custom-call(bf16[2,3,1536,256]{3,2,1,0:T(8,128)(2,1)} %w_ref.3), custom_call_target="tpu_custom_call" | custom-call | tf_op jit(solution)/shard_map/quantize_far/pallas_call | solution.py:119
  11.8 4.1 %collective-permute-start.4 = (bf16[2,16,1280]{2,1,0:T(8,128)(2,1)S(1)}, bf16[2,16,1280]{2,1,0:T(8,128)(2,1)S(1)}, u32[]{:S(2)}, u32[]{:S(2)}) collective-permute-start(bf16[2,16,1280]{2,1,0:T(8,128)(2,1)S(1)} %get-tuple-element.70), channel_id=1, source_target_pairs={{0,48},{16,0},{32,16},{48,32},{1,49},{17,1},{33,17},{49,33},{2,50}... | collective-permute-start | bytes 245768 | tf_op jit(solution)/shard_map/ppermute | solution.py:637
  17.1 2.9 %collective-permute-done.4 = bf16[2,16,1280]{2,1,0:T(8,128)(2,1)S(1)} collective-permute-done((bf16[2,16,1280]{2,1,0:T(8,128)(2,1)S(1)}, bf16[2,16,1280]{2,1,0:T(8,128)(2,1)S(1)}, u32[]{:S(2)}, u32[]{:S(2)}) %collective-permute-start.4) | collective-permute-done | bytes 81952 | tf_op jit(solution)/shard_map/ppermute | solution.py:637
  24.4 6.3 %quantize_rest.1 = (bf16[2,2304,256]{2,1,0:T(8,128)(2,1)}, bf16[768,256]{1,0:T(8,128)(2,1)}, bf16[768,256]{1,0:T(8,128)(2,1)}) custom-call(s32[6]{0:T(128)} %copy-done.2, bf16[2,3,1536,256]{3,2,1,0:T(8,128)(2,1)} %w_ref.3), custom_call_target="tpu_custom_call" | custom-call | tf_op jit(solution)/shard_map/quantize_rest/pallas_call | solution.py:175
  30.7 3.8 %all-to-all-start = ((bf16[2,2304,256]{2,1,0:T(8,128)(2,1)}), bf16[2,2304,256]{2,1,0:T(8,128)(2,1)S(1)}, u32[]{:S(2)}, u32[]{:S(2)}) async-start(bf16[2,2304,256]{2,1,0:T(8,128)(2,1)} %get-tuple-element.71), calls=%async_computation | async-start | bytes 4718592 | tf_op jit(solution)/shard_map/all_to_all | solution.py:629
  34.6 3.0 %all-to-all-done.mixed_ref = bf16[2,2304,256]{2,1,0:T(8,128)(2,1)S(1)} async-done(((bf16[2,2304,256]{2,1,0:T(8,128)(2,1)}), bf16[2,2304,256]{2,1,0:T(8,128)(2,1)S(1)}, u32[]{:S(2)}, u32[]{:S(2)}) %all-to-all-start) | async-done | bytes 2359328 | tf_op jit(solution)/shard_map/all_to_all | solution.py:629
  49.6 3.6 %collective-permute-start.8 = (bf16[184,384]{1,0:T(8,128)(2,1)S(1)}, bf16[184,384]{1,0:T(8,128)(2,1)S(1)}, u32[]{:S(2)}, u32[]{:S(2)}) collective-permute-start(bf16[184,384]{1,0:T(8,128)(2,1)S(1)} %get-tuple-element.87), channel_id=1, source_target_pairs={{0,32},{16,48},{32,0},{48,16},{1,33},{17,49},{33,1},{49,17},{2,34}... | collective-permute-start | bytes 423944 | tf_op jit(solution)/shard_map/ppermute | solution.py:637
  54.8 4.2 %collective-permute-done.8.refs_2_ = bf16[184,384]{1,0:T(8,128)(2,1)S(1)} collective-permute-done((bf16[184,384]{1,0:T(8,128)(2,1)S(1)}, bf16[184,384]{1,0:T(8,128)(2,1)S(1)}, u32[]{:S(2)}, u32[]{:S(2)}) %collective-permute-start.8) | collective-permute-done | bytes 141344 | tf_op jit(solution)/shard_map/ppermute | solution.py:637
  71.8 15.1 %all_to_all.45.p_ref = bf16[16,8,1024]{2,1,0:T(8,128)(2,1)S(1)} all-to-all(bf16[16,8,1024]{2,1,0:T(8,128)(2,1)S(1)} %bitcast.24), channel_id=1, replica_groups=mesh['xh'=2,'z'=4,'c'=2,'xl'=2,'y'=4] {'xh','xl','y'}, dimensions={0} | all-to-all | bytes 524288 | tf_op jit(solution)/shard_map/all_to_all | solution.py:629
  87.0 12.1 %all_to_all.46 = bf16[16,8,1152]{2,1,0:T(8,128)(2,1)S(1)} all-to-all(bf16[16,8,1152]{2,1,0:T(8,128)(2,1)S(1)} %get-tuple-element.95), channel_id=1, replica_groups=mesh['xh'=2,'z'=4,'c'=2,'xl'=2,'y'=4] {'xh','xl','y'}, dimensions={0} | all-to-all | bytes 589824 | tf_op jit(solution)/shard_map/all_to_all | solution.py:629
  103.6 3.0 %collective-permute-start.18 = (bf16[184,384]{1,0:T(8,128)(2,1)S(1)}, bf16[184,384]{1,0:T(8,128)(2,1)S(1)}, u32[]{:S(2)}, u32[]{:S(2)}) collective-permute-start(bf16[184,384]{1,0:T(8,128)(2,1)S(1)} %get-tuple-element.100), channel_id=1, source_target_pairs={{0,32},{16,48},{32,0},{48,16},{1,33},{17,49},{33,1},{49,17},{2,34}... | collective-permute-start | bytes 423944 | tf_op jit(solution)/shard_map/ppermute | solution.py:637
  110.1 3.7 %collective-permute-done.18.refs_2_ = bf16[184,384]{1,0:T(8,128)(2,1)S(1)} collective-permute-done((bf16[184,384]{1,0:T(8,128)(2,1)S(1)}, bf16[184,384]{1,0:T(8,128)(2,1)S(1)}, u32[]{:S(2)}, u32[]{:S(2)}) %collective-permute-start.18) | collective-permute-done | bytes 141344 | tf_op jit(solution)/shard_map/ppermute | solution.py:637
  125.4 12.2 %all_to_all.47.p_ref = bf16[16,8,1024]{2,1,0:T(8,128)(2,1)S(1)} all-to-all(bf16[16,8,1024]{2,1,0:T(8,128)(2,1)S(1)} %bitcast.25), channel_id=1, replica_groups=mesh['xh'=2,'z'=4,'c'=2,'xl'=2,'y'=4] {'xh','xl','y'}, dimensions={0} | all-to-all | bytes 524288 | tf_op jit(solution)/shard_map/all_to_all | solution.py:629
  137.8 12.1 %all_to_all.48 = bf16[16,8,1152]{2,1,0:T(8,128)(2,1)S(1)} all-to-all(bf16[16,8,1152]{2,1,0:T(8,128)(2,1)S(1)} %get-tuple-element.107), channel_id=1, replica_groups=mesh['xh'=2,'z'=4,'c'=2,'xl'=2,'y'=4] {'xh','xl','y'}, dimensions={0} | all-to-all | bytes 589824 | tf_op jit(solution)/shard_map/all_to_all | solution.py:629
  153.6 3.1 %collective-permute-start.26 = (bf16[184,384]{1,0:T(8,128)(2,1)S(1)}, bf16[184,384]{1,0:T(8,128)(2,1)S(1)}, u32[]{:S(2)}, u32[]{:S(2)}) collective-permute-start(bf16[184,384]{1,0:T(8,128)(2,1)S(1)} %get-tuple-element.110), channel_id=1, source_target_pairs={{0,32},{16,48},{32,0},{48,16},{1,33},{17,49},{33,1},{49,17},{2,34}... | collective-permute-start | bytes 423944 | tf_op jit(solution)/shard_map/ppermute | solution.py:637
  157.6 3.6 %collective-permute-done.25.refs_1_ = bf16[184,384]{1,0:T(8,128)(2,1)S(1)} collective-permute-done((bf16[184,384]{1,0:T(8,128)(2,1)S(1)}, bf16[184,384]{1,0:T(8,128)(2,1)S(1)}, u32[]{:S(2)}, u32[]{:S(2)}) %collective-permute-start.25) | collective-permute-done | bytes 141344 | tf_op jit(solution)/shard_map/ppermute | solution.py:637
  165.3 3.2 %collective-permute-start.29 = (bf16[88,384]{1,0:T(8,128)(2,1)S(1)}, bf16[88,384]{1,0:T(8,128)(2,1)S(1)}, u32[]{:S(2)}, u32[]{:S(2)}) collective-permute-start(bf16[88,384]{1,0:T(8,128)(2,1)S(1)} %activate.6.refs_1_), channel_id=1, source_target_pairs={{0,32},{16,48},{32,0},{48,16},{1,33},{17,49},{33,1},{49,17},{2,34}... | collective-permute-start | bytes 202760 | tf_op jit(solution)/shard_map/ppermute | solution.py:637
  176.0 12.3 %all_to_all.49.p_ref = bf16[16,8,1024]{2,1,0:T(8,128)(2,1)S(1)} all-to-all(bf16[16,8,1024]{2,1,0:T(8,128)(2,1)S(1)} %bitcast.26), channel_id=1, replica_groups=mesh['xh'=2,'z'=4,'c'=2,'xl'=2,'y'=4] {'xh','xl','y'}, dimensions={0} | all-to-all | bytes 524288 | tf_op jit(solution)/shard_map/all_to_all | solution.py:629
  188.4 12.1 %all_to_all.50 = bf16[16,8,1152]{2,1,0:T(8,128)(2,1)S(1)} all-to-all(bf16[16,8,1152]{2,1,0:T(8,128)(2,1)S(1)} %get-tuple-element.115), channel_id=1, replica_groups=mesh['xh'=2,'z'=4,'c'=2,'xl'=2,'y'=4] {'xh','xl','y'}, dimensions={0} | all-to-all | bytes 589824 | tf_op jit(solution)/shard_map/all_to_all | solution.py:629
  208.3 5.9 %collective-permute-done.33.refs_1_ = bf16[184,384]{1,0:T(8,128)(2,1)S(1)} collective-permute-done((bf16[184,384]{1,0:T(8,128)(2,1)S(1)}, bf16[184,384]{1,0:T(8,128)(2,1)S(1)}, u32[]{:S(2)}, u32[]{:S(2)}) %collective-permute-start.33) | collective-permute-done | bytes 141344 | tf_op jit(solution)/shard_map/ppermute | solution.py:637
  215.9 3.2 %collective-permute-start.37 = (bf16[88,384]{1,0:T(8,128)(2,1)S(1)}, bf16[88,384]{1,0:T(8,128)(2,1)S(1)}, u32[]{:S(2)}, u32[]{:S(2)}) collective-permute-start(bf16[88,384]{1,0:T(8,128)(2,1)S(1)} %activate.7.refs_1_), channel_id=1, source_target_pairs={{0,32},{16,48},{32,0},{48,16},{1,33},{17,49},{33,1},{49,17},{2,34}... | collective-permute-start | bytes 202760 | tf_op jit(solution)/shard_map/ppermute | solution.py:637
  226.5 12.2 %all_to_all.51.p_ref = bf16[16,8,1024]{2,1,0:T(8,128)(2,1)S(1)} all-to-all(bf16[16,8,1024]{2,1,0:T(8,128)(2,1)S(1)} %bitcast.27), channel_id=1, replica_groups=mesh['xh'=2,'z'=4,'c'=2,'xl'=2,'y'=4] {'xh','xl','y'}, dimensions={0} | all-to-all | bytes 524288 | tf_op jit(solution)/shard_map/all_to_all | solution.py:629
  239.4 15.1 %all_to_all.52.whole_ref = bf16[8,8,1024]{2,1,0:T(8,128)(2,1)S(1)} all-to-all(bf16[8,8,1024]{2,1,0:T(8,128)(2,1)S(1)} %broadcast_in_dim.2), channel_id=1, replica_groups=mesh['xh'=2,'z'=4,'c'=2,'xl'=2,'y'=4] {'xl','y'}, dimensions={0} | all-to-all | bytes 262144 | tf_op jit(solution)/shard_map/all_to_all | solution.py:629
  (120 shorter events, 91.6 us)
Async XLA Ops:
  1.8 9.4 %collective-permute-start.1 = (bf16[4,16,1280]{2,1,0:T(8,128)(2,1)}, bf16[4,16,1280]{2,1,0:T(8,128)(2,1)S(1)}, u32[]{:S(2)}, u32[]{:S(2)}) collective-permute-start(bf16[4,16,1280]{2,1,0:T(8,128)(2,1)} %first_rows.1.own_ref), channel_id=1, source_target_pairs={{0,64},{64,0},{1,65},{65,1},{2,66},{66,2},{3,67},{67,3},{4,68},{68... | collective-permute-start | bytes 491528 | tf_op jit(solution)/shard_map/ppermute | solution.py:649
  8.6 31.0 %collective-permute-start = (bf16[1536,256]{1,0:T(8,128)(2,1)}, bf16[1536,256]{1,0:T(8,128)(2,1)S(1)}, u32[]{:S(2)}, u32[]{:S(2)}) collective-permute-start(bf16[1536,256]{1,0:T(8,128)(2,1)} %get-tuple-element.66), channel_id=1, source_target_pairs={{0,64},{64,0},{1,65},{65,1},{2,66},{66,2},{3,67},{67,3},{4,68},{68... | collective-permute-start | bytes 2359304 | tf_op jit(solution)/shard_map/ppermute | solution.py:652
  9.1 35.8 %collective-permute-start.6 = (bf16[1536,256]{1,0:T(8,128)(2,1)}, bf16[1536,256]{1,0:T(8,128)(2,1)}, u32[]{:S(2)}, u32[]{:S(2)}) collective-permute-start(bf16[1536,256]{1,0:T(8,128)(2,1)} %get-tuple-element.77), channel_id=1, source_target_pairs={{0,72},{72,0},{8,64},{64,8},{1,73},{73,1},{9,65},{65,9},{2,74},{74... | collective-permute-start | bytes 2359304 | tf_op jit(solution)/shard_map/ppermute | solution.py:653
  11.8 8.3 %collective-permute-start.4 = (bf16[2,16,1280]{2,1,0:T(8,128)(2,1)S(1)}, bf16[2,16,1280]{2,1,0:T(8,128)(2,1)S(1)}, u32[]{:S(2)}, u32[]{:S(2)}) collective-permute-start(bf16[2,16,1280]{2,1,0:T(8,128)(2,1)S(1)} %get-tuple-element.70), channel_id=1, source_target_pairs={{0,48},{16,0},{32,16},{48,32},{1,49},{17,1},{33,17},{49,33},{2,50}... | collective-permute-start | bytes 245768 | tf_op jit(solution)/shard_map/ppermute | solution.py:637
  15.9 6.9 %collective-permute-start.3 = (bf16[2,16,1280]{2,1,0:T(8,128)(2,1)S(1)}, bf16[2,16,1280]{2,1,0:T(8,128)(2,1)S(1)}, u32[]{:S(2)}, u32[]{:S(2)}) collective-permute-start(bf16[2,16,1280]{2,1,0:T(8,128)(2,1)S(1)} %get-tuple-element.69), channel_id=1, source_target_pairs={{0,32},{16,48},{32,0},{48,16},{1,33},{17,49},{33,1},{49,17},{2,34}... | collective-permute-start | bytes 245768 | tf_op jit(solution)/shard_map/ppermute | solution.py:637
  15.9 8.3 %collective-permute-start.2 = (bf16[2,16,1280]{2,1,0:T(8,128)(2,1)S(1)}, bf16[2,16,1280]{2,1,0:T(8,128)(2,1)S(1)}, u32[]{:S(2)}, u32[]{:S(2)}) collective-permute-start(bf16[2,16,1280]{2,1,0:T(8,128)(2,1)S(1)} %get-tuple-element.68), channel_id=1, source_target_pairs={{0,16},{16,32},{32,48},{48,0},{1,17},{17,33},{33,49},{49,1},{2,18}... | collective-permute-start | bytes 245768 | tf_op jit(solution)/shard_map/ppermute | solution.py:637
  24.2 13.6 %collective-permute-start.5 = (bf16[4,2,16,1280]{3,2,1,0:T(8,128)(2,1)S(1)}, bf16[4,2,16,1280]{3,2,1,0:T(8,128)(2,1)}, u32[]{:S(2)}, u32[]{:S(2)}) collective-permute-start(bf16[4,2,16,1280]{3,2,1,0:T(8,128)(2,1)S(1)} %pad_maximum_fusion.own_ref), channel_id=1, source_target_pairs={{0,8},{8,0},{1,9},{9,1},{2,10},{10,2},{3,11},{11,3},{4,12},{12,4},... | collective-permute-start | bytes 983048 | tf_op jit(solution)/shard_map/ppermute | solution.py:633
  30.7 6.9 %all-to-all-start = ((bf16[2,2304,256]{2,1,0:T(8,128)(2,1)}), bf16[2,2304,256]{2,1,0:T(8,128)(2,1)S(1)}, u32[]{:S(2)}, u32[]{:S(2)}) async-start(bf16[2,2304,256]{2,1,0:T(8,128)(2,1)} %get-tuple-element.71), calls=%async_computation | async-start | bytes 4718592 | tf_op jit(solution)/shard_map/all_to_all | solution.py:629
  39.6 29.2 %collective-permute-start.13 = (bf16[768,256]{1,0:T(8,128)(2,1)S(1)}, bf16[768,256]{1,0:T(8,128)(2,1)S(1)}, u32[]{:S(2)}, u32[]{:S(2)}) collective-permute-start(bf16[768,256]{1,0:T(8,128)(2,1)S(1)} %copy-done.6), channel_id=1, source_target_pairs={{0,64},{64,0},{1,65},{65,1},{2,66},{66,2},{3,67},{67,3},{4,68},{68... | collective-permute-start | bytes 1179656 | tf_op jit(solution)/shard_map/ppermute | solution.py:663
  40.1 28.7 %collective-permute-start.14 = (bf16[768,256]{1,0:T(8,128)(2,1)S(1)}, bf16[768,256]{1,0:T(8,128)(2,1)S(1)}, u32[]{:S(2)}, u32[]{:S(2)}) collective-permute-start(bf16[768,256]{1,0:T(8,128)(2,1)S(1)} %copy-done.5), channel_id=1, source_target_pairs={{0,72},{72,0},{8,64},{64,8},{1,73},{73,1},{9,65},{65,9},{2,74},{74... | collective-permute-start | bytes 1179656 | tf_op jit(solution)/shard_map/ppermute | solution.py:664
  47.6 7.2 %collective-permute-start.7 = (bf16[184,384]{1,0:T(8,128)(2,1)S(1)}, bf16[184,384]{1,0:T(8,128)(2,1)S(1)}, u32[]{:S(2)}, u32[]{:S(2)}) collective-permute-start(bf16[184,384]{1,0:T(8,128)(2,1)S(1)} %get-tuple-element.86), channel_id=1, source_target_pairs={{0,16},{16,32},{32,48},{48,0},{1,17},{17,33},{33,49},{49,1},{2,18}... | collective-permute-start | bytes 423944 | tf_op jit(solution)/shard_map/ppermute | solution.py:637
  49.6 9.3 %collective-permute-start.8 = (bf16[184,384]{1,0:T(8,128)(2,1)S(1)}, bf16[184,384]{1,0:T(8,128)(2,1)S(1)}, u32[]{:S(2)}, u32[]{:S(2)}) collective-permute-start(bf16[184,384]{1,0:T(8,128)(2,1)S(1)} %get-tuple-element.87), channel_id=1, source_target_pairs={{0,32},{16,48},{32,0},{48,16},{1,33},{17,49},{33,1},{49,17},{2,34}... | collective-permute-start | bytes 423944 | tf_op jit(solution)/shard_map/ppermute | solution.py:637
  53.2 6.6 %collective-permute-start.9 = (bf16[184,384]{1,0:T(8,128)(2,1)S(1)}, bf16[184,384]{1,0:T(8,128)(2,1)S(1)}, u32[]{:S(2)}, u32[]{:S(2)}) collective-permute-start(bf16[184,384]{1,0:T(8,128)(2,1)S(1)} %get-tuple-element.88), channel_id=1, source_target_pairs={{0,48},{16,0},{32,16},{48,32},{1,49},{17,1},{33,17},{49,33},{2,50}... | collective-permute-start | bytes 423944 | tf_op jit(solution)/shard_map/ppermute | solution.py:637
  102.7 7.4 %collective-permute-start.17 = (bf16[184,384]{1,0:T(8,128)(2,1)S(1)}, bf16[184,384]{1,0:T(8,128)(2,1)S(1)}, u32[]{:S(2)}, u32[]{:S(2)}) collective-permute-start(bf16[184,384]{1,0:T(8,128)(2,1)S(1)} %get-tuple-element.99), channel_id=1, source_target_pairs={{0,16},{16,32},{32,48},{48,0},{1,17},{17,33},{33,49},{49,1},{2,18}... | collective-permute-start | bytes 423944 | tf_op jit(solution)/shard_map/ppermute | solution.py:637
  103.6 10.2 %collective-permute-start.18 = (bf16[184,384]{1,0:T(8,128)(2,1)S(1)}, bf16[184,384]{1,0:T(8,128)(2,1)S(1)}, u32[]{:S(2)}, u32[]{:S(2)}) collective-permute-start(bf16[184,384]{1,0:T(8,128)(2,1)S(1)} %get-tuple-element.100), channel_id=1, source_target_pairs={{0,32},{16,48},{32,0},{48,16},{1,33},{17,49},{33,1},{49,17},{2,34}... | collective-permute-start | bytes 423944 | tf_op jit(solution)/shard_map/ppermute | solution.py:637
  106.7 7.1 %collective-permute-start.19 = (bf16[184,384]{1,0:T(8,128)(2,1)S(1)}, bf16[184,384]{1,0:T(8,128)(2,1)S(1)}, u32[]{:S(2)}, u32[]{:S(2)}) collective-permute-start(bf16[184,384]{1,0:T(8,128)(2,1)S(1)} %get-tuple-element.101), channel_id=1, source_target_pairs={{0,48},{16,0},{32,16},{48,32},{1,49},{17,1},{33,17},{49,33},{2,50}... | collective-permute-start | bytes 423944 | tf_op jit(solution)/shard_map/ppermute | solution.py:637
  153.4 7.8 %collective-permute-start.25 = (bf16[184,384]{1,0:T(8,128)(2,1)S(1)}, bf16[184,384]{1,0:T(8,128)(2,1)S(1)}, u32[]{:S(2)}, u32[]{:S(2)}) collective-permute-start(bf16[184,384]{1,0:T(8,128)(2,1)S(1)} %get-tuple-element.109), channel_id=1, source_target_pairs={{0,16},{16,32},{32,48},{48,0},{1,17},{17,33},{33,49},{49,1},{2,18}... | collective-permute-start | bytes 423944 | tf_op jit(solution)/shard_map/ppermute | solution.py:637
  153.6 9.9 %collective-permute-start.26 = (bf16[184,384]{1,0:T(8,128)(2,1)S(1)}, bf16[184,384]{1,0:T(8,128)(2,1)S(1)}, u32[]{:S(2)}, u32[]{:S(2)}) collective-permute-start(bf16[184,384]{1,0:T(8,128)(2,1)S(1)} %get-tuple-element.110), channel_id=1, source_target_pairs={{0,32},{16,48},{32,0},{48,16},{1,33},{17,49},{33,1},{49,17},{2,34}... | collective-permute-start | bytes 423944 | tf_op jit(solution)/shard_map/ppermute | solution.py:637
  156.7 7.4 %collective-permute-start.27 = (bf16[184,384]{1,0:T(8,128)(2,1)S(1)}, bf16[184,384]{1,0:T(8,128)(2,1)S(1)}, u32[]{:S(2)}, u32[]{:S(2)}) collective-permute-start(bf16[184,384]{1,0:T(8,128)(2,1)S(1)} %get-tuple-element.111), channel_id=1, source_target_pairs={{0,48},{16,0},{32,16},{48,32},{1,49},{17,1},{33,17},{49,33},{2,50}... | collective-permute-start | bytes 423944 | tf_op jit(solution)/shard_map/ppermute | solution.py:637
  165.3 6.7 %collective-permute-start.29 = (bf16[88,384]{1,0:T(8,128)(2,1)S(1)}, bf16[88,384]{1,0:T(8,128)(2,1)S(1)}, u32[]{:S(2)}, u32[]{:S(2)}) collective-permute-start(bf16[88,384]{1,0:T(8,128)(2,1)S(1)} %activate.6.refs_1_), channel_id=1, source_target_pairs={{0,32},{16,48},{32,0},{48,16},{1,33},{17,49},{33,1},{49,17},{2,34}... | collective-permute-start | bytes 202760 | tf_op jit(solution)/shard_map/ppermute | solution.py:637
  204.1 10.1 %collective-permute-start.33 = (bf16[184,384]{1,0:T(8,128)(2,1)S(1)}, bf16[184,384]{1,0:T(8,128)(2,1)S(1)}, u32[]{:S(2)}, u32[]{:S(2)}) collective-permute-start(bf16[184,384]{1,0:T(8,128)(2,1)S(1)} %get-tuple-element.117), channel_id=1, source_target_pairs={{0,16},{16,32},{32,48},{48,0},{1,17},{17,33},{33,49},{49,1},{2,18}... | collective-permute-start | bytes 423944 | tf_op jit(solution)/shard_map/ppermute | solution.py:637
  204.1 10.0 %collective-permute-start.34 = (bf16[184,384]{1,0:T(8,128)(2,1)S(1)}, bf16[184,384]{1,0:T(8,128)(2,1)S(1)}, u32[]{:S(2)}, u32[]{:S(2)}) collective-permute-start(bf16[184,384]{1,0:T(8,128)(2,1)S(1)} %get-tuple-element.118), channel_id=1, source_target_pairs={{0,32},{16,48},{32,0},{48,16},{1,33},{17,49},{33,1},{49,17},{2,34}... | collective-permute-start | bytes 423944 | tf_op jit(solution)/shard_map/ppermute | solution.py:637
  207.0 7.7 %collective-permute-start.35 = (bf16[184,384]{1,0:T(8,128)(2,1)S(1)}, bf16[184,384]{1,0:T(8,128)(2,1)S(1)}, u32[]{:S(2)}, u32[]{:S(2)}) collective-permute-start(bf16[184,384]{1,0:T(8,128)(2,1)S(1)} %get-tuple-element.119), channel_id=1, source_target_pairs={{0,48},{16,0},{32,16},{48,32},{1,49},{17,1},{33,17},{49,33},{2,50}... | collective-permute-start | bytes 423944 | tf_op jit(solution)/shard_map/ppermute | solution.py:637
  215.9 6.7 %collective-permute-start.37 = (bf16[88,384]{1,0:T(8,128)(2,1)S(1)}, bf16[88,384]{1,0:T(8,128)(2,1)S(1)}, u32[]{:S(2)}, u32[]{:S(2)}) collective-permute-start(bf16[88,384]{1,0:T(8,128)(2,1)S(1)} %activate.7.refs_1_), channel_id=1, source_target_pairs={{0,32},{16,48},{32,0},{48,16},{1,33},{17,49},{33,1},{49,17},{2,34}... | collective-permute-start | bytes 202760 | tf_op jit(solution)/shard_map/ppermute | solution.py:637
  (25 other events, 129.3 us)
